TPU v7x, 256 devices: a whole 4x4x8 slice. The times are simulated.
256 devices in a mesh: expert: 2 (over core), hidden: 32 (over x, z), replica: 4 (over y).
Axes of the slice: x: 4, y: 4, z: 8, core: 2. Of those that a mesh axis runs over, the one named last changes fastest.
Arguments:
- activations: bfloat16 [2, 4096, 4096], P('expert', 'replica', 'hidden'), may hold values from -6 to 6
- hidden_grad: bfloat16 [2, 4096, 14336], P('expert', 'replica', 'hidden'), may hold values from -0.1875 to 0.1875
- error_buffer: bfloat16 [2, 4, 4096, 14336], P('expert', 'replica', None, 'hidden'), may hold values from -4 to 4
- q_previous: float32 [2, 14336, 32], P('expert', 'hidden'), may hold values from -0.046875 to 0.046875
Outputs:
- p_factor: float32 [2, 4096, 32], P('expert')
- q_factor: float32 [2, 14336, 32], P('expert', 'hidden')
- new_error: bfloat16 [2, 4, 4096, 14336], P('expert', 'replica', None, 'hidden')
All inputs are finite; a program needn't handle non-finite values.
Results may differ from a plain program's by a relative error of at most 0.0055.
Values may be sent and summed in bfloat16 or wider, within the bound.
No kernel may reach another device: no remote copies, remote signals or barrier semaphores. Data moves between devices by JAX's collectives and lax.ppermute only.
A program may use at most 64 MiB of HBM per device.

v0:
```python
import jax
import jax.numpy as jnp
from jax import lax
from jax.sharding import PartitionSpec as P


def gram_of(rows_f32):
    return jnp.dot(
        rows_f32.T, rows_f32, precision=lax.Precision.HIGHEST, preferred_element_type=jnp.float32
    )


def solve_rows(gram_matrix, rows_f32):
    lower_tri = jnp.linalg.cholesky(gram_matrix)
    return jax.scipy.linalg.solve_triangular(lower_tri, rows_f32.T, lower=True).T


def shards(activations, hidden_grad, error_buffer, q_previous):
    cotangent = hidden_grad[0]
    replicas = lax.axis_size("replica")
    gradient = lax.dot_general(
        lax.all_gather(activations, "hidden", axis=2, tiled=True)[0],
        cotangent,
        (((0,), (0,)), ((), ())),
        preferred_element_type=jnp.float32,
    )
    corrected = (error_buffer[0, 0].astype(jnp.float32) + gradient).astype(jnp.bfloat16)
    q_low = q_previous[0].astype(jnp.bfloat16)
    p_partial = jnp.dot(corrected, q_low, preferred_element_type=jnp.float32)
    p_sum = lax.psum(p_partial, ("hidden", "replica")) / replicas
    p_orth = solve_rows(gram_of(p_sum), p_sum)
    p_low = p_orth.astype(jnp.bfloat16)
    q_partial = lax.dot_general(
        corrected, p_low, (((0,), (0,)), ((), ())), preferred_element_type=jnp.float32
    )
    q_sum = lax.psum(q_partial, "replica") / replicas
    q_round = q_sum.astype(jnp.bfloat16)
    approx = lax.dot_general(
        p_low, q_round, (((1,), (1,)), ((), ())), preferred_element_type=jnp.float32
    )
    new_error = (corrected.astype(jnp.float32) - approx).astype(jnp.bfloat16)
    return (p_orth[None], q_sum[None], new_error[None, None])


def solution(mesh):
    in_specs = (
        P("expert", "replica", "hidden"),
        P("expert", "replica", "hidden"),
        P("expert", "replica", None, "hidden"),
        P("expert", "hidden", None),
    )
    out_specs = (
        P("expert", None, None),
        P("expert", "hidden", None),
        P("expert", "replica", None, "hidden"),
    )
    return jax.shard_map(shards, mesh=mesh, in_specs=in_specs, out_specs=out_specs, check_vma=False)
```

profile of v0, /device:TPU:32, one launch (start us, length us, event | category | flops | bytes accessed | tf_op | source)
XLA Modules:
  0.0 385.1 jit_solution(12712155853580593267)
XLA Ops:
  7.2 0.0 copy-start
  7.2 0.0 all-gather.2.cloned.1.call-start
  7.2 0.7 all-gather.2.cloned.1.call-update
  7.9 0.0 copy-start.3
  7.9 0.0 all-reduce.2.cloned.1.call-start
  8.0 109.1 %all-gather.2.cloned.1.call-done = bf16[1,1024,4096]{2,1,0:T(8,128)(2,1)} async-done(((bf16[1,1024,128]{2,1,0:T(8,128)(2,1)}), bf16[1,1024,4096]{2,1,0:T(8,128)(2,1)}) %all-gather.2.cloned.1.call-update) | async-done | bytes 8388624 | tf_op jit(solution)/shard_map/all_gather | solution.py:22
  117.0 0.0 copy-done
  117.0 8.1 %fusion.2 = bf16[4096,448]{0,1:T(8,128)(2,1)S(1)} fusion(bf16[1,1024,4096]{2,1,0:T(8,128)(2,1)} %all-gather.2.cloned.1.call-done, bf16[1,1,4096,448]{2,3,1,0:T(8,128)(2,1)} %param.6, bf16[1,1024,448]{1,2,0:T(8,128)(2,1)S(1)} %copy-done), kind=kOutput, calls=%fused_computation.3 | convolution fusion | flops 3763601408 | bytes 16646144 | tf_op jit(solution)/shard_map/dot_general | solution.py:21
  125.2 0.0 copy-start.1
  125.2 1.8 copy-done.1
  127.0 0.0 copy-done.3
  127.0 1.6 fusion.16
  128.6 0.0 all-reduce.2.cloned.1.call-update
  128.6 212.9 %all-reduce.2.cloned.1.call-done = f32[4096,32]{0,1:T(8,128)} async-done(((f32[4096,32]{0,1:T(8,128)}), f32[4096,32]{0,1:T(8,128)}) %all-reduce.2.cloned.1.call-update) | async-done | bytes 524304 | tf_op jit(solution)/shard_map/psum | solution.py:30
  341.5 1.8 fusion.9
  343.3 0.1 copy.7
  343.4 2.9 cholesky.16
  346.4 0.6 compare_reduce_fusion
  347.0 0.7 fusion.20
  347.7 2.4 custom-call.7
  350.1 1.7 fusion.7
  351.8 0.0 copy-start.2
  351.8 3.3 fusion.14
  355.1 17.4 %psum.15 = f32[448,32]{0,1:T(8,128)S(1)} all-reduce(f32[448,32]{0,1:T(8,128)S(1)} %fusion.14), channel_id=1, replica_groups=mesh['expert'=2,'hidden'=32,'replica'=4] {'replica'}, use_global_device_ids=true, to_apply=%region_3.4 | all-reduce | flops 14336 | bytes 114688 | tf_op jit(solution)/shard_map/psum | solution.py:36
  372.6 5.0 %fusion.5 = bf16[1,1,4096,448]{2,3,1,0:T(8,128)(2,1)} fusion(bf16[4096,448]{0,1:T(8,128)(2,1)} %copy-done.1, f32[4096,32]{0,1:T(8,128)S(1)} %fusion.7, f32[448,32]{0,1:T(8,128)S(1)} %psum.15), kind=kOutput, calls=%fused_computation.5 | convolution fusion | flops 123105280 | bytes 7921664 | tf_op jit(solution)/shard_map/dot_general | solution.py:38
  377.6 0.0 copy-done.2
  377.6 0.6 multiply_bitcast_fusion
  (2 shorter events, 0.0 us)
Async XLA Ops:
  7.2 109.9 %copy-start = (bf16[1,1024,448]{1,2,0:T(8,128)(2,1)S(1)}, bf16[1,1024,448]{1,2,0:T(8,128)(2,1)}, u32[]{:S(2)}) copy-start(bf16[1,1024,448]{1,2,0:T(8,128)(2,1)} %param.5) | copy-start | bytes 2752516
  7.2 109.9 %all-gather.2.cloned.1.call-start = ((), (), s32[]{:S(2)}) async-start(), calls=%async_computation | async-start | bytes 8650752 | tf_op jit(solution)/shard_map/all_gather | solution.py:22
  7.9 119.1 %copy-start.3 = (f32[1,448,32]{1,2,0:T(8,128)S(1)}, f32[1,448,32]{1,2,0:T(8,128)}, u32[]{:S(2)}) copy-start(f32[1,448,32]{1,2,0:T(8,128)} %param.7) | copy-start | bytes 172036
  7.9 333.6 %all-reduce.2.cloned.1.call-start = ((), (), s32[]{:S(2)}) async-start(), calls=%async_computation.1 | async-start | bytes 1048576 | tf_op jit(solution)/shard_map/psum | solution.py:30
  125.2 1.8 copy-start.1
  351.8 25.8 %copy-start.2 = (f32[4096,32]{0,1:T(8,128)}, f32[4096,32]{0,1:T(8,128)S(1)}, u32[]{:S(2)}) copy-start(f32[4096,32]{0,1:T(8,128)S(1)} %fusion.7) | copy-start | bytes 1572868
Sparse Core Ops, SparseCore 0:
  10.5 106.5 all-gather.1
  128.7 212.7 all-reduce.1
where the time goes:
time: 386 us; the launch traced here: 385 us
  waiting for transfers between devices  323 us (84%)
  matrix products  21.5 us (6%)
  blocking collectives  17.4 us (5%)
  between operations  14.1 us (4%)
  other arithmetic  7.32 us (2%)
    psum x1, waiting for transfers between devices, shards(): p_sum = lax.psum(p_partial, ('hidden', 'replica')) / replicas  213 us
    all_gather x1, waiting for transfers between devices, shards(): lax.all_gather(activations, 'hidden', axis=2, tiled=True)[0]  109 us
    psum x1, blocking collectives, shards(): q_sum = lax.psum(q_partial, 'replica') / replicas  17.4 us
    dot_general x1, matrix products, shards(): lax.dot_general(lax.all_gather(activations, 'hidden', axis=2, tiled=True)...  8.13 us
  transfers between devices with their start and end apart: 2, of which 2 were waited for; matrix products, arithmetic and copies ran while one was open for 0% of the time, Pallas kernels for 0%

commit v1 on v0

v1 whole, which is shorter than its diff:
```python
import jax
import jax.numpy as jnp
from jax import lax
from jax.experimental import pallas as pl
from jax.experimental.pallas import tpu as pltpu
from jax.sharding import PartitionSpec as P

F32 = jnp.float32
BF16 = jnp.bfloat16
VMEM = pl.BlockSpec(memory_space=pltpu.VMEM)
LIMIT = pltpu.CompilerParams(vmem_limit_bytes=48 * 1024 * 1024)
NT = (((1,), (1,)), ((), ()))
TN = (((0,), (0,)), ((), ()))


def split3(v):
    a = v.astype(BF16)
    r = v - a.astype(F32)
    b = r.astype(BF16)
    c = (r - b.astype(F32)).astype(BF16)
    return jnp.concatenate([a, b, c], axis=0)


def fold3(v):
    n = v.shape[0] // 3
    return v[:n] + v[n : 2 * n] + v[2 * n :]


def first_kernel(q_ref, e_ref, h_ref, out_ref):
    q = q_ref[...].astype(BF16)
    eq = jnp.dot(q, e_ref[...], preferred_element_type=F32)
    t = jnp.dot(q, h_ref[...], preferred_element_type=F32)
    for i in range(4):
        out_ref[i, 0:32, :] = eq[:, 128 * i : 128 * (i + 1)]
        out_ref[i, 32:40, :] = t[8 * i : 8 * (i + 1), :]


def first(q_t, e_t, h_t):
    return pl.pallas_call(
        first_kernel,
        grid=(8,),
        in_specs=[
            pl.BlockSpec((32, 448), lambda g: (0, 0)),
            pl.BlockSpec((448, 512), lambda g: (0, g)),
            pl.BlockSpec((448, 128), lambda g: (0, g)),
        ],
        out_specs=pl.BlockSpec((4, 40, 128), lambda g: (g, 0, 0)),
        out_shape=jax.ShapeDtypeStruct((32, 40, 128), F32),
        compiler_params=LIMIT,
        name="eq_hq",
    )(q_t, e_t, h_t)


def split_sum_kernel(r_ref, eq_ref, t_ref):
    s = jnp.sum(r_ref[...], axis=0)
    eq_ref[...] = s[0:32]
    t_ref[...] = jnp.broadcast_to(s[32:40][None], t_ref.shape)


def split_sum(r):
    return pl.pallas_call(
        split_sum_kernel,
        in_specs=[VMEM],
        out_specs=[VMEM, VMEM],
        out_shape=[
            jax.ShapeDtypeStruct((32, 128), F32),
            jax.ShapeDtypeStruct((32, 8, 128), F32),
        ],
        compiler_params=LIMIT,
        name="sum_first",
    )(r)


def tile_sum_kernel(r_ref, t_ref):
    t_ref[...] = jnp.broadcast_to(jnp.sum(r_ref[...], axis=0)[None], t_ref.shape)


def tile_sum(r):
    return pl.pallas_call(
        tile_sum_kernel,
        in_specs=[VMEM],
        out_specs=VMEM,
        out_shape=jax.ShapeDtypeStruct((32, 8, 128), F32),
        compiler_params=LIMIT,
        name="sum_tiles",
    )(r)


def rows_of(t_ref):
    return jnp.concatenate([t_ref[4 * j : 4 * j + 4].reshape(32, 128) for j in range(8)], axis=1)


def slab_kernel(eq_ref, t_ref, x_ref, out_ref):
    t = split3(rows_of(t_ref))
    out_ref[...] = eq_ref[...] + fold3(jnp.dot(t, x_ref[...], preferred_element_type=F32))


def slab(eq, t, x):
    return pl.pallas_call(
        slab_kernel,
        in_specs=[VMEM] * 3,
        out_specs=VMEM,
        out_shape=jax.ShapeDtypeStruct((32, 128), F32),
        compiler_params=LIMIT,
        name="p_slab",
    )(eq, t, x)


def xp_kernel(p_ref, x_ref, out_ref):
    y = lax.dot_general(p_ref[...], x_ref[...], NT, preferred_element_type=F32)
    for j in range(8):
        for i in range(4):
            out_ref[4 * j + i] = y[8 * i : 8 * i + 8, 128 * j : 128 * j + 128]


def xp(p_slab, x):
    return pl.pallas_call(
        xp_kernel,
        in_specs=[VMEM] * 2,
        out_specs=VMEM,
        out_shape=jax.ShapeDtypeStruct((32, 8, 128), F32),
        compiler_params=LIMIT,
        name="x_p",
    )(p_slab, x)


def q_kernel(p_ref, y_ref, e_ref, h_ref, out_ref):
    y = split3(rows_of(y_ref))
    part = lax.dot_general(p_ref[...], e_ref[...], NT, preferred_element_type=F32)
    out_ref[...] = part + fold3(lax.dot_general(y, h_ref[...], NT, preferred_element_type=F32))


def q_part(p_low, y, e_t, h_t):
    return pl.pallas_call(
        q_kernel,
        in_specs=[VMEM] * 4,
        out_specs=VMEM,
        out_shape=jax.ShapeDtypeStruct((32, 448), F32),
        compiler_params=LIMIT,
        name="q_part",
    )(p_low, y, e_t, h_t)


def final_kernel(x_ref, h_ref, e_ref, p_ref, q_ref, out_ref):
    q = q_ref[...].astype(BF16)
    for c in range(2):
        cols = slice(256 * c, 256 * (c + 1))
        x = jnp.concatenate([x_ref[2 * c], x_ref[2 * c + 1]], axis=1)
        grad = jnp.dot(h_ref[...], x, preferred_element_type=F32)
        corrected = (e_ref[:, cols].astype(F32) + grad).astype(BF16)
        approx = lax.dot_general(q, p_ref[:, cols], TN, preferred_element_type=F32)
        out_ref[:, cols] = (corrected.astype(F32) - approx).astype(BF16)


def final(x_all, h_t, e_t, p_low, q_t):
    return pl.pallas_call(
        final_kernel,
        grid=(8,),
        in_specs=[
            pl.BlockSpec((4, 1024, 128), lambda g: (g, 0, 0)),
            pl.BlockSpec((448, 1024), lambda g: (0, 0)),
            pl.BlockSpec((448, 512), lambda g: (0, g)),
            pl.BlockSpec((32, 512), lambda g: (0, g)),
            pl.BlockSpec((32, 448), lambda g: (0, 0)),
        ],
        out_specs=pl.BlockSpec((448, 512), lambda g: (0, g)),
        out_shape=jax.ShapeDtypeStruct((448, 4096), BF16),
        compiler_params=LIMIT,
        name="new_error",
    )(x_all, h_t, e_t, p_low, q_t)


def swap(v):
    return lax.all_to_all(v, "hidden", 0, 0)


def sum_replicas(v):
    others = [lax.ppermute(v, "replica", [(i, (i + s) % 4) for i in range(4)]) for s in (1, 3, 2)]
    return v + others[0] + others[1] + others[2]


def shards(activations, hidden_grad, error_buffer, q_previous):
    x = activations[0]
    h_t = hidden_grad[0].T
    e_t = error_buffer[0, 0].T
    q_t = q_previous[0].T
    x_all = lax.all_gather(x, "hidden", axis=0)
    eq, t = split_sum(swap(first(q_t, e_t, h_t)))
    p_slab = sum_replicas(slab(eq, swap(t), x)) * 0.25
    p_sum = swap(jnp.broadcast_to(p_slab[None], (32, 32, 128)))
    p_sum = p_sum.transpose(1, 0, 2).reshape(32, 4096)
    gram = lax.dot_general(
        p_sum, p_sum, NT, precision=lax.Precision.HIGHEST, preferred_element_type=F32
    )
    p_factor = jax.scipy.linalg.solve_triangular(jnp.linalg.cholesky(gram), p_sum, lower=True)
    p_low = p_factor.astype(BF16)
    own = lax.dynamic_slice(p_low, (0, lax.axis_index("hidden") * 128), (32, 128))
    y = swap(tile_sum(swap(xp(own, x))))
    q_factor = sum_replicas(q_part(p_low, y, e_t, h_t)) * 0.25
    new_error = final(x_all, h_t, e_t, p_low, q_factor)
    return (p_factor.T[None], q_factor.T[None], new_error.T[None, None])


def solution(mesh):
    in_specs = (
        P("expert", "replica", "hidden"),
        P("expert", "replica", "hidden"),
        P("expert", "replica", None, "hidden"),
        P("expert", "hidden", None),
    )
    out_specs = (
        P("expert", None, None),
        P("expert", "hidden", None),
        P("expert", "replica", None, "hidden"),
    )
    return jax.shard_map(shards, mesh=mesh, in_specs=in_specs, out_specs=out_specs, check_vma=False)
```

time: 386 us -> 173 us (0.45)
  waiting for transfers between devices: 323 us -> 32 us
  blocking collectives: 17.4 us -> 81.2 us
  matrix products: 21.5 us -> 2 us
  Pallas kernels: 0 us -> 14.7 us
  starting transfers between devices: 0.08 us -> 12.4 us
  local copies, waits for them, and re-layouts: 1.92 us -> 9.07 us
    psum x1 -> x0, waiting for transfers between devices: 213 us -> none  [shards(): p_sum = lax.psum(p_partial, ('hidden', 'replica')) / replicas]
    all_gather x1, waiting for transfers between devices: 109 us -> 0.02 us  [shards(): x_all = lax.all_gather(x, 'hidden', axis=0)]
    all_to_all x0 -> x4, blocking collectives: none -> 81.2 us  [swap(): return lax.all_to_all(v, 'hidden', 0, 0)]
    all_to_all x0 -> x1, waiting for transfers between devices: none -> 21.9 us  [swap(): return lax.all_to_all(v, 'hidden', 0, 0)]
    dot_general x5 -> x1, matrix products: 19.8 us -> 0.55 us  [shards(): lax.dot_general(p_sum, p_sum, NT, precision=lax.Precision.HIGHEST, prefer...]
    psum x1 -> x0, blocking collectives: 17.4 us -> none  [shards(): q_sum = lax.psum(q_partial, 'replica') / replicas]
    pallas_call x0 -> x7, Pallas kernels: none -> 14.7 us  [the longest x1 10.4 us: final(): pl.pallas_call(final_kernel, grid=(8,), in_specs=[pl.BlockSpec((4, 1024,...]
    ppermute x0 -> x6, waiting for transfers between devices: none -> 9.39 us  [sum_replicas(): lax.ppermute(v, 'replica', [(i, (i + s) % 4) for i in range(4)])]
  transfers between devices with their start and end apart: 2 -> 8, of which waited for: 2 -> 5; matrix products, arithmetic and copies ran while one was open for 0% -> 6% of each run, Pallas kernels for 0% -> 2%
where the time goes in v1:
time: 173 us; the launch traced here: 172 us
  blocking collectives  81.2 us (47%)
  waiting for transfers between devices  32 us (18%)
  Pallas kernels  14.7 us (8%)
  between operations  14.1 us (8%)
  starting transfers between devices  12.4 us (7%)
  local copies, waits for them, and re-layouts  9.07 us (5%)
  other arithmetic  6.72 us (4%)
  matrix products  2 us (1%)
    all_to_all x4, blocking collectives, swap(): return lax.all_to_all(v, 'hidden', 0, 0)  81.2 us
    all_to_all x1, waiting for transfers between devices, swap(): return lax.all_to_all(v, 'hidden', 0, 0)  21.9 us
    pallas_call x1, Pallas kernels, final(): pl.pallas_call(final_kernel, grid=(8,), in_specs=[pl.BlockSpec((4, 1024,...  10.4 us
    ppermute x6, waiting for transfers between devices, sum_replicas(): lax.ppermute(v, 'replica', [(i, (i + s) % 4) for i in range(4)])  9.39 us
    unnamed x16, local copies, waits for them, and re-layouts  8.14 us
    ppermute x6, starting transfers between devices, sum_replicas(): lax.ppermute(v, 'replica', [(i, (i + s) % 4) for i in range(4)])  7.87 us
    all_to_all x1, starting transfers between devices, swap(): return lax.all_to_all(v, 'hidden', 0, 0)  4.52 us
    another operation x3, other arithmetic, shards(): jnp.linalg.cholesky(gram)  3.6 us
  transfers between devices with their start and end apart: 8, of which 5 were waited for; matrix products, arithmetic and copies ran while one was open for 6% of the time, Pallas kernels for 2%

profile of v1, /device:TPU:32, one launch (start us, length us, event | category | flops | bytes accessed | tf_op | source)
XLA Modules:
  0.0 172.2 jit_solution(17151295445993494631)
XLA Ops:
  7.2 0.0 all-gather.2.cloned.1.call-start
  7.2 0.7 all-gather.2.cloned.1.call-update
  7.9 0.0 copy-start
  7.9 2.0 %copy-done = bf16[1,1,4096,448]{2,3,1,0:T(8,128)(2,1)S(1)} copy-done((bf16[1,1,4096,448]{2,3,1,0:T(8,128)(2,1)S(1)}, bf16[1,1,4096,448]{2,3,1,0:T(8,128)(2,1)}, u32[]{:S(2)}) %copy-start) | copy-done | bytes 3670040
  9.9 0.0 copy-start.3
  9.9 1.2 copy-done.3
  11.1 0.8 copy-done.7
  12.0 2.4 %eq_hq.1 = f32[32,40,128]{2,1,0:T(8,128)S(1)} custom-call(f32[32,448]{1,0:T(8,128)S(1)} %bitcast.53, bf16[448,4096]{1,0:T(8,128)(2,1)S(1)} %bitcast.44, bf16[448,1024]{1,0:T(8,128)(2,1)S(1)} %bitcast.47), custom_call_target="tpu_custom_call" | custom-call | tf_op jit(solution)/shard_map/eq_hq/pallas_call | solution.py:39
  14.4 0.0 copy-start.4
  14.4 37.0 %all_to_all.25.r_ref = f32[32,40,128]{2,1,0:T(8,128)S(1)} all-to-all(f32[32,40,128]{2,1,0:T(8,128)S(1)} %eq_hq.1), channel_id=1, replica_groups=mesh['expert'=2,'hidden'=32,'replica'=4] {'hidden'}, dimensions={0} | all-to-all | bytes 1310720 | tf_op jit(solution)/shard_map/all_to_all | solution.py:174
  51.3 0.1 sum_first.1
  51.4 14.3 %all_to_all.26.t_ref = f32[32,8,128]{2,1,0:T(8,128)S(1)} all-to-all(f32[32,8,128]{2,1,0:T(8,128)S(1)} %get-tuple-element.6), channel_id=1, replica_groups=mesh['expert'=2,'hidden'=32,'replica'=4] {'hidden'}, dimensions={0} | all-to-all | bytes 262144 | tf_op jit(solution)/shard_map/all_to_all | solution.py:174
  65.7 0.0 copy-done.5
  65.7 0.2 p_slab.1
  65.9 3.3 %collective-permute-start.2 = (f32[32,128]{1,0:T(8,128)S(1)}, f32[32,128]{1,0:T(8,128)S(1)}, u32[]{:S(2)}, u32[]{:S(2)}) collective-permute-start(f32[32,128]{1,0:T(8,128)S(1)} %p_slab.1), channel_id=1, source_target_pairs={{0,2},{1,3},{2,0},{3,1},{4,6},{5,7},{6,4},{7,5},{8,10},{9,11},{10,... | collective-permute-start | bytes 49160 | tf_op jit(solution)/shard_map/ppermute | solution.py:178
  69.3 1.0 collective-permute-start.1
  70.3 1.0 collective-permute-start
  71.3 0.0 collective-permute-done.2
  71.3 1.7 collective-permute-done.1
  73.0 2.2 %collective-permute-done = f32[32,128]{1,0:T(8,128)S(1)} collective-permute-done((f32[32,128]{1,0:T(8,128)S(1)}, f32[32,128]{1,0:T(8,128)S(1)}, u32[]{:S(2)}, u32[]{:S(2)}) %collective-permute-start) | collective-permute-done | bytes 16416 | tf_op jit(solution)/shard_map/ppermute | solution.py:178
  75.2 0.9 broadcast_in_dim.17
  76.1 4.5 %all-to-all-start.2 = ((f32[32,32,128]{2,1,0:T(8,128)}), f32[32,32,128]{2,1,0:T(8,128)S(1)}, u32[]{:S(2)}, u32[]{:S(2)}) async-start(f32[32,32,128]{2,1,0:T(8,128)} %broadcast_in_dim.17), calls=%async_computation.2 | async-start | bytes 1048576 | tf_op jit(solution)/shard_map/all_to_all | solution.py:174
  80.6 21.9 %all-to-all-done.2 = f32[32,32,128]{2,1,0:T(8,128)S(1)} async-done(((f32[32,32,128]{2,1,0:T(8,128)}), f32[32,32,128]{2,1,0:T(8,128)S(1)}, u32[]{:S(2)}, u32[]{:S(2)}) %all-to-all-start.2) | async-done | bytes 524320 | tf_op jit(solution)/shard_map/all_to_all | solution.py:174
  102.5 0.5 convolution_bitcast_fusion
  103.0 0.1 copy.10
  103.1 2.9 %cholesky.16 = f32[32,32]{1,0:T(8,128)S(1)} custom-call(f32[32,32]{1,0:T(8,128)S(1)} %fusion.6), custom_call_target="Cholesky" | custom-call | tf_op jit(solution)/shard_map/jit(cholesky)/cholesky | solution.py:195
  106.1 0.6 compare_reduce_fusion
  106.7 0.7 fusion.4
  107.4 2.4 %custom-call.7 = f32[1,32,32]{1,2,0:T(8,128)S(1)} custom-call(f32[1,32,32]{2,1,0:T(8,128)S(1)} %fusion.4), custom_call_target="InvertDiagBlocksLowerTriangular" | custom-call | tf_op jit(solution)/shard_map/jit(_solve_triangular)/triangular_solve | solution.py:195
  109.8 1.4 fusion.7
  111.3 0.2 x_p.1
  111.4 15.7 %all_to_all.27.r_ref = f32[32,8,128]{2,1,0:T(8,128)S(1)} all-to-all(f32[32,8,128]{2,1,0:T(8,128)S(1)} %x_p.1), channel_id=1, replica_groups=mesh['expert'=2,'hidden'=32,'replica'=4] {'hidden'}, dimensions={0} | all-to-all | bytes 262144 | tf_op jit(solution)/shard_map/all_to_all | solution.py:174
  127.2 14.2 %all_to_all.28.y_ref = f32[32,8,128]{2,1,0:T(8,128)S(1)} all-to-all(f32[32,8,128]{2,1,0:T(8,128)S(1)} %sum_tiles.1), channel_id=1, replica_groups=mesh['expert'=2,'hidden'=32,'replica'=4] {'hidden'}, dimensions={0} | all-to-all | bytes 262144 | tf_op jit(solution)/shard_map/all_to_all | solution.py:174
  141.4 0.0 copy-done.4
  141.4 2.0 %copy-done.1 = bf16[1,1,4096,448]{2,3,1,0:T(8,128)(2,1)S(1)} copy-done((bf16[1,1,4096,448]{2,3,1,0:T(8,128)(2,1)S(1)}, bf16[1,1,4096,448]{2,3,1,0:T(8,128)(2,1)}, u32[]{:S(2)}) %copy-start.1) | copy-done | bytes 3670040
  143.5 1.4 q_part.1
  144.8 0.5 collective-permute-start.5
  145.3 2.0 %collective-permute-start.4 = (f32[32,448]{1,0:T(8,128)S(1)}, f32[32,448]{1,0:T(8,128)S(1)}, u32[]{:S(2)}, u32[]{:S(2)}) collective-permute-start(f32[32,448]{1,0:T(8,128)S(1)} %q_part.1), channel_id=1, source_target_pairs={{0,3},{1,0},{2,1},{3,2},{4,7},{5,4},{6,5},{7,6},{8,11},{9,8},{10,9... | collective-permute-start | bytes 172040 | tf_op jit(solution)/shard_map/ppermute | solution.py:178
  147.3 0.0 collective-permute-start.3
  147.4 3.3 %collective-permute-done.5 = f32[32,448]{1,0:T(8,128)S(1)} collective-permute-done((f32[32,448]{1,0:T(8,128)S(1)}, f32[32,448]{1,0:T(8,128)S(1)}, u32[]{:S(2)}, u32[]{:S(2)}) %collective-permute-start.5) | collective-permute-done | bytes 57376 | tf_op jit(solution)/shard_map/ppermute | solution.py:178
  150.7 0.0 collective-permute-done.4
  150.7 2.1 %collective-permute-done.3 = f32[32,448]{1,0:T(8,128)S(1)} collective-permute-done((f32[32,448]{1,0:T(8,128)S(1)}, f32[32,448]{1,0:T(8,128)S(1)}, u32[]{:S(2)}, u32[]{:S(2)}) %collective-permute-start.3) | collective-permute-done | bytes 57376 | tf_op jit(solution)/shard_map/ppermute | solution.py:178
  152.8 0.0 copy-start.6
  152.8 0.0 all-gather.2.cloned.1.call-done.x_ref
  152.9 0.0 copy-start.2
  152.9 2.0 %copy-done.2 = bf16[1,1,4096,448]{2,3,1,0:T(8,128)(2,1)S(1)} copy-done((bf16[1,1,4096,448]{2,3,1,0:T(8,128)(2,1)S(1)}, bf16[1,1,4096,448]{2,3,1,0:T(8,128)(2,1)}, u32[]{:S(2)}) %copy-start.2) | copy-done | bytes 3670040
  154.9 10.4 %new_error.1 = bf16[448,4096]{1,0:T(8,128)(2,1)} custom-call(bf16[32,1024,128]{2,1,0:T(8,128)(2,1)} %all-gather.2.cloned.1.call-done.x_ref, bf16[448,1024]{1,0:T(8,128)(2,1)S(1)} %bitcast.49, bf16[448,4096]{1,0:T(8,128)(2,1)S(1)} %bitcast.46, bf16[32,4096]{1,0:T(8,128)(2,1)S(1)} %get-tuple-element.7.p_ref, f32[32,448]{1,0:T(8,128)S(1)} %add_multiply_fusion.q_ref), custom_call_target="tpu_custom_call" | custom-call | tf_op jit(solution)/shard_map/new_error/pallas_call | solution.py:156
  165.3 0.0 copy-done.6
  (9 shorter events, 0.1 us)
Async XLA Ops:
  7.2 145.7 %all-gather.2.cloned.1.call-start = ((), (), s32[]{:S(2)}) async-start(), calls=%async_computation.5 | async-start | bytes 8650752 | tf_op jit(solution)/shard_map/all_gather | solution.py:187
  7.9 2.0 %copy-start = (bf16[1,1,4096,448]{2,3,1,0:T(8,128)(2,1)S(1)}, bf16[1,1,4096,448]{2,3,1,0:T(8,128)(2,1)}, u32[]{:S(2)}) copy-start(bf16[1,1,4096,448]{2,3,1,0:T(8,128)(2,1)} %param.6) | copy-start | bytes 11010052
  9.9 1.2 copy-start.3
  11.1 0.8 copy-start.7
  12.0 53.7 %copy-start.5 = (bf16[1,1024,128]{2,1,0:T(8,128)(2,1)S(1)}, bf16[1,1024,128]{2,1,0:T(8,128)(2,1)}, u32[]{:S(2)}) copy-start(bf16[1,1024,128]{2,1,0:T(8,128)(2,1)} %param.4) | copy-start | bytes 786436
  14.4 127.1 %copy-start.4 = (bf16[1,1024,448]{1,2,0:T(8,128)(2,1)S(1)}, bf16[1,1024,448]{1,2,0:T(8,128)(2,1)}, u32[]{:S(2)}) copy-start(bf16[1,1024,448]{1,2,0:T(8,128)(2,1)} %param.5) | copy-start | bytes 2752516
  65.9 5.4 %collective-permute-start.2 = (f32[32,128]{1,0:T(8,128)S(1)}, f32[32,128]{1,0:T(8,128)S(1)}, u32[]{:S(2)}, u32[]{:S(2)}) collective-permute-start(f32[32,128]{1,0:T(8,128)S(1)} %p_slab.1), channel_id=1, source_target_pairs={{0,2},{1,3},{2,0},{3,1},{4,6},{5,7},{6,4},{7,5},{8,10},{9,11},{10,... | collective-permute-start | bytes 49160 | tf_op jit(solution)/shard_map/ppermute | solution.py:178
  69.3 3.7 %collective-permute-start.1 = (f32[32,128]{1,0:T(8,128)S(1)}, f32[32,128]{1,0:T(8,128)S(1)}, u32[]{:S(2)}, u32[]{:S(2)}) collective-permute-start(f32[32,128]{1,0:T(8,128)S(1)} %p_slab.1), channel_id=1, source_target_pairs={{0,3},{1,0},{2,1},{3,2},{4,7},{5,4},{6,5},{7,6},{8,11},{9,8},{10,9... | collective-permute-start | bytes 49160 | tf_op jit(solution)/shard_map/ppermute | solution.py:178
  70.3 4.9 %collective-permute-start = (f32[32,128]{1,0:T(8,128)S(1)}, f32[32,128]{1,0:T(8,128)S(1)}, u32[]{:S(2)}, u32[]{:S(2)}) collective-permute-start(f32[32,128]{1,0:T(8,128)S(1)} %p_slab.1), channel_id=1, source_target_pairs={{0,1},{1,2},{2,3},{3,0},{4,5},{5,6},{6,7},{7,4},{8,9},{9,10},{10,1... | collective-permute-start | bytes 49160 | tf_op jit(solution)/shard_map/ppermute | solution.py:178
  76.1 26.4 %all-to-all-start.2 = ((f32[32,32,128]{2,1,0:T(8,128)}), f32[32,32,128]{2,1,0:T(8,128)S(1)}, u32[]{:S(2)}, u32[]{:S(2)}) async-start(f32[32,32,128]{2,1,0:T(8,128)} %broadcast_in_dim.17), calls=%async_computation.2 | async-start | bytes 1048576 | tf_op jit(solution)/shard_map/all_to_all | solution.py:174
  141.4 2.0 %copy-start.1 = (bf16[1,1,4096,448]{2,3,1,0:T(8,128)(2,1)S(1)}, bf16[1,1,4096,448]{2,3,1,0:T(8,128)(2,1)}, u32[]{:S(2)}) copy-start(bf16[1,1,4096,448]{2,3,1,0:T(8,128)(2,1)} %param.6) | copy-start | bytes 11010052
  144.8 5.8 %collective-permute-start.5 = (f32[32,448]{1,0:T(8,128)S(1)}, f32[32,448]{1,0:T(8,128)S(1)}, u32[]{:S(2)}, u32[]{:S(2)}) collective-permute-start(f32[32,448]{1,0:T(8,128)S(1)} %q_part.1), channel_id=1, source_target_pairs={{0,2},{1,3},{2,0},{3,1},{4,6},{5,7},{6,4},{7,5},{8,10},{9,11},{10,... | collective-permute-start | bytes 172040 | tf_op jit(solution)/shard_map/ppermute | solution.py:178
  145.3 5.3 %collective-permute-start.4 = (f32[32,448]{1,0:T(8,128)S(1)}, f32[32,448]{1,0:T(8,128)S(1)}, u32[]{:S(2)}, u32[]{:S(2)}) collective-permute-start(f32[32,448]{1,0:T(8,128)S(1)} %q_part.1), channel_id=1, source_target_pairs={{0,3},{1,0},{2,1},{3,2},{4,7},{5,4},{6,5},{7,6},{8,11},{9,8},{10,9... | collective-permute-start | bytes 172040 | tf_op jit(solution)/shard_map/ppermute | solution.py:178
  147.3 5.5 %collective-permute-start.3 = (f32[32,448]{1,0:T(8,128)S(1)}, f32[32,448]{1,0:T(8,128)S(1)}, u32[]{:S(2)}, u32[]{:S(2)}) collective-permute-start(f32[32,448]{1,0:T(8,128)S(1)} %q_part.1), channel_id=1, source_target_pairs={{0,1},{1,2},{2,3},{3,0},{4,5},{5,6},{6,7},{7,4},{8,9},{9,10},{10,1... | collective-permute-start | bytes 172040 | tf_op jit(solution)/shard_map/ppermute | solution.py:178
  152.8 12.5 %copy-start.6 = (f32[32,448]{1,0:T(8,128)}, f32[32,448]{1,0:T(8,128)S(1)}, u32[]{:S(2)}) copy-start(f32[32,448]{1,0:T(8,128)S(1)} %add_multiply_fusion.q_ref) | copy-start | bytes 172036
  152.9 2.0 %copy-start.2 = (bf16[1,1,4096,448]{2,3,1,0:T(8,128)(2,1)S(1)}, bf16[1,1,4096,448]{2,3,1,0:T(8,128)(2,1)}, u32[]{:S(2)}) copy-start(bf16[1,1,4096,448]{2,3,1,0:T(8,128)(2,1)} %param.6) | copy-start | bytes 11010052
Sparse Core Ops, SparseCore 0:
  10.6 115.3 all-gather.1

commit v2 on v0

v2 whole, which is shorter than its diff:
```python
import functools

import jax
import jax.numpy as jnp
from jax import lax
from jax.experimental import pallas as pl
from jax.experimental.pallas import tpu as pltpu
from jax.sharding import PartitionSpec as P

F32 = jnp.float32
BF16 = jnp.bfloat16
VMEM = pl.BlockSpec(memory_space=pltpu.VMEM)
SMEM = pl.BlockSpec(memory_space=pltpu.SMEM)


def vmem(mib):
    return pltpu.CompilerParams(vmem_limit_bytes=mib * 1024 * 1024)

NT = (((1,), (1,)), ((), ()))
TN = (((0,), (0,)), ((), ()))
SOURCE_Z = (0, -1, 1, -2, 2, -3, 3, 4)


def split3(v):
    a = v.astype(BF16)
    r = v - a.astype(F32)
    b = r.astype(BF16)
    c = (r - b.astype(F32)).astype(BF16)
    return jnp.concatenate([a, b, c], axis=0)


def fold3(v):
    n = v.shape[0] // 3
    return v[:n] + v[n : 2 * n] + v[2 * n :]


def first_kernel(x_ref, q_ref, e_ref, h_ref, *outs):
    q = q_ref[...].astype(BF16)
    t = jnp.dot(q, h_ref[...], preferred_element_type=F32)
    high = t.astype(BF16)
    low = (t - high.astype(F32)).astype(BF16)
    for s, out in enumerate(outs):
        cols = pl.ds(pl.multiple_of((x_ref[0] + s) % 4 * 1024, 1024), 1024)
        eq = jnp.dot(q, e_ref[:, cols], preferred_element_type=F32)
        out[0:32, :] = high
        out[32:64, :] = low
        out[64:96, :] = eq.astype(BF16)


def first(x_index, q_t, e_t, h_t):
    return pl.pallas_call(
        first_kernel,
        in_specs=[SMEM] + [VMEM] * 3,
        out_specs=[VMEM] * 4,
        out_shape=[jax.ShapeDtypeStruct((96, 1024), BF16)] * 4,
        compiler_params=vmem(10),
        name="eq_hq",
    )(x_index, q_t, e_t, h_t)


def column_kernel(z_ref, m0_ref, m1_ref, m2_ref, m3_ref, *refs):
    x_refs, out_ref = refs[:8], refs[8]
    m = sum(r[...].astype(F32) for r in (m0_ref, m1_ref, m2_ref, m3_ref))
    t = split3(m[0:32] + m[32:64])
    eq = m[64:96]
    for j in range(8):
        out_ref[z_ref[j]] = fold3(jnp.dot(t, x_refs[j][...], preferred_element_type=F32))
    for z in range(8):
        out_ref[z] += eq[:, 128 * z : 128 * (z + 1)]


def column(z_index, messages, own):
    return pl.pallas_call(
        column_kernel,
        in_specs=[SMEM] + [VMEM] * 12,
        out_specs=VMEM,
        out_shape=jax.ShapeDtypeStruct((8, 32, 128), F32),
        compiler_params=vmem(8),
        name="p_column",
    )(z_index, *messages, *own)


def add_spread_kernel(scale, in_ref, out_ref):
    s = jnp.sum(in_ref[...], axis=0) * scale
    out_ref[...] = jnp.broadcast_to(s[None], out_ref.shape)


def add_spread(v, copies, scale):
    return pl.pallas_call(
        functools.partial(add_spread_kernel, scale),
        in_specs=[VMEM],
        out_specs=VMEM,
        out_shape=jax.ShapeDtypeStruct((copies, *v.shape[1:]), F32),
        compiler_params=vmem(4),
        name="add_spread",
    )(v)


def pack_kernel(*refs):
    rows = refs[0].shape[0]
    for i, ref in enumerate(refs[:-1]):
        refs[-1][rows * i : rows * (i + 1), :] = ref[...]


def pack(arrays):
    rows = arrays[0].shape[0]
    return pl.pallas_call(
        pack_kernel,
        in_specs=[VMEM] * len(arrays),
        out_specs=VMEM,
        out_shape=jax.ShapeDtypeStruct((rows * len(arrays), 128), BF16),
        compiler_params=vmem(6),
        name="pack",
    )(*arrays)


def correct_kernel(at_ref, h_ref, e_ref, *refs):
    x_refs, out_ref = refs[:-1], refs[-1]
    slabs = [(r, i) for r in x_refs for i in range(r.shape[0] // 1024)]
    for pair in range(len(slabs) // 2):
        two = slabs[2 * pair : 2 * pair + 2]
        x = jnp.concatenate([r[1024 * i : 1024 * (i + 1), :] for r, i in two], axis=1)
        grad = jnp.dot(h_ref[...], x, preferred_element_type=F32)
        for s in range(2):
            cols = pl.ds(pl.multiple_of(at_ref[2 * pair + s], 128), 128)
            both = e_ref[:, cols].astype(F32) + grad[:, 128 * s : 128 * (s + 1)]
            out_ref[:, cols] = both.astype(BF16)


def correct_more_kernel(at_ref, h_ref, e_ref, c_ref, *refs):
    correct_kernel(at_ref, h_ref, e_ref, *refs)


def correct(places, h_t, e_t, arrays, before=None):
    kept = [] if before is None else [before]
    return pl.pallas_call(
        correct_kernel if before is None else correct_more_kernel,
        in_specs=[SMEM] + [VMEM] * (2 + len(kept) + len(arrays)),
        out_specs=VMEM,
        out_shape=jax.ShapeDtypeStruct((448, 4096), BF16),
        input_output_aliases={} if before is None else {3: 0},
        compiler_params=vmem(22),
        name="corrected",
    )(places, h_t, e_t, *kept, *arrays)


def project_kernel(p_ref, c_ref, out_ref):
    p = split3(jnp.concatenate([p_ref[i] for i in range(32)], axis=1))
    out_ref[...] = fold3(lax.dot_general(p, c_ref[...], NT, preferred_element_type=F32))


def project(p_blocks, c_t):
    return pl.pallas_call(
        project_kernel,
        in_specs=[VMEM] * 2,
        out_specs=VMEM,
        out_shape=jax.ShapeDtypeStruct((32, 448), F32),
        compiler_params=vmem(10),
        name="c_p",
    )(p_blocks, c_t)


def factor_kernel(p_ref, inv_ref, p_out_ref, low_ref):
    p = jnp.concatenate([p_ref[i] for i in range(32)], axis=1)
    gram = lax.dot_general(
        p, p, NT, precision=lax.Precision.HIGHEST, preferred_element_type=F32
    )
    row = lax.broadcasted_iota(jnp.int32, (32, 128), 0)
    col = lax.broadcasted_iota(jnp.int32, (32, 128), 1)
    work = jnp.concatenate([gram, jnp.zeros((32, 96), F32)], axis=1)
    work = jnp.where(col == row + 32, 1.0, work)
    scale = jnp.zeros((32, 1), F32)
    for j in range(32):
        pivot = work[j : j + 1, j : j + 1]
        below = jnp.where(row[:, :1] > j, work[:, j : j + 1], 0.0)
        scale = jnp.where(row[:, :1] == j, pivot, scale)
        work = work - below * (work[j : j + 1, :] / pivot)
    inverse = work[:, 32:64] / jnp.sqrt(scale)
    inv_ref[...] = inverse
    out = jnp.dot(inverse, p, precision=lax.Precision.HIGHEST, preferred_element_type=F32)
    p_out_ref[...] = out
    low_ref[...] = out.astype(BF16)


def factor(p_blocks):
    return pl.pallas_call(
        factor_kernel,
        in_specs=[VMEM],
        out_specs=[VMEM] * 3,
        out_shape=[
            jax.ShapeDtypeStruct((32, 32), F32),
            jax.ShapeDtypeStruct((32, 4096), F32),
            jax.ShapeDtypeStruct((32, 4096), BF16),
        ],
        compiler_params=vmem(8),
        name="factor",
    )(p_blocks)


def final_kernel(inv_ref, a_ref, b_ref, c_ref, d_ref, low_ref, cor_ref, q_ref, out_ref, keep):
    @pl.when(pl.program_id(0) == 0)
    def _():
        w = (a_ref[...] + b_ref[...] + c_ref[...] + d_ref[...]) * 0.25
        q = jnp.dot(
            inv_ref[...], w, precision=lax.Precision.HIGHEST, preferred_element_type=F32
        )
        q_ref[...] = q
        keep[...] = q.astype(BF16)

    cols = pl.ds(pl.multiple_of(pl.program_id(0) * 512, 512), 512)
    approx = lax.dot_general(keep[...], low_ref[:, cols], TN, preferred_element_type=F32)
    out_ref[...] = (cor_ref[:, cols].astype(F32) - approx).astype(BF16)


def final(inverse, parts, p_low, c_t):
    whole = lambda *shape: pl.BlockSpec(shape, lambda g: (0, 0))
    return pl.pallas_call(
        final_kernel,
        grid=(8,),
        in_specs=[VMEM] * 7,
        out_specs=[whole(32, 448), pl.BlockSpec((448, 512), lambda g: (0, g))],
        out_shape=[
            jax.ShapeDtypeStruct((32, 448), F32),
            jax.ShapeDtypeStruct((448, 4096), BF16),
        ],
        scratch_shapes=[pltpu.VMEM((32, 448), BF16)],
        compiler_params=vmem(12),
        name="new_error",
    )(inverse, *parts, p_low, c_t)


def swap(v, axis="hidden", groups=None):
    return lax.all_to_all(v, axis, 0, 0, axis_index_groups=groups)


def replicas(v):
    return [v] + [
        lax.ppermute(v, "replica", [(i, (i + s) % 4) for i in range(4)]) for s in (1, 3, 2)
    ]


def move(v, dx, dz):
    pairs = [(h, (h // 8 + dx) % 4 * 8 + (h % 8 + dz) % 8) for h in range(32)]
    return lax.ppermute(v, "hidden", pairs)


def after(v, *before):
    return lax.optimization_barrier((v, *before))[0]


def shards(activations, hidden_grad, error_buffer, q_previous):
    x = activations[0]
    h_t = hidden_grad[0].T
    e_t = error_buffer[0, 0].T
    q_t = q_previous[0].T
    me = lax.axis_index("hidden")
    x_index, z_index = me // 8, me % 8
    z_order = jnp.stack([(z_index + rz) % 8 for rz in SOURCE_Z]).astype(jnp.int32)

    def places(sources):
        order = [(x_index + rx) % 4 * 1024 + z_order * 128 for rx in sources]
        return jnp.concatenate(order).astype(jnp.int32)

    mine, *others = first(x_index.astype(jnp.int32)[None], q_t, e_t, h_t)
    plus, minus = [x, move(x, 0, 1)], [x, move(x, 0, -1)]
    far = move(x, 2, 0)
    messages = [mine] + [move(m, dx, 0) for m, dx in zip(others, (1, 2, -1))]
    plus.append(move(after(plus[1], mine, far), 0, 1))
    minus.append(move(after(minus[1], mine, far), 0, -1))
    f_plus, f_minus = [after(far, plus[2], minus[2])], [after(far, plus[2], minus[2])]
    plus.append(move(plus[2], 0, 1))
    minus.append(move(minus[2], 0, -1))
    last = move(after(plus[3], *messages), 0, 1)
    own = [x, plus[1], minus[1], plus[2], minus[2], plus[3], minus[3], last]
    bundle = after(pack(own[:5]), plus[3], minus[3], *messages)
    near = [move(bundle, 1, 0), move(bundle, -1, 0)]
    bundle = pack(own[5:])
    near += [move(bundle, 1, 0), move(bundle, -1, 0)]
    for _ in range(3):
        f_plus.append(move(f_plus[-1], 0, 1))
        f_minus.append(move(f_minus[-1], 0, -1))
    f_last = move(f_minus[3], 0, -1)
    far = [far, f_plus[1], f_minus[1], f_plus[2], f_minus[2], f_plus[3], f_minus[3], f_last]
    column_groups = [[8 * i + z for z in range(8)] for i in range(4)]
    p_parts = after(column(z_order, messages, own), f_plus[1], f_minus[1])
    p_parts = swap(p_parts, groups=column_groups)
    p_parts = swap(after(add_spread(p_parts, 4, 1.0), f_plus[2], f_minus[2]), "replica")
    p_blocks = swap(after(add_spread(p_parts, 32, 0.25), f_plus[3], f_minus[3]))
    at = places((0, -1, 1, 2))
    at_first = jnp.concatenate([at[0:8], at[24:32]])
    at_second = jnp.concatenate([at[8:13], at[16:21], at[13:16], at[21:24]])
    c_t = correct(at_first, h_t, e_t, [*own, *far])
    c_t = correct(at_second, h_t, e_t, near, c_t)
    parts = replicas(project(p_blocks, c_t))
    inverse, p_factor, p_low = factor(p_blocks)
    q_factor, new_error = final(inverse, parts, p_low, c_t)
    return (p_factor.T[None], q_factor.T[None], new_error.T[None, None])


def solution(mesh):
    in_specs = (
        P("expert", "replica", "hidden"),
        P("expert", "replica", "hidden"),
        P("expert", "replica", None, "hidden"),
        P("expert", "hidden", None),
    )
    out_specs = (
        P("expert", None, None),
        P("expert", "hidden", None),
        P("expert", "replica", None, "hidden"),
    )
    return jax.shard_map(shards, mesh=mesh, in_specs=in_specs, out_specs=out_specs, check_vma=False)
```

time: 386 us -> 128 us (0.33)
  waiting for transfers between devices: 323 us -> 22.8 us
  starting transfers between devices: 0.08 us -> 47.8 us
  Pallas kernels: 0 us -> 25.6 us
  matrix products: 21.5 us -> 0 us
  local copies, waits for them, and re-layouts: 1.92 us -> 20 us
  between operations: 14.1 us -> 0.78 us
  blocking collectives: 17.4 us -> 9.89 us
  other arithmetic: 7.32 us -> 0.16 us
    psum x1 -> x0, waiting for transfers between devices: 213 us -> none  [shards(): p_sum = lax.psum(p_partial, ('hidden', 'replica')) / replicas]
    all_gather x1 -> x0, waiting for transfers between devices: 109 us -> none  [shards(): lax.all_gather(activations, 'hidden', axis=2, tiled=True)[0]]
    ppermute x0 -> x25, starting transfers between devices: none -> 33.5 us  [the longest x22 30.2 us: move(): return lax.ppermute(v, 'hidden', pairs)]
    pallas_call x0 -> x11, Pallas kernels: none -> 25.6 us  [the longest x2 9.23 us: correct(): pl.pallas_call(correct_kernel if before is None else correct_more_kernel,...]
    dot_general x5 -> x0, matrix products: 19.8 us -> none  [the longest x1 8.13 us: shards(): lax.dot_general(lax.all_gather(activations, 'hidden', axis=2, tiled=True)...]
    unnamed x8 -> x44, local copies, waits for them, and re-layouts: 1.85 us -> 19.8 us
    psum x1 -> x0, blocking collectives: 17.4 us -> none  [shards(): q_sum = lax.psum(q_partial, 'replica') / replicas]
    ppermute x0 -> x25, waiting for transfers between devices: none -> 17.2 us  [the longest x22 17.1 us: move(): return lax.ppermute(v, 'hidden', pairs)]
  transfers between devices with their start and end apart: 2 -> 27, of which waited for: 2 -> 8; matrix products, arithmetic and copies ran while one was open for 0% -> 0% of each run, Pallas kernels for 0% -> 15%
where the time goes in v2:
time: 128 us; the launch traced here: 127 us
  starting transfers between devices  47.8 us (37%)
  Pallas kernels  25.6 us (20%)
  waiting for transfers between devices  22.8 us (18%)
  local copies, waits for them, and re-layouts  20 us (16%)
  blocking collectives  9.89 us (8%)
    ppermute x22, starting transfers between devices, move(): return lax.ppermute(v, 'hidden', pairs)  30.2 us
    unnamed x44, local copies, waits for them, and re-layouts  19.8 us
    ppermute x22, waiting for transfers between devices, move(): return lax.ppermute(v, 'hidden', pairs)  17.1 us
    all_to_all x2, starting transfers between devices, swap(): return lax.all_to_all(v, axis, 0, 0, axis_index_groups=groups)  14.2 us
    all_to_all x1, blocking collectives, swap(): return lax.all_to_all(v, axis, 0, 0, axis_index_groups=groups)  9.89 us
    pallas_call x2, Pallas kernels, correct(): pl.pallas_call(correct_kernel if before is None else correct_more_kernel,...  9.23 us
    all_to_all x2, waiting for transfers between devices, swap(): return lax.all_to_all(v, axis, 0, 0, axis_index_groups=groups)  5.65 us
    pallas_call x1, Pallas kernels, factor(): pl.pallas_call(factor_kernel, in_specs=[VMEM], out_specs=[VMEM] * 3, out_...  5.45 us
  transfers between devices with their start and end apart: 27, of which 8 were waited for; matrix products, arithmetic and copies ran while one was open for 0% of the time, Pallas kernels for 15%

profile of v2, /device:TPU:32, one launch (start us, length us, event | category | flops | bytes accessed | tf_op | source)
XLA Modules:
  0.0 127.0 jit_solution(3305151730813014005)
XLA Ops:
  0.6 3.1 %collective-permute-start.5 = (bf16[1024,128]{1,0:T(8,128)(2,1)}, bf16[1024,128]{1,0:T(8,128)(2,1)S(1)}, u32[]{:S(2)}, u32[]{:S(2)}) collective-permute-start(bf16[1024,128]{1,0:T(8,128)(2,1)} %bitcast.36), channel_id=1, source_target_pairs={{0,64},{4,68},{8,72},{12,76},{16,80},{20,84},{24,88},{28,92},{32,9... | collective-permute-start | bytes 786440 | tf_op jit(solution)/shard_map/ppermute | solution.py:244
  3.7 1.9 %collective-permute-start.3 = (bf16[1024,128]{1,0:T(8,128)(2,1)}, bf16[1024,128]{1,0:T(8,128)(2,1)S(1)}, u32[]{:S(2)}, u32[]{:S(2)}) collective-permute-start(bf16[1024,128]{1,0:T(8,128)(2,1)} %bitcast.37), channel_id=1, source_target_pairs={{0,4},{4,8},{8,12},{12,16},{16,20},{20,24},{24,28},{28,0},{32,36},... | collective-permute-start | bytes 786440 | tf_op jit(solution)/shard_map/ppermute | solution.py:244
  5.8 2.0 %copy-done.3 = bf16[1,1,4096,448]{2,3,1,0:T(8,128)(2,1)S(1)} copy-done((bf16[1,1,4096,448]{2,3,1,0:T(8,128)(2,1)S(1)}, bf16[1,1,4096,448]{2,3,1,0:T(8,128)(2,1)}, u32[]{:S(2)}) %copy-start.3) | copy-done | bytes 3670040
  7.8 1.2 copy-done.5
  9.0 0.8 copy-done.21
  9.8 0.9 eq_hq.1
  11.7 1.9 %collective-permute-start.6 = (bf16[1024,128]{1,0:T(8,128)(2,1)S(1)}, bf16[1024,128]{1,0:T(8,128)(2,1)S(1)}, u32[]{:S(2)}, u32[]{:S(2)}) collective-permute-start(bf16[1024,128]{1,0:T(8,128)(2,1)S(1)} %collective-permute-done.3.refs_1_), channel_id=1, source_target_pairs={{0,4},{4,8},{8,12},{12,16},{16,20},{20,24},{24,28},{28,0},{32,36},... | collective-permute-start | bytes 786440 | tf_op jit(solution)/shard_map/ppermute | solution.py:244
  13.6 2.3 %collective-permute-start.7 = (bf16[1024,128]{1,0:T(8,128)(2,1)S(1)}, bf16[1024,128]{1,0:T(8,128)(2,1)S(1)}, u32[]{:S(2)}, u32[]{:S(2)}) collective-permute-start(bf16[1024,128]{1,0:T(8,128)(2,1)S(1)} %collective-permute-done.4.refs_2_), channel_id=1, source_target_pairs={{0,28},{4,0},{8,4},{12,8},{16,12},{20,16},{24,20},{28,24},{32,60},... | collective-permute-start | bytes 786440 | tf_op jit(solution)/shard_map/ppermute | solution.py:244
  16.6 4.8 %collective-permute-done.6.refs_3_ = bf16[1024,128]{1,0:T(8,128)(2,1)S(1)} collective-permute-done((bf16[1024,128]{1,0:T(8,128)(2,1)S(1)}, bf16[1024,128]{1,0:T(8,128)(2,1)S(1)}, u32[]{:S(2)}, u32[]{:S(2)}) %collective-permute-start.6) | collective-permute-done | bytes 262176 | tf_op jit(solution)/shard_map/ppermute | solution.py:244
  21.9 2.5 %collective-permute-start.12 = (bf16[1024,128]{1,0:T(8,128)(2,1)S(1)}, bf16[1024,128]{1,0:T(8,128)(2,1)S(1)}, u32[]{:S(2)}, u32[]{:S(2)}) collective-permute-start(bf16[1024,128]{1,0:T(8,128)(2,1)S(1)} %collective-permute-done.5.refs_8_), channel_id=1, source_target_pairs={{0,28},{4,0},{8,4},{12,8},{16,12},{20,16},{24,20},{28,24},{32,60},... | collective-permute-start | bytes 786440 | tf_op jit(solution)/shard_map/ppermute | solution.py:244
  24.8 0.7 copy-done.9
  25.5 0.8 collective-permute-start.1
  26.3 0.7 copy-done.15
  27.0 2.4 %collective-permute-start.2 = (bf16[96,1024]{1,0:T(8,128)(2,1)S(1)}, bf16[96,1024]{1,0:T(8,128)(2,1)S(1)}, u32[]{:S(2)}, u32[]{:S(2)}) collective-permute-start(bf16[96,1024]{1,0:T(8,128)(2,1)S(1)} %get-tuple-element.23), channel_id=1, source_target_pairs={{0,96},{4,100},{8,104},{12,108},{16,112},{20,116},{24,120},{28,124... | collective-permute-start | bytes 589832 | tf_op jit(solution)/shard_map/ppermute | solution.py:244
  29.5 3.2 %collective-permute-done.1.m2_ref = bf16[96,1024]{1,0:T(8,128)(2,1)S(1)} collective-permute-done((bf16[96,1024]{1,0:T(8,128)(2,1)S(1)}, bf16[96,1024]{1,0:T(8,128)(2,1)S(1)}, u32[]{:S(2)}, u32[]{:S(2)}) %collective-permute-start.1) | collective-permute-done | bytes 196640 | tf_op jit(solution)/shard_map/ppermute | solution.py:244
  33.4 2.8 %collective-permute-start.9 = (bf16[1024,128]{1,0:T(8,128)(2,1)S(1)}, bf16[1024,128]{1,0:T(8,128)(2,1)S(1)}, u32[]{:S(2)}, u32[]{:S(2)}) collective-permute-start(bf16[1024,128]{1,0:T(8,128)(2,1)S(1)} %collective-permute-done.7.refs_4_), channel_id=1, source_target_pairs={{0,28},{4,0},{8,4},{12,8},{16,12},{20,16},{24,20},{28,24},{32,60},... | collective-permute-start | bytes 786440 | tf_op jit(solution)/shard_map/ppermute | solution.py:244
  36.1 0.7 copy-done.19
  36.8 0.9 collective-permute-start.10
  37.7 2.5 %collective-permute-start.14 = (bf16[1024,128]{1,0:T(8,128)(2,1)S(1)}, bf16[1024,128]{1,0:T(8,128)(2,1)}, u32[]{:S(2)}, u32[]{:S(2)}) collective-permute-start(bf16[1024,128]{1,0:T(8,128)(2,1)S(1)} %collective-permute-done.12.refs_10_), channel_id=1, source_target_pairs={{0,28},{4,0},{8,4},{12,8},{16,12},{20,16},{24,20},{28,24},{32,60},... | collective-permute-start | bytes 786440 | tf_op jit(solution)/shard_map/ppermute | solution.py:244
  40.8 1.1 pack.2
  41.9 1.0 collective-permute-done.9.refs_6_.refs_1_
  43.0 1.8 %collective-permute-start.19 = (bf16[5120,128]{1,0:T(8,128)(2,1)}, bf16[5120,128]{1,0:T(8,128)(2,1)}, u32[]{:S(2)}, u32[]{:S(2)}) collective-permute-start(bf16[5120,128]{1,0:T(8,128)(2,1)} %pack.2), channel_id=1, source_target_pairs={{0,96},{4,100},{8,104},{12,108},{16,112},{20,116},{24,120},{28,124... | collective-permute-start | bytes 3932168 | tf_op jit(solution)/shard_map/ppermute | solution.py:244
  45.2 0.9 copy-done.14
  46.1 0.9 copy-done.16
  47.1 0.9 copy-done.18
  48.0 0.9 copy-done.20
  48.9 1.8 %p_column.1 = f32[8,32,128]{2,1,0:T(8,128)} custom-call(s32[8]{0:T(128)S(1)} %stack.35.z_ref, bf16[96,1024]{1,0:T(8,128)(2,1)S(1)} %copy-done.14, bf16[96,1024]{1,0:T(8,128)(2,1)S(1)} %copy-done.16, bf16[96,1024]{1,0:T(8,128)(2,1)S(1)} %copy-done.18, bf16[96,1024]{1,0:T(8,128)(2,1)S(1)} %copy-done.20, bf16[1024,128]{1,0:T(8,128)(2,1)S(1)} %bitcast.40, ...), custom_call_target="tpu_custom_call" | custom-call | tf_op jit(solution)/shard_map/p_column/pallas_call | solution.py:73
  50.7 8.0 %all-to-all-start = ((f32[8,32,128]{2,1,0:T(8,128)}), f32[8,32,128]{2,1,0:T(8,128)S(1)}, u32[]{:S(2)}, u32[]{:S(2)}) async-start(f32[8,32,128]{2,1,0:T(8,128)} %p_column.1), calls=%async_computation | async-start | bytes 262144 | tf_op jit(solution)/shard_map/all_to_all | solution.py:233
  58.9 1.9 %collective-permute-start.15 = (bf16[1024,128]{1,0:T(8,128)(2,1)}, bf16[1024,128]{1,0:T(8,128)(2,1)}, u32[]{:S(2)}, u32[]{:S(2)}) collective-permute-start(bf16[1024,128]{1,0:T(8,128)(2,1)} %collective-permute-done.13.refs_11_), channel_id=1, source_target_pairs={{0,4},{4,8},{8,12},{12,16},{16,20},{20,24},{24,28},{28,0},{32,36},... | collective-permute-start | bytes 786440 | tf_op jit(solution)/shard_map/ppermute | solution.py:244
  60.8 5.7 %all-to-all-done.in_ref = f32[8,32,128]{2,1,0:T(8,128)S(1)} async-done(((f32[8,32,128]{2,1,0:T(8,128)}), f32[8,32,128]{2,1,0:T(8,128)S(1)}, u32[]{:S(2)}, u32[]{:S(2)}) %all-to-all-start) | async-done | bytes 131104 | tf_op jit(solution)/shard_map/all_to_all | solution.py:233
  66.5 9.9 %all_to_all.15.in_ref = f32[4,32,128]{2,1,0:T(8,128)S(1)} all-to-all(f32[4,32,128]{2,1,0:T(8,128)S(1)} %add_spread.2), channel_id=1, replica_groups=mesh['expert'=2,'hidden'=32,'replica'=4] {'replica'}, dimensions={0} | all-to-all | bytes 131072 | tf_op jit(solution)/shard_map/all_to_all | solution.py:233
  76.4 0.8 copy-done.8
  77.2 6.2 %all-to-all-start.2 = ((f32[32,32,128]{2,1,0:T(8,128)}), f32[32,32,128]{2,1,0:T(8,128)S(1)}, u32[]{:S(2)}, u32[]{:S(2)}) async-start(f32[32,32,128]{2,1,0:T(8,128)} %copy-done.8), calls=%async_computation.2 | async-start | bytes 1048576 | tf_op jit(solution)/shard_map/all_to_all | solution.py:233
  83.4 0.9 pack.3
  84.4 2.7 %collective-permute-start.21 = (bf16[3072,128]{1,0:T(8,128)(2,1)}, bf16[3072,128]{1,0:T(8,128)(2,1)}, u32[]{:S(2)}, u32[]{:S(2)}) collective-permute-start(bf16[3072,128]{1,0:T(8,128)(2,1)} %pack.3), channel_id=1, source_target_pairs={{0,96},{4,100},{8,104},{12,108},{16,112},{20,116},{24,120},{28,124... | collective-permute-start | bytes 2359304 | tf_op jit(solution)/shard_map/ppermute | solution.py:244
  88.0 7.1 %collective-permute-done.17.refs_15_ = bf16[1024,128]{1,0:T(8,128)(2,1)S(1)} collective-permute-done((bf16[1024,128]{1,0:T(8,128)(2,1)}, bf16[1024,128]{1,0:T(8,128)(2,1)S(1)}, u32[]{:S(2)}, u32[]{:S(2)}) %collective-permute-start.17) | collective-permute-done | bytes 262176 | tf_op jit(solution)/shard_map/ppermute | solution.py:244
  95.1 2.0 %copy-done.4 = bf16[1,1,4096,448]{2,3,1,0:T(8,128)(2,1)S(1)} copy-done((bf16[1,1,4096,448]{2,3,1,0:T(8,128)(2,1)S(1)}, bf16[1,1,4096,448]{2,3,1,0:T(8,128)(2,1)}, u32[]{:S(2)}) %copy-start.4) | copy-done | bytes 3670040
  97.1 0.9 copy-done.10
  98.1 0.9 copy-done.12
  99.0 4.2 %corrected.2.c_ref = bf16[448,4096]{1,0:T(8,128)(2,1)S(1)} custom-call(s32[16]{0:T(128)S(1)} %pad_add_fusion.1.at_ref, bf16[448,1024]{1,0:T(8,128)(2,1)S(1)} %bitcast.34, bf16[448,4096]{1,0:T(8,128)(2,1)S(1)} %bitcast.31, bf16[1024,128]{1,0:T(8,128)(2,1)S(1)} %bitcast.41, bf16[1024,128]{1,0:T(8,128)(2,1)S(1)} %collective-permute-done.3.refs_1_, ...), custom_call_target="tpu_custom_call" | custom-call | tf_op jit(solution)/shard_map/corrected/pallas_call | solution.py:136
  103.3 5.0 %corrected.3.c_ref.cor_ref = bf16[448,4096]{1,0:T(8,128)(2,1)S(1)} custom-call(s32[16]{0:T(128)S(1)} %pad_add_fusion.at_ref, bf16[448,1024]{1,0:T(8,128)(2,1)S(1)} %bitcast.35, bf16[448,4096]{1,0:T(8,128)(2,1)S(1)} %bitcast.32, bf16[448,4096]{1,0:T(8,128)(2,1)S(1)} %corrected.2.c_ref, ...), custom_call_target="tpu_custom_call", output_to_operand_aliasing={{}: (3, {})} | custom-call | tf_op jit(solution)/shard_map/corrected/pallas_call | solution.py:136
  108.3 1.8 %copy-done = bf16[448,4096]{1,0:T(8,128)(2,1)} copy-done((bf16[448,4096]{1,0:T(8,128)(2,1)}, bf16[448,4096]{1,0:T(8,128)(2,1)S(1)}, u32[]{:S(2)}) %copy-start) | copy-done | bytes 3670040
  110.2 2.0 %copy-done.1 = bf16[448,4096]{1,0:T(8,128)(2,1)S(1)} copy-done((bf16[448,4096]{1,0:T(8,128)(2,1)S(1)}, bf16[448,4096]{1,0:T(8,128)(2,1)}, u32[]{:S(2)}) %copy-start.1) | copy-done | bytes 3670040
  112.2 1.2 c_p.1.a_ref
  113.4 1.0 collective-permute-start.24
  114.4 2.3 %collective-permute-start.23 = (f32[32,448]{1,0:T(8,128)S(1)}, f32[32,448]{1,0:T(8,128)S(1)}, u32[]{:S(2)}, u32[]{:S(2)}) collective-permute-start(f32[32,448]{1,0:T(8,128)S(1)} %c_p.1.a_ref), channel_id=1, source_target_pairs={{0,3},{1,0},{2,1},{3,2},{4,7},{5,4},{6,5},{7,6},{8,11},{9,8},{10,9... | collective-permute-start | bytes 172040 | tf_op jit(solution)/shard_map/ppermute | solution.py:238
  116.7 5.4 %factor.1 = (f32[32,32]{1,0:T(8,128)S(1)}, f32[32,4096]{1,0:T(8,128)}, bf16[32,4096]{1,0:T(8,128)(2,1)S(1)}) custom-call(f32[32,32,128]{2,1,0:T(8,128)S(1)} %all-to-all-done.2.p_ref), custom_call_target="tpu_custom_call" | custom-call | tf_op jit(solution)/shard_map/factor/pallas_call | solution.py:186
  122.2 4.8 %new_error.1 = (f32[32,448]{1,0:T(8,128)}, bf16[448,4096]{1,0:T(8,128)(2,1)}) custom-call(f32[32,32]{1,0:T(8,128)S(1)} %get-tuple-element.32.inv_ref, f32[32,448]{1,0:T(8,128)S(1)} %c_p.1.a_ref, f32[32,448]{1,0:T(8,128)S(1)} %collective-permute-done.22.b_ref, f32[32,448]{1,0:T(8,128)S(1)} %collective-permute-done.23.c_ref, ...), custom_call_target="tpu_custom_call" | custom-call | tf_op jit(solution)/shard_map/new_error/pallas_call | solution.py:217
  (68 shorter events, 5.4 us)
Async XLA Ops:
  0.6 10.8 %collective-permute-start.5 = (bf16[1024,128]{1,0:T(8,128)(2,1)}, bf16[1024,128]{1,0:T(8,128)(2,1)S(1)}, u32[]{:S(2)}, u32[]{:S(2)}) collective-permute-start(bf16[1024,128]{1,0:T(8,128)(2,1)} %bitcast.36), channel_id=1, source_target_pairs={{0,64},{4,68},{8,72},{12,76},{16,80},{20,84},{24,88},{28,92},{32,9... | collective-permute-start | bytes 786440 | tf_op jit(solution)/shard_map/ppermute | solution.py:244
  3.7 8.0 %collective-permute-start.3 = (bf16[1024,128]{1,0:T(8,128)(2,1)}, bf16[1024,128]{1,0:T(8,128)(2,1)S(1)}, u32[]{:S(2)}, u32[]{:S(2)}) collective-permute-start(bf16[1024,128]{1,0:T(8,128)(2,1)} %bitcast.37), channel_id=1, source_target_pairs={{0,4},{4,8},{8,12},{12,16},{16,20},{20,24},{24,28},{28,0},{32,36},... | collective-permute-start | bytes 786440 | tf_op jit(solution)/shard_map/ppermute | solution.py:244
  5.7 8.0 %collective-permute-start.4 = (bf16[1024,128]{1,0:T(8,128)(2,1)}, bf16[1024,128]{1,0:T(8,128)(2,1)S(1)}, u32[]{:S(2)}, u32[]{:S(2)}) collective-permute-start(bf16[1024,128]{1,0:T(8,128)(2,1)} %bitcast.38), channel_id=1, source_target_pairs={{0,28},{4,0},{8,4},{12,8},{16,12},{20,16},{24,20},{28,24},{32,60},... | collective-permute-start | bytes 786440 | tf_op jit(solution)/shard_map/ppermute | solution.py:244
  5.8 2.0 %copy-start.3 = (bf16[1,1,4096,448]{2,3,1,0:T(8,128)(2,1)S(1)}, bf16[1,1,4096,448]{2,3,1,0:T(8,128)(2,1)}, u32[]{:S(2)}) copy-start(bf16[1,1,4096,448]{2,3,1,0:T(8,128)(2,1)} %param.6) | copy-start | bytes 11010052
  7.8 1.2 copy-start.5
  9.0 0.8 copy-start.21
  9.8 30.9 %copy-start.7 = (bf16[1,1024,128]{2,1,0:T(8,128)(2,1)S(1)}, bf16[1,1024,128]{2,1,0:T(8,128)(2,1)}, u32[]{:S(2)}) copy-start(bf16[1,1024,128]{2,1,0:T(8,128)(2,1)} %param.4) | copy-start | bytes 786436
  10.8 0.7 copy-start.13
  11.7 9.7 %collective-permute-start.6 = (bf16[1024,128]{1,0:T(8,128)(2,1)S(1)}, bf16[1024,128]{1,0:T(8,128)(2,1)S(1)}, u32[]{:S(2)}, u32[]{:S(2)}) collective-permute-start(bf16[1024,128]{1,0:T(8,128)(2,1)S(1)} %collective-permute-done.3.refs_1_), channel_id=1, source_target_pairs={{0,4},{4,8},{8,12},{12,16},{16,20},{20,24},{24,28},{28,0},{32,36},... | collective-permute-start | bytes 786440 | tf_op jit(solution)/shard_map/ppermute | solution.py:244
  13.6 8.2 %collective-permute-start.7 = (bf16[1024,128]{1,0:T(8,128)(2,1)S(1)}, bf16[1024,128]{1,0:T(8,128)(2,1)S(1)}, u32[]{:S(2)}, u32[]{:S(2)}) collective-permute-start(bf16[1024,128]{1,0:T(8,128)(2,1)S(1)} %collective-permute-done.4.refs_2_), channel_id=1, source_target_pairs={{0,28},{4,0},{8,4},{12,8},{16,12},{20,16},{24,20},{28,24},{32,60},... | collective-permute-start | bytes 786440 | tf_op jit(solution)/shard_map/ppermute | solution.py:244
  16.0 10.3 %collective-permute-start = (bf16[96,1024]{1,0:T(8,128)(2,1)S(1)}, bf16[96,1024]{1,0:T(8,128)(2,1)S(1)}, u32[]{:S(2)}, u32[]{:S(2)}) collective-permute-start(bf16[96,1024]{1,0:T(8,128)(2,1)S(1)} %get-tuple-element.21), channel_id=1, source_target_pairs={{0,32},{4,36},{8,40},{12,44},{16,48},{20,52},{24,56},{28,60},{32,6... | collective-permute-start | bytes 589832 | tf_op jit(solution)/shard_map/ppermute | solution.py:244
  21.4 15.4 %collective-permute-start.8 = (bf16[1024,128]{1,0:T(8,128)(2,1)S(1)}, bf16[1024,128]{1,0:T(8,128)(2,1)S(1)}, u32[]{:S(2)}, u32[]{:S(2)}) collective-permute-start(bf16[1024,128]{1,0:T(8,128)(2,1)S(1)} %collective-permute-done.6.refs_3_), channel_id=1, source_target_pairs={{0,4},{4,8},{8,12},{12,16},{16,20},{20,24},{24,28},{28,0},{32,36},... | collective-permute-start | bytes 786440 | tf_op jit(solution)/shard_map/ppermute | solution.py:244
  21.9 15.9 %collective-permute-start.12 = (bf16[1024,128]{1,0:T(8,128)(2,1)S(1)}, bf16[1024,128]{1,0:T(8,128)(2,1)S(1)}, u32[]{:S(2)}, u32[]{:S(2)}) collective-permute-start(bf16[1024,128]{1,0:T(8,128)(2,1)S(1)} %collective-permute-done.5.refs_8_), channel_id=1, source_target_pairs={{0,28},{4,0},{8,4},{12,8},{16,12},{20,16},{24,20},{28,24},{32,60},... | collective-permute-start | bytes 786440 | tf_op jit(solution)/shard_map/ppermute | solution.py:244
  24.4 15.8 %collective-permute-start.11 = (bf16[1024,128]{1,0:T(8,128)(2,1)S(1)}, bf16[1024,128]{1,0:T(8,128)(2,1)}, u32[]{:S(2)}, u32[]{:S(2)}) collective-permute-start(bf16[1024,128]{1,0:T(8,128)(2,1)S(1)} %collective-permute-done.5.refs_8_), channel_id=1, source_target_pairs={{0,4},{4,8},{8,12},{12,16},{16,20},{20,24},{24,28},{28,0},{32,36},... | collective-permute-start | bytes 786440 | tf_op jit(solution)/shard_map/ppermute | solution.py:244
  24.8 0.7 copy-start.9
  25.5 7.2 %collective-permute-start.1 = (bf16[96,1024]{1,0:T(8,128)(2,1)S(1)}, bf16[96,1024]{1,0:T(8,128)(2,1)S(1)}, u32[]{:S(2)}, u32[]{:S(2)}) collective-permute-start(bf16[96,1024]{1,0:T(8,128)(2,1)S(1)} %get-tuple-element.22), channel_id=1, source_target_pairs={{0,64},{4,68},{8,72},{12,76},{16,80},{20,84},{24,88},{28,92},{32,9... | collective-permute-start | bytes 589832 | tf_op jit(solution)/shard_map/ppermute | solution.py:244
  26.3 0.7 copy-start.15
  27.0 9.1 %collective-permute-start.2 = (bf16[96,1024]{1,0:T(8,128)(2,1)S(1)}, bf16[96,1024]{1,0:T(8,128)(2,1)S(1)}, u32[]{:S(2)}, u32[]{:S(2)}) collective-permute-start(bf16[96,1024]{1,0:T(8,128)(2,1)S(1)} %get-tuple-element.23), channel_id=1, source_target_pairs={{0,96},{4,100},{8,104},{12,108},{16,112},{20,116},{24,120},{28,124... | collective-permute-start | bytes 589832 | tf_op jit(solution)/shard_map/ppermute | solution.py:244
  33.4 9.6 %collective-permute-start.9 = (bf16[1024,128]{1,0:T(8,128)(2,1)S(1)}, bf16[1024,128]{1,0:T(8,128)(2,1)S(1)}, u32[]{:S(2)}, u32[]{:S(2)}) collective-permute-start(bf16[1024,128]{1,0:T(8,128)(2,1)S(1)} %collective-permute-done.7.refs_4_), channel_id=1, source_target_pairs={{0,28},{4,0},{8,4},{12,8},{16,12},{20,16},{24,20},{28,24},{32,60},... | collective-permute-start | bytes 786440 | tf_op jit(solution)/shard_map/ppermute | solution.py:244
  36.1 0.7 copy-start.19
  36.8 8.4 %collective-permute-start.10 = (bf16[1024,128]{1,0:T(8,128)(2,1)S(1)}, bf16[1024,128]{1,0:T(8,128)(2,1)S(1)}, u32[]{:S(2)}, u32[]{:S(2)}) collective-permute-start(bf16[1024,128]{1,0:T(8,128)(2,1)S(1)} %collective-permute-done.8.refs_5_.refs_0_), channel_id=1, source_target_pairs={{0,4},{4,8},{8,12},{12,16},{16,20},{20,24},{24,28},{28,0},{32,36},... | collective-permute-start | bytes 786440 | tf_op jit(solution)/shard_map/ppermute | solution.py:244
  37.7 39.5 %copy-start.11 = (bf16[1024,128]{1,0:T(8,128)(2,1)}, bf16[1024,128]{1,0:T(8,128)(2,1)S(1)}, u32[]{:S(2)}) copy-start(bf16[1024,128]{1,0:T(8,128)(2,1)S(1)} %collective-permute-done.12.refs_10_) | copy-start | bytes 786436
  37.7 21.0 %collective-permute-start.14 = (bf16[1024,128]{1,0:T(8,128)(2,1)S(1)}, bf16[1024,128]{1,0:T(8,128)(2,1)}, u32[]{:S(2)}, u32[]{:S(2)}) collective-permute-start(bf16[1024,128]{1,0:T(8,128)(2,1)S(1)} %collective-permute-done.12.refs_10_), channel_id=1, source_target_pairs={{0,28},{4,0},{8,4},{12,8},{16,12},{20,16},{24,20},{28,24},{32,60},... | collective-permute-start | bytes 786440 | tf_op jit(solution)/shard_map/ppermute | solution.py:244
  40.2 18.7 %collective-permute-start.13 = (bf16[1024,128]{1,0:T(8,128)(2,1)}, bf16[1024,128]{1,0:T(8,128)(2,1)}, u32[]{:S(2)}, u32[]{:S(2)}) collective-permute-start(bf16[1024,128]{1,0:T(8,128)(2,1)} %collective-permute-done.11.refs_9_), channel_id=1, source_target_pairs={{0,4},{4,8},{8,12},{12,16},{16,20},{20,24},{24,28},{28,0},{32,36},... | collective-permute-start | bytes 786440 | tf_op jit(solution)/shard_map/ppermute | solution.py:244
  41.9 53.2 %copy-start.6 = (bf16[1,1024,448]{1,2,0:T(8,128)(2,1)S(1)}, bf16[1,1024,448]{1,2,0:T(8,128)(2,1)}, u32[]{:S(2)}) copy-start(bf16[1,1024,448]{1,2,0:T(8,128)(2,1)} %param.5) | copy-start | bytes 2752516
  43.0 60.3 %collective-permute-start.19 = (bf16[5120,128]{1,0:T(8,128)(2,1)}, bf16[5120,128]{1,0:T(8,128)(2,1)}, u32[]{:S(2)}, u32[]{:S(2)}) collective-permute-start(bf16[5120,128]{1,0:T(8,128)(2,1)} %pack.2), channel_id=1, source_target_pairs={{0,96},{4,100},{8,104},{12,108},{16,112},{20,116},{24,120},{28,124... | collective-permute-start | bytes 3932168 | tf_op jit(solution)/shard_map/ppermute | solution.py:244
  44.8 58.5 %collective-permute-start.18 = (bf16[5120,128]{1,0:T(8,128)(2,1)}, bf16[5120,128]{1,0:T(8,128)(2,1)}, u32[]{:S(2)}, u32[]{:S(2)}) collective-permute-start(bf16[5120,128]{1,0:T(8,128)(2,1)} %pack.2), channel_id=1, source_target_pairs={{0,32},{4,36},{8,40},{12,44},{16,48},{20,52},{24,56},{28,60},{32,6... | collective-permute-start | bytes 3932168 | tf_op jit(solution)/shard_map/ppermute | solution.py:244
  45.2 0.9 copy-start.14
  46.1 0.9 copy-start.16
  47.1 0.9 copy-start.18
  48.0 0.9 copy-start.20
  50.7 15.7 %all-to-all-start = ((f32[8,32,128]{2,1,0:T(8,128)}), f32[8,32,128]{2,1,0:T(8,128)S(1)}, u32[]{:S(2)}, u32[]{:S(2)}) async-start(f32[8,32,128]{2,1,0:T(8,128)} %p_column.1), calls=%async_computation | async-start | bytes 262144 | tf_op jit(solution)/shard_map/all_to_all | solution.py:233
  58.8 18.4 %collective-permute-start.16 = (bf16[1024,128]{1,0:T(8,128)(2,1)}, bf16[1024,128]{1,0:T(8,128)(2,1)}, u32[]{:S(2)}, u32[]{:S(2)}) collective-permute-start(bf16[1024,128]{1,0:T(8,128)(2,1)} %collective-permute-done.14.refs_12_), channel_id=1, source_target_pairs={{0,28},{4,0},{8,4},{12,8},{16,12},{20,16},{24,20},{28,24},{32,60},... | collective-permute-start | bytes 786440 | tf_op jit(solution)/shard_map/ppermute | solution.py:244
  58.9 18.4 %collective-permute-start.15 = (bf16[1024,128]{1,0:T(8,128)(2,1)}, bf16[1024,128]{1,0:T(8,128)(2,1)}, u32[]{:S(2)}, u32[]{:S(2)}) collective-permute-start(bf16[1024,128]{1,0:T(8,128)(2,1)} %collective-permute-done.13.refs_11_), channel_id=1, source_target_pairs={{0,4},{4,8},{8,12},{12,16},{16,20},{20,24},{24,28},{28,0},{32,36},... | collective-permute-start | bytes 786440 | tf_op jit(solution)/shard_map/ppermute | solution.py:244
  76.4 0.8 copy-start.8
  77.2 32.9 %all-to-all-start.2 = ((f32[32,32,128]{2,1,0:T(8,128)}), f32[32,32,128]{2,1,0:T(8,128)S(1)}, u32[]{:S(2)}, u32[]{:S(2)}) async-start(f32[32,32,128]{2,1,0:T(8,128)} %copy-done.8), calls=%async_computation.2 | async-start | bytes 1048576 | tf_op jit(solution)/shard_map/all_to_all | solution.py:233
  84.4 18.9 %collective-permute-start.21 = (bf16[3072,128]{1,0:T(8,128)(2,1)}, bf16[3072,128]{1,0:T(8,128)(2,1)}, u32[]{:S(2)}, u32[]{:S(2)}) collective-permute-start(bf16[3072,128]{1,0:T(8,128)(2,1)} %pack.3), channel_id=1, source_target_pairs={{0,96},{4,100},{8,104},{12,108},{16,112},{20,116},{24,120},{28,124... | collective-permute-start | bytes 2359304 | tf_op jit(solution)/shard_map/ppermute | solution.py:244
  87.1 16.1 %collective-permute-start.20 = (bf16[3072,128]{1,0:T(8,128)(2,1)}, bf16[3072,128]{1,0:T(8,128)(2,1)}, u32[]{:S(2)}, u32[]{:S(2)}) collective-permute-start(bf16[3072,128]{1,0:T(8,128)(2,1)} %pack.3), channel_id=1, source_target_pairs={{0,32},{4,36},{8,40},{12,44},{16,48},{20,52},{24,56},{28,60},{32,6... | collective-permute-start | bytes 2359304 | tf_op jit(solution)/shard_map/ppermute | solution.py:244
  87.1 8.0 %collective-permute-start.17 = (bf16[1024,128]{1,0:T(8,128)(2,1)}, bf16[1024,128]{1,0:T(8,128)(2,1)S(1)}, u32[]{:S(2)}, u32[]{:S(2)}) collective-permute-start(bf16[1024,128]{1,0:T(8,128)(2,1)} %collective-permute-done.16.refs_14_), channel_id=1, source_target_pairs={{0,28},{4,0},{8,4},{12,8},{16,12},{20,16},{24,20},{28,24},{32,60},... | collective-permute-start | bytes 786440 | tf_op jit(solution)/shard_map/ppermute | solution.py:244
  95.1 2.0 %copy-start.4 = (bf16[1,1,4096,448]{2,3,1,0:T(8,128)(2,1)S(1)}, bf16[1,1,4096,448]{2,3,1,0:T(8,128)(2,1)}, u32[]{:S(2)}) copy-start(bf16[1,1,4096,448]{2,3,1,0:T(8,128)(2,1)} %param.6) | copy-start | bytes 11010052
  97.1 0.9 copy-start.10
  98.1 0.9 copy-start.12
  108.3 1.8 %copy-start = (bf16[448,4096]{1,0:T(8,128)(2,1)}, bf16[448,4096]{1,0:T(8,128)(2,1)S(1)}, u32[]{:S(2)}) copy-start(bf16[448,4096]{1,0:T(8,128)(2,1)S(1)} %corrected.3.c_ref.cor_ref) | copy-start | bytes 11010052
  110.2 2.0 %copy-start.1 = (bf16[448,4096]{1,0:T(8,128)(2,1)S(1)}, bf16[448,4096]{1,0:T(8,128)(2,1)}, u32[]{:S(2)}) copy-start(bf16[448,4096]{1,0:T(8,128)(2,1)} %copy-done) | copy-start | bytes 11010052
  112.2 10.0 %copy-start.2 = (bf16[448,4096]{1,0:T(8,128)(2,1)S(1)}, bf16[448,4096]{1,0:T(8,128)(2,1)}, u32[]{:S(2)}) copy-start(bf16[448,4096]{1,0:T(8,128)(2,1)} %copy-done) | copy-start | bytes 11010052
  113.4 8.8 %collective-permute-start.24 = (f32[32,448]{1,0:T(8,128)S(1)}, f32[32,448]{1,0:T(8,128)S(1)}, u32[]{:S(2)}, u32[]{:S(2)}) collective-permute-start(f32[32,448]{1,0:T(8,128)S(1)} %c_p.1.a_ref), channel_id=1, source_target_pairs={{0,2},{1,3},{2,0},{3,1},{4,6},{5,7},{6,4},{7,5},{8,10},{9,11},{10,... | collective-permute-start | bytes 172040 | tf_op jit(solution)/shard_map/ppermute | solution.py:238
  114.4 7.7 %collective-permute-start.23 = (f32[32,448]{1,0:T(8,128)S(1)}, f32[32,448]{1,0:T(8,128)S(1)}, u32[]{:S(2)}, u32[]{:S(2)}) collective-permute-start(f32[32,448]{1,0:T(8,128)S(1)} %c_p.1.a_ref), channel_id=1, source_target_pairs={{0,3},{1,0},{2,1},{3,2},{4,7},{5,4},{6,5},{7,6},{8,11},{9,8},{10,9... | collective-permute-start | bytes 172040 | tf_op jit(solution)/shard_map/ppermute | solution.py:238
  116.7 5.5 %collective-permute-start.22 = (f32[32,448]{1,0:T(8,128)S(1)}, f32[32,448]{1,0:T(8,128)S(1)}, u32[]{:S(2)}, u32[]{:S(2)}) collective-permute-start(f32[32,448]{1,0:T(8,128)S(1)} %c_p.1.a_ref), channel_id=1, source_target_pairs={{0,1},{1,2},{2,3},{3,0},{4,5},{5,6},{6,7},{7,4},{8,9},{9,10},{10,1... | collective-permute-start | bytes 172040 | tf_op jit(solution)/shard_map/ppermute | solution.py:238
  (1 other events, 0.7 us)

commit v3 on v2

v3 whole, which is shorter than its diff:
```python
import functools

import jax
import jax.numpy as jnp
from jax import lax
from jax.experimental import pallas as pl
from jax.experimental.pallas import tpu as pltpu
from jax.sharding import PartitionSpec as P

F32 = jnp.float32
BF16 = jnp.bfloat16
VMEM = pl.BlockSpec(memory_space=pltpu.VMEM)
SMEM = pl.BlockSpec(memory_space=pltpu.SMEM)
HBM = pl.BlockSpec(memory_space=pltpu.HBM)
ANY = pl.BlockSpec(memory_space=pl.ANY)


def vmem(mib):
    return pltpu.CompilerParams(vmem_limit_bytes=mib * 1024 * 1024)

NT = (((1,), (1,)), ((), ()))
TN = (((0,), (0,)), ((), ()))
SOURCE_Z = (0, -1, 1, -2, 2, -3, 3, 4)


def in_hbm(v):
    return pltpu.with_memory_space_constraint(v, pltpu.HBM)


def in_vmem(v):
    return pltpu.with_memory_space_constraint(v, pltpu.VMEM)


def load_all(pairs, sems):
    copies = [pltpu.make_async_copy(a, b, sems.at[i]) for i, (a, b) in enumerate(pairs)]
    for copy in copies:
        copy.start()
    return copies


def split3(v):
    a = v.astype(BF16)
    r = v - a.astype(F32)
    b = r.astype(BF16)
    c = (r - b.astype(F32)).astype(BF16)
    return jnp.concatenate([a, b, c], axis=0)


def fold3(v):
    n = v.shape[0] // 3
    return v[:n] + v[n : 2 * n] + v[2 * n :]


def first_kernel(x_ref, q_hbm, e_hbm, h_hbm, *refs):
    outs, (q_ref, e_ref, h_ref, sems) = refs[:4], refs[4:]
    columns = [pl.ds(pl.multiple_of((x_ref[0] + s) % 4 * 1024, 1024), 1024) for s in range(4)]
    loads = load_all(
        [(q_hbm, q_ref), (h_hbm, h_ref)]
        + [(e_hbm.at[:, columns[s]], e_ref.at[s]) for s in (1, 3, 2, 0)],
        sems,
    )
    loads[0].wait()
    q = q_ref[...].astype(BF16)
    loads[1].wait()
    t = jnp.dot(q, h_ref[...], preferred_element_type=F32)
    high = t.astype(BF16)
    low = (t - high.astype(F32)).astype(BF16)
    for load, s in zip(loads[2:], (1, 3, 2, 0)):
        load.wait()
        eq = jnp.dot(q, e_ref[s], preferred_element_type=F32)
        outs[s][0:32, :] = high
        outs[s][32:64, :] = low
        outs[s][64:96, :] = eq.astype(BF16)


def first(x_index, q_t, e_t, h_t):
    return pl.pallas_call(
        first_kernel,
        in_specs=[SMEM] + [HBM] * 3,
        out_specs=[VMEM] * 4,
        out_shape=[jax.ShapeDtypeStruct((96, 1024), BF16)] * 4,
        scratch_shapes=[
            pltpu.VMEM((32, 448), F32),
            pltpu.VMEM((4, 448, 1024), BF16),
            pltpu.VMEM((448, 1024), BF16),
            pltpu.SemaphoreType.DMA((6,)),
        ],
        compiler_params=vmem(12),
        name="eq_hq",
    )(x_index, in_hbm(q_t), in_hbm(e_t), in_hbm(h_t))


def products(t, x_ref, slabs):
    out = []
    for pair in range(0, slabs, 2):
        two = [x_ref[1024 * j : 1024 * (j + 1), :] for j in range(pair, min(pair + 2, slabs))]
        p = fold3(jnp.dot(t, jnp.concatenate(two, axis=1), preferred_element_type=F32))
        out += [p[:, 128 * s : 128 * (s + 1)] for s in range(len(two))]
    return out


def column_kernel(z_ref, *refs):
    messages, xs, (out_ref, t_ref, m_ref, x_ref, sems) = refs[:4], refs[4:11], refs[11:]
    loads = load_all(
        [(m, m_ref.at[i]) for i, m in enumerate(messages)]
        + [(v, x_ref.at[pl.ds(1024 * i, 1024), :]) for i, v in enumerate(xs)],
        sems,
    )
    for load in loads[:4]:
        load.wait()
    m = sum(m_ref[i].astype(F32) for i in range(4))
    t = split3(m[0:32] + m[32:64])
    t_ref[...] = t
    for z in range(8):
        out_ref[z] = m[64:96, 128 * z : 128 * (z + 1)]
    for load in loads[4:]:
        load.wait()
    for j, p in enumerate(products(t, x_ref, 7)):
        out_ref[z_ref[j]] += p


def column(z_index, messages, slabs):
    return pl.pallas_call(
        column_kernel,
        in_specs=[SMEM] + [ANY] * 11,
        out_specs=[VMEM] * 2,
        out_shape=[
            jax.ShapeDtypeStruct((8, 32, 128), F32),
            jax.ShapeDtypeStruct((96, 1024), BF16),
        ],
        scratch_shapes=[
            pltpu.VMEM((4, 96, 1024), BF16),
            pltpu.VMEM((7 * 1024, 128), BF16),
            pltpu.SemaphoreType.DMA((11,)),
        ],
        compiler_params=vmem(8),
        name="p_column",
    )(z_index, *messages, *slabs)


def column_rest_kernel(z_ref, part_ref, t_ref, *refs):
    slabs, (out_ref, x_ref, sems) = refs[:1], refs[1:]
    copies = [(v, x_ref.at[pl.ds(1024 * i, 1024), :]) for i, v in enumerate(slabs)]
    loads = load_all(copies, sems)
    out_ref[...] = part_ref[...]
    for load in loads:
        load.wait()
    for j, p in enumerate(products(t_ref[...], x_ref, 1)):
        out_ref[z_ref[7 + j]] += p


def column_rest(z_index, part, t, slabs):
    return pl.pallas_call(
        column_rest_kernel,
        in_specs=[SMEM] + [VMEM] * 2 + [ANY],
        out_specs=VMEM,
        out_shape=jax.ShapeDtypeStruct((8, 32, 128), F32),
        scratch_shapes=[pltpu.VMEM((1024, 128), BF16), pltpu.SemaphoreType.DMA((1,))],
        compiler_params=vmem(6),
        name="p_column_rest",
    )(z_index, part, t, *slabs)


def add_spread_kernel(scale, in_ref, out_ref):
    s = jnp.sum(in_ref[...], axis=0) * scale
    out_ref[...] = jnp.broadcast_to(s[None], out_ref.shape)


def add_spread(v, copies, scale):
    return pl.pallas_call(
        functools.partial(add_spread_kernel, scale),
        in_specs=[VMEM],
        out_specs=VMEM,
        out_shape=jax.ShapeDtypeStruct((copies, *v.shape[1:]), F32),
        compiler_params=vmem(4),
        name="add_spread",
    )(v)


def pack_kernel(*refs):
    parts, (out, sems) = refs[:-2], refs[-2:]
    copies = [(v, out.at[pl.ds(1024 * i, 1024), :]) for i, v in enumerate(parts)]
    for copy in load_all(copies, sems):
        copy.wait()


def pack(arrays):
    return pl.pallas_call(
        pack_kernel,
        in_specs=[ANY] * len(arrays),
        out_specs=HBM,
        out_shape=pltpu.HBM((1024 * len(arrays), 128), BF16),
        scratch_shapes=[pltpu.SemaphoreType.DMA((len(arrays),))],
        compiler_params=vmem(4),
        name="pack",
    )(*arrays)


def slab_copies(at_ref, first, e_hbm, x_hbm, e_ref, x_ref):
    slabs = [(r, i) for r in x_hbm for i in range(r.shape[0] // 1024)]
    pairs = []
    for place, (r, i) in enumerate(slabs):
        cols = pl.ds(pl.multiple_of(at_ref[first + place] * 128, 128), 128)
        pairs.append((r.at[pl.ds(1024 * i, 1024), :], x_ref.at[place]))
        pairs.append((e_hbm.at[:, cols], e_ref.at[place]))
    return pairs


def correct_pair(pair, loads, h_ref, e_ref, x_ref, out_ref):
    for load in loads[4 * pair : 4 * pair + 4]:
        load.wait()
    x = jnp.concatenate([x_ref[2 * pair], x_ref[2 * pair + 1]], axis=1)
    grad = jnp.dot(h_ref[...], x, preferred_element_type=F32)
    for s in range(2):
        place = 2 * pair + s
        both = e_ref[place].astype(F32) + grad[:, 128 * s : 128 * (s + 1)]
        out_ref[place] = both.astype(BF16)


def correct_kernel(at_ref, h_hbm, e_hbm, *refs):
    x_hbm, (out_ref, h_ref, e_ref, x_ref, sems) = refs[:-5], refs[-5:]
    copies = slab_copies(at_ref, 0, e_hbm, x_hbm, e_ref, x_ref)
    loads = load_all([(h_hbm, h_ref)] + copies, sems)
    loads[0].wait()
    for pair in range(at_ref.shape[0] // 2):
        correct_pair(pair, loads[1:], h_ref, e_ref, x_ref, out_ref)


def correct_scratch(n):
    return [
        pltpu.VMEM((448, 1024), BF16),
        pltpu.VMEM((n, 448, 128), BF16),
        pltpu.VMEM((n, 1024, 128), BF16),
        pltpu.SemaphoreType.DMA((1 + 2 * n,)),
    ]


def correct(places, h_t, e_t, arrays):
    n = places.shape[0]
    return pl.pallas_call(
        correct_kernel,
        in_specs=[SMEM] + [HBM] * (2 + len(arrays)),
        out_specs=VMEM,
        out_shape=pltpu.VMEM((n, 448, 128), BF16),
        scratch_shapes=correct_scratch(n),
        compiler_params=vmem(20),
        name="corrected",
    )(places, *[in_hbm(v) for v in [h_t, e_t, *arrays]])


def finish_kernel(kept_count, at_ref, p_ref, *refs):
    kept_refs, (h_hbm, e_hbm), refs = (
        refs[:kept_count],
        refs[kept_count : kept_count + 2],
        refs[kept_count + 2 :],
    )
    x_hbm, (w_ref, out_hbm, h_ref, e_ref, x_ref, sems, out_ref, out_sem) = refs[:-8], refs[-8:]
    rest = len(x_hbm)
    copies = slab_copies(at_ref, 32 - rest, e_hbm, x_hbm, e_ref, x_ref)
    loads = load_all([(h_hbm, h_ref)] + copies, sems)
    slabs = [(r, i) for r in [*kept_refs, out_ref] for i in range(r.shape[0])]

    def project_pair(pair):
        two = (2 * pair, 2 * pair + 1)
        p = jnp.concatenate([p_ref[at_ref[i]] for i in two], axis=1)
        c = jnp.concatenate([slabs[i][0][slabs[i][1]] for i in two], axis=1)
        return lax.dot_general(split3(p), c, NT, preferred_element_type=F32)

    total = sum(project_pair(pair) for pair in range(16 - rest // 2))
    loads[0].wait()
    for pair in range(rest // 2):
        correct_pair(pair, loads[1:], h_ref, e_ref, x_ref, out_ref)
    store = pltpu.make_async_copy(out_ref, out_hbm, out_sem)
    store.start()
    total = total + sum(project_pair(pair) for pair in range(16 - rest // 2, 16))
    w_ref[...] = fold3(total)
    store.wait()


def finish(places, p_blocks, kept, h_t, e_t, rest):
    n = len(rest)
    return pl.pallas_call(
        functools.partial(finish_kernel, len(kept)),
        in_specs=[SMEM] + [VMEM] * (1 + len(kept)) + [HBM] * (2 + n),
        out_specs=[VMEM, HBM],
        out_shape=[jax.ShapeDtypeStruct((32, 448), F32), pltpu.HBM((n, 448, 128), BF16)],
        scratch_shapes=correct_scratch(n)
        + [pltpu.VMEM((n, 448, 128), BF16), pltpu.SemaphoreType.DMA],
        compiler_params=vmem(14),
        name="c_p",
    )(places, p_blocks, *[in_vmem(v) for v in kept], *[in_hbm(v) for v in [h_t, e_t, *rest]])


def load_pieces(kept_refs, hbm, buffer, sem):
    load = pltpu.make_async_copy(hbm, buffer, sem)
    load.start()
    return [(r, i) for r in [*kept_refs, buffer] for i in range(r.shape[0])], load


def factor_kernel(p_ref, inv_ref, p_out_ref, low_ref):
    p = jnp.concatenate([p_ref[i] for i in range(32)], axis=1)
    gram = lax.dot_general(
        p, p, NT, precision=lax.Precision.HIGHEST, preferred_element_type=F32
    )
    row = lax.broadcasted_iota(jnp.int32, (32, 128), 0)
    col = lax.broadcasted_iota(jnp.int32, (32, 128), 1)
    work = jnp.concatenate([gram, jnp.zeros((32, 96), F32)], axis=1)
    work = jnp.where(col == row + 32, 1.0, work)
    scale = jnp.zeros((32, 1), F32)
    for j in range(32):
        pivot = work[j : j + 1, j : j + 1]
        below = jnp.where(row[:, :1] > j, work[:, j : j + 1], 0.0)
        scale = jnp.where(row[:, :1] == j, pivot, scale)
        work = work - below * (work[j : j + 1, :] / pivot)
    inverse = work[:, 32:64] / jnp.sqrt(scale)
    inv_ref[...] = inverse
    out = jnp.dot(inverse, p, precision=lax.Precision.HIGHEST, preferred_element_type=F32)
    p_out_ref[...] = out
    low_ref[...] = out.astype(BF16)


def factor(p_blocks):
    return pl.pallas_call(
        factor_kernel,
        in_specs=[VMEM],
        out_specs=[VMEM] * 3,
        out_shape=[
            jax.ShapeDtypeStruct((32, 32), F32),
            jax.ShapeDtypeStruct((32, 4096), F32),
            jax.ShapeDtypeStruct((32, 4096), BF16),
        ],
        compiler_params=vmem(8),
        name="factor",
    )(p_blocks)


def final_kernel(at_ref, inv_ref, a_ref, b_ref, c_ref, d_ref, low_ref, *refs):
    kept_refs, (c_hbm, q_ref, out_hbm, buffer, stage, sem, out_sems) = refs[:-7], refs[-7:]
    slabs, load = load_pieces(kept_refs, c_hbm, buffer, sem)
    w = (a_ref[...] + b_ref[...] + c_ref[...] + d_ref[...]) * 0.25
    q = jnp.dot(inv_ref[...], w, precision=lax.Precision.HIGHEST, preferred_element_type=F32)
    q_ref[...] = q
    rows = q.T.astype(BF16)
    stores = []
    for pair in range(16):
        if 2 * pair == 32 - buffer.shape[0]:
            load.wait()
        places = [pl.ds(pl.multiple_of(at_ref[2 * pair + s] * 128, 128), 128) for s in range(2)]
        p = jnp.concatenate([low_ref[:, place] for place in places], axis=1)
        approx = jnp.dot(rows, p, preferred_element_type=F32)
        for s, place in enumerate(places):
            i = 2 * pair + s
            kept = slabs[i][0][slabs[i][1]].astype(F32)
            stage[i] = (kept - approx[:, 128 * s : 128 * (s + 1)]).astype(BF16)
            store = pltpu.make_async_copy(stage.at[i], out_hbm.at[:, place], out_sems.at[i])
            store.start()
            stores.append(store)
    for store in stores:
        store.wait()


def final(places, inverse, parts, p_low, kept, piece):
    return pl.pallas_call(
        final_kernel,
        in_specs=[SMEM] + [VMEM] * (6 + len(kept)) + [HBM],
        out_specs=[VMEM, HBM],
        out_shape=[
            jax.ShapeDtypeStruct((32, 448), F32),
            jax.ShapeDtypeStruct((448, 4096), BF16),
        ],
        scratch_shapes=[
            pltpu.VMEM(piece.shape, BF16),
            pltpu.VMEM((32, 448, 128), BF16),
            pltpu.SemaphoreType.DMA,
            pltpu.SemaphoreType.DMA((32,)),
        ],
        compiler_params=vmem(14),
        name="new_error",
    )(places, inverse, *parts, p_low, *[in_vmem(v) for v in kept], in_hbm(piece))


def swap(v, axis="hidden", groups=None):
    return lax.all_to_all(v, axis, 0, 0, axis_index_groups=groups)


def replicas(v):
    return [v] + [
        lax.ppermute(v, "replica", [(i, (i + s) % 4) for i in range(4)]) for s in (1, 3, 2)
    ]


def move(v, dx, dz):
    pairs = [(h, (h // 8 + dx) % 4 * 8 + (h % 8 + dz) % 8) for h in range(32)]
    return lax.ppermute(v, "hidden", pairs)


def together(*values):
    return lax.optimization_barrier(values)


def shards(activations, hidden_grad, error_buffer, q_previous):
    x = activations[0]
    me = lax.axis_index("hidden")
    x_index, z_index = me // 8, me % 8
    z_order = jnp.stack([(z_index + rz) % 8 for rz in SOURCE_Z]).astype(jnp.int32)

    def places(rx):
        return (x_index + rx) % 4 * 8 + z_order

    e_t, h_t = error_buffer[0, 0].T, hidden_grad[0].T
    mine, *others = first(x_index.astype(jnp.int32)[None], q_previous[0].T, e_t, h_t)
    p1, m1, f0 = move(x, 0, 1), move(x, 0, -1), move(x, 2, 0)
    g1, g2, g3 = [move(m, dx, 0) for m, dx in zip(others, (1, 2, -1))]
    p1, m1, mine = together(p1, m1, mine)
    p2, m2 = move(p1, 0, 1), move(m1, 0, -1)
    p2, m2, f0 = together(p2, m2, f0)
    p3, m3 = move(p2, 0, 1), move(m2, 0, -1)
    fp1, fm1 = move(f0, 0, 1), move(f0, 0, -1)
    bundle = pack([x, p1, m1, p2, m2, p3, m3])
    p3, fp1, fm1 = together(p3, fp1, fm1)
    end = move(p3, 0, 1)
    bundle, g1, g2, g3 = together(bundle, g1, g2, g3)
    near = [move(bundle, 1, 0), move(bundle, -1, 0)]
    near_end = [move(end, 1, 0), move(end, -1, 0)]
    part, t = column(z_order, [mine, g1, g2, g3], [x, p1, m1, p2, m2, p3, m3])
    column_groups = [[8 * i + z for z in range(8)] for i in range(4)]
    p_parts = swap(column_rest(z_order, part, t, [end]), groups=column_groups)
    kept_own = correct(places(0), h_t, e_t, [bundle, end])
    fp2, fm2 = move(fp1, 0, 1), move(fm1, 0, -1)
    fp2, fm2, kept_own = together(fp2, fm2, kept_own)
    fp3, fm3, f_end = move(fp2, 0, 1), move(fm2, 0, -1), move(fm2, 0, -2)
    p_parts, kept_own = together(add_spread(p_parts, 4, 1.0), kept_own)
    p_parts = add_spread(swap(p_parts, "replica"), 32, 0.25)
    p_parts, fp3, fm3, f_end = together(p_parts, fp3, fm3, f_end)
    far = [f0, fp1, fm1, fp2, fm2, fp3, fm3, f_end]
    p_blocks = swap(p_parts)
    at_near = jnp.concatenate([places(-1)[:7], places(1)[:7]])
    at_rest = jnp.concatenate([places(-1)[7:], places(1)[7:], places(2)])
    at = jnp.concatenate([places(0), at_near, at_rest])
    kept = [kept_own, correct(at_near, h_t, e_t, near)]
    w_part, piece = finish(at, p_blocks, kept, h_t, e_t, [*near_end, *far])
    parts = replicas(w_part)
    inverse, p_factor, p_low = factor(p_blocks)
    q_factor, new_error = final(at, inverse, parts, p_low, kept, piece)
    return (p_factor.T[None], q_factor.T[None], new_error.T[None, None])


def solution(mesh):
    in_specs = (
        P("expert", "replica", "hidden"),
        P("expert", "replica", "hidden"),
        P("expert", "replica", None, "hidden"),
        P("expert", "hidden", None),
    )
    out_specs = (
        P("expert", None, None),
        P("expert", "hidden", None),
        P("expert", "replica", None, "hidden"),
    )
    return jax.shard_map(shards, mesh=mesh, in_specs=in_specs, out_specs=out_specs, check_vma=False)
```

time: 128 us -> 120 us (0.938)
  local copies, waits for them, and re-layouts: 20 us -> 2.69 us
  Pallas kernels: 25.6 us -> 37.4 us
  waiting for transfers between devices: 22.8 us -> 12.9 us
  starting transfers between devices: 47.8 us -> 55.3 us
    unnamed x44 -> x16, local copies, waits for them, and re-layouts: 19.8 us -> 0.03 us
    pallas_call x8, Pallas kernels: 20.1 us -> 31.1 us  [the longest x2 10.9 us: correct(): pl.pallas_call(correct_kernel, in_specs=[SMEM] + [HBM] * (2 + len(arrays)...]
    ppermute x22, waiting for transfers between devices: 17.1 us -> 11.9 us  [move(): return lax.ppermute(v, 'hidden', pairs)]
    all_to_all x2, waiting for transfers between devices: 5.65 us -> 1.04 us  [swap(): return lax.all_to_all(v, axis, 0, 0, axis_index_groups=groups)]
    ppermute x22, starting transfers between devices: 30.2 us -> 33.8 us  [move(): return lax.ppermute(v, 'hidden', pairs)]
    ppermute x3, starting transfers between devices: 3.3 us -> 5.29 us  [replicas(): lax.ppermute(v, 'replica', [(i, (i + s) % 4) for i in range(4)])]
    all_to_all x2, starting transfers between devices: 14.2 us -> 16.2 us  [swap(): return lax.all_to_all(v, axis, 0, 0, axis_index_groups=groups)]
    concatenate x0 -> x1, local copies, waits for them, and re-layouts: none -> 1.35 us  [shards(): at = jnp.concatenate([places(0), at_near, at_rest])]
  transfers between devices with their start and end apart: 27 -> 27, of which waited for: 8 -> 8; matrix products, arithmetic and copies ran while one was open for 0% -> 2% of each run, Pallas kernels for 15% -> 21%
where the time goes in v3:
time: 120 us; the launch traced here: 119 us
  starting transfers between devices  55.3 us (46%)
  Pallas kernels  37.4 us (31%)
  waiting for transfers between devices  12.9 us (11%)
  blocking collectives  9.89 us (8%)
  local copies, waits for them, and re-layouts  2.69 us (2%)
    ppermute x22, starting transfers between devices, move(): return lax.ppermute(v, 'hidden', pairs)  33.8 us
    all_to_all x2, starting transfers between devices, swap(): return lax.all_to_all(v, axis, 0, 0, axis_index_groups=groups)  16.2 us
    ppermute x22, waiting for transfers between devices, move(): return lax.ppermute(v, 'hidden', pairs)  11.9 us
    pallas_call x2, Pallas kernels, correct(): pl.pallas_call(correct_kernel, in_specs=[SMEM] + [HBM] * (2 + len(arrays)...  10.9 us
    all_to_all x1, blocking collectives, swap(): return lax.all_to_all(v, axis, 0, 0, axis_index_groups=groups)  9.89 us
    pallas_call x1, Pallas kernels, finish(): pl.pallas_call(functools.partial(finish_kernel, len(kept)), in_specs=[SME...  6.91 us
    pallas_call x1, Pallas kernels, factor(): pl.pallas_call(factor_kernel, in_specs=[VMEM], out_specs=[VMEM] * 3, out_...  5.45 us
    pallas_call x1, Pallas kernels, final(): pl.pallas_call(final_kernel, in_specs=[SMEM] + [VMEM] * (6 + len(kept)) +...  5.42 us
  transfers between devices with their start and end apart: 27, of which 8 were waited for; matrix products, arithmetic and copies ran while one was open for 2% of the time, Pallas kernels for 21%

profile of v3, /device:TPU:32, one launch (start us, length us, event | category | flops | bytes accessed | tf_op | source)
XLA Modules:
  0.0 119.3 jit_solution(16585393858003407838)
XLA Ops:
  0.6 2.0 %collective-permute-start = (bf16[1024,128]{1,0:T(8,128)(2,1)}, bf16[1024,128]{1,0:T(8,128)(2,1)S(1)}, u32[]{:S(2)}, u32[]{:S(2)}) collective-permute-start(bf16[1024,128]{1,0:T(8,128)(2,1)} %bitcast.30), channel_id=1, source_target_pairs={{0,4},{4,8},{8,12},{12,16},{16,20},{20,24},{24,28},{28,0},{32,36},... | collective-permute-start | bytes 786440 | tf_op jit(solution)/shard_map/ppermute | solution.py:394
  2.6 0.1 collective-permute-start.1
  2.7 3.0 %collective-permute-start.4 = (bf16[1024,128]{1,0:T(8,128)(2,1)}, bf16[1024,128]{1,0:T(8,128)(2,1)S(1)}, u32[]{:S(2)}, u32[]{:S(2)}) collective-permute-start(bf16[1024,128]{1,0:T(8,128)(2,1)} %bitcast.32), channel_id=1, source_target_pairs={{0,64},{4,68},{8,72},{12,76},{16,80},{20,84},{24,88},{28,92},{32,9... | collective-permute-start | bytes 786440 | tf_op jit(solution)/shard_map/ppermute | solution.py:394
  5.8 2.7 %eq_hq.1 = (bf16[96,1024]{1,0:T(8,128)(2,1)S(1)}, bf16[96,1024]{1,0:T(8,128)(2,1)S(1)}, bf16[96,1024]{1,0:T(8,128)(2,1)S(1)}, bf16[96,1024]{1,0:T(8,128)(2,1)S(1)}) custom-call(s32[1]{0:T(128)} %bitcast.9.x_ref, f32[32,448]{1,0:T(8,128)} %bitcast.43, bf16[448,4096]{1,0:T(8,128)(2,1)} %bitcast.35, bf16[448,1024]{1,0:T(8,128)(2,1)} %bitcast.39), custom_call_target="tpu_custom_call" | custom-call | tf_op jit(solution)/shard_map/eq_hq/pallas_call | solution.py:77
  8.5 0.5 collective-permute-done.refs_1_.refs_5_
  9.0 1.8 %collective-permute-done.1.refs_2_.refs_6_ = bf16[1024,128]{1,0:T(8,128)(2,1)S(1)} collective-permute-done((bf16[1024,128]{1,0:T(8,128)(2,1)}, bf16[1024,128]{1,0:T(8,128)(2,1)S(1)}, u32[]{:S(2)}, u32[]{:S(2)}) %collective-permute-start.1) | collective-permute-done | bytes 262176 | tf_op jit(solution)/shard_map/ppermute | solution.py:394
  10.8 3.1 %collective-permute-start.2 = (bf16[1024,128]{1,0:T(8,128)(2,1)S(1)}, bf16[1024,128]{1,0:T(8,128)(2,1)S(1)}, u32[]{:S(2)}, u32[]{:S(2)}) collective-permute-start(bf16[1024,128]{1,0:T(8,128)(2,1)S(1)} %collective-permute-done.refs_1_.refs_5_), channel_id=1, source_target_pairs={{0,4},{4,8},{8,12},{12,16},{16,20},{20,24},{24,28},{28,0},{32,36},... | collective-permute-start | bytes 786440 | tf_op jit(solution)/shard_map/ppermute | solution.py:394
  13.9 5.0 %collective-permute-done.2.refs_3_.refs_7_ = bf16[1024,128]{1,0:T(8,128)(2,1)S(1)} collective-permute-done((bf16[1024,128]{1,0:T(8,128)(2,1)S(1)}, bf16[1024,128]{1,0:T(8,128)(2,1)S(1)}, u32[]{:S(2)}, u32[]{:S(2)}) %collective-permute-start.2) | collective-permute-done | bytes 262176 | tf_op jit(solution)/shard_map/ppermute | solution.py:394
  18.9 2.8 %collective-permute-done.3.refs_4_.refs_8_ = bf16[1024,128]{1,0:T(8,128)(2,1)S(1)} collective-permute-done((bf16[1024,128]{1,0:T(8,128)(2,1)S(1)}, bf16[1024,128]{1,0:T(8,128)(2,1)S(1)}, u32[]{:S(2)}, u32[]{:S(2)}) %collective-permute-start.3) | collective-permute-done | bytes 262176 | tf_op jit(solution)/shard_map/ppermute | solution.py:394
  21.7 1.7 %collective-permute-start.5 = (bf16[1024,128]{1,0:T(8,128)(2,1)S(1)}, bf16[1024,128]{1,0:T(8,128)(2,1)S(1)}, u32[]{:S(2)}, u32[]{:S(2)}) collective-permute-start(bf16[1024,128]{1,0:T(8,128)(2,1)S(1)} %collective-permute-done.2.refs_3_.refs_7_), channel_id=1, source_target_pairs={{0,4},{4,8},{8,12},{12,16},{16,20},{20,24},{24,28},{28,0},{32,36},... | collective-permute-start | bytes 786440 | tf_op jit(solution)/shard_map/ppermute | solution.py:394
  23.4 0.3 collective-permute-start.6
  23.7 1.5 %collective-permute-start.7 = (bf16[96,1024]{1,0:T(8,128)(2,1)S(1)}, bf16[96,1024]{1,0:T(8,128)(2,1)S(1)}, u32[]{:S(2)}, u32[]{:S(2)}) collective-permute-start(bf16[96,1024]{1,0:T(8,128)(2,1)S(1)} %get-tuple-element.44), channel_id=1, source_target_pairs={{0,32},{4,36},{8,40},{12,44},{16,48},{20,52},{24,56},{28,60},{32,6... | collective-permute-start | bytes 589832 | tf_op jit(solution)/shard_map/ppermute | solution.py:394
  25.2 2.7 %collective-permute-start.8 = (bf16[96,1024]{1,0:T(8,128)(2,1)S(1)}, bf16[96,1024]{1,0:T(8,128)(2,1)S(1)}, u32[]{:S(2)}, u32[]{:S(2)}) collective-permute-start(bf16[96,1024]{1,0:T(8,128)(2,1)S(1)} %get-tuple-element.45), channel_id=1, source_target_pairs={{0,64},{4,68},{8,72},{12,76},{16,80},{20,84},{24,88},{28,92},{32,9... | collective-permute-start | bytes 589832 | tf_op jit(solution)/shard_map/ppermute | solution.py:394
  27.9 1.4 %collective-permute-start.9 = (bf16[96,1024]{1,0:T(8,128)(2,1)S(1)}, bf16[96,1024]{1,0:T(8,128)(2,1)S(1)}, u32[]{:S(2)}, u32[]{:S(2)}) collective-permute-start(bf16[96,1024]{1,0:T(8,128)(2,1)S(1)} %get-tuple-element.46), channel_id=1, source_target_pairs={{0,96},{4,100},{8,104},{12,108},{16,112},{20,116},{24,120},{28,124... | collective-permute-start | bytes 589832 | tf_op jit(solution)/shard_map/ppermute | solution.py:394
  29.4 1.7 %collective-permute-start.10 = (bf16[1024,128]{1,0:T(8,128)(2,1)S(1)}, bf16[1024,128]{1,0:T(8,128)(2,1)}, u32[]{:S(2)}, u32[]{:S(2)}) collective-permute-start(bf16[1024,128]{1,0:T(8,128)(2,1)S(1)} %collective-permute-done.4.refs_6_), channel_id=1, source_target_pairs={{0,4},{4,8},{8,12},{12,16},{16,20},{20,24},{24,28},{28,0},{32,36},... | collective-permute-start | bytes 786440 | tf_op jit(solution)/shard_map/ppermute | solution.py:394
  31.1 0.3 collective-permute-start.11
  31.4 1.3 %pack.1.refs_0_ = bf16[7168,128]{1,0:T(8,128)(2,1)} custom-call(bf16[1024,128]{1,0:T(8,128)(2,1)S(1)} %bitcast.33, bf16[1024,128]{1,0:T(8,128)(2,1)S(1)} %collective-permute-done.refs_1_.refs_5_, bf16[1024,128]{1,0:T(8,128)(2,1)S(1)} %collective-permute-done.1.refs_2_.refs_6_, bf16[1024,128]{1,0:T(8,128)(2,1)S(1)} %collective-permute-done.2.refs_3_.refs_7_, ...), custom_call_target="tpu_custom_call" | custom-call | tf_op jit(solution)/shard_map/pack/pallas_call | solution.py:188
  32.7 1.4 %collective-permute-done.8.refs_2_ = bf16[96,1024]{1,0:T(8,128)(2,1)S(1)} collective-permute-done((bf16[96,1024]{1,0:T(8,128)(2,1)S(1)}, bf16[96,1024]{1,0:T(8,128)(2,1)S(1)}, u32[]{:S(2)}, u32[]{:S(2)}) %collective-permute-start.8) | collective-permute-done | bytes 196640 | tf_op jit(solution)/shard_map/ppermute | solution.py:394
  34.1 1.8 %collective-permute-start.18 = (bf16[7168,128]{1,0:T(8,128)(2,1)}, bf16[7168,128]{1,0:T(8,128)(2,1)}, u32[]{:S(2)}, u32[]{:S(2)}) collective-permute-start(bf16[7168,128]{1,0:T(8,128)(2,1)} %pack.1.refs_0_), channel_id=1, source_target_pairs={{0,32},{4,36},{8,40},{12,44},{16,48},{20,52},{24,56},{28,60},{32,6... | collective-permute-start | bytes 5505032 | tf_op jit(solution)/shard_map/ppermute | solution.py:394
  35.9 1.5 %collective-permute-start.19 = (bf16[7168,128]{1,0:T(8,128)(2,1)}, bf16[7168,128]{1,0:T(8,128)(2,1)}, u32[]{:S(2)}, u32[]{:S(2)}) collective-permute-start(bf16[7168,128]{1,0:T(8,128)(2,1)} %pack.1.refs_0_), channel_id=1, source_target_pairs={{0,96},{4,100},{8,104},{12,108},{16,112},{20,116},{24,120},{28,124... | collective-permute-start | bytes 5505032 | tf_op jit(solution)/shard_map/ppermute | solution.py:394
  37.3 0.3 collective-permute-done.11.refs_8_
  37.6 1.8 %collective-permute-start.12 = (bf16[1024,128]{1,0:T(8,128)(2,1)S(1)}, bf16[1024,128]{1,0:T(8,128)(2,1)S(1)}, u32[]{:S(2)}, u32[]{:S(2)}) collective-permute-start(bf16[1024,128]{1,0:T(8,128)(2,1)S(1)} %collective-permute-done.5.refs_5_.refs_9_), channel_id=1, source_target_pairs={{0,4},{4,8},{8,12},{12,16},{16,20},{20,24},{24,28},{28,0},{32,36},... | collective-permute-start | bytes 786440 | tf_op jit(solution)/shard_map/ppermute | solution.py:394
  39.4 2.7 %collective-permute-start.13 = (bf16[1024,128]{1,0:T(8,128)(2,1)}, bf16[1024,128]{1,0:T(8,128)(2,1)S(1)}, u32[]{:S(2)}, u32[]{:S(2)}) collective-permute-start(bf16[1024,128]{1,0:T(8,128)(2,1)} %collective-permute-done.10.refs_7_), channel_id=1, source_target_pairs={{0,4},{4,8},{8,12},{12,16},{16,20},{20,24},{24,28},{28,0},{32,36},... | collective-permute-start | bytes 786440 | tf_op jit(solution)/shard_map/ppermute | solution.py:394
  42.1 0.1 stack.35.z_ref
  42.2 2.4 %p_column.1 = (f32[8,32,128]{2,1,0:T(8,128)S(1)}, bf16[96,1024]{1,0:T(8,128)(2,1)S(1)}) custom-call(s32[8]{0:T(128)S(1)} %stack.35.z_ref, bf16[96,1024]{1,0:T(8,128)(2,1)S(1)} %get-tuple-element.39.refs_0_, bf16[96,1024]{1,0:T(8,128)(2,1)S(1)} %collective-permute-done.7.refs_1_, bf16[96,1024]{1,0:T(8,128)(2,1)S(1)} %collective-permute-done.8.refs_2_, ...), custom_call_target="tpu_custom_call" | custom-call | tf_op jit(solution)/shard_map/p_column/pallas_call | solution.py:123
  44.6 0.1 collective-permute-done.12.refs_0_.refs_1_
  44.7 1.4 %p_column_rest.1 = f32[8,32,128]{2,1,0:T(8,128)} custom-call(s32[8]{0:T(128)S(1)} %stack.35.z_ref, f32[8,32,128]{2,1,0:T(8,128)S(1)} %get-tuple-element.52.part_ref, bf16[96,1024]{1,0:T(8,128)(2,1)S(1)} %get-tuple-element.53.t_ref, bf16[1024,128]{1,0:T(8,128)(2,1)S(1)} %collective-permute-done.12.refs_0_.refs_1_), custom_call_target="tpu_custom_call" | custom-call | tf_op jit(solution)/shard_map/p_column_rest/pallas_call | solution.py:153
  46.1 7.6 %all-to-all-start = ((f32[8,32,128]{2,1,0:T(8,128)}), f32[8,32,128]{2,1,0:T(8,128)S(1)}, u32[]{:S(2)}, u32[]{:S(2)}) async-start(f32[8,32,128]{2,1,0:T(8,128)} %p_column_rest.1), calls=%async_computation | async-start | bytes 262144 | tf_op jit(solution)/shard_map/all_to_all | solution.py:383
  53.7 4.6 %corrected.2.refs_0_ = bf16[8,448,128]{2,1,0:T(8,128)(2,1)S(1)} custom-call(s32[8]{0:T(128)S(1)} %get-tuple-element.76.at_ref, bf16[448,1024]{1,0:T(8,128)(2,1)} %bitcast.40, bf16[448,4096]{1,0:T(8,128)(2,1)} %bitcast.36, bf16[7168,128]{1,0:T(8,128)(2,1)} %pack.1.refs_0_, bf16[1024,128]{1,0:T(8,128)(2,1)} %copy-done.1), custom_call_target="tpu_custom_call" | custom-call | tf_op jit(solution)/shard_map/corrected/pallas_call | solution.py:240
  58.4 1.5 %collective-permute-start.15 = (bf16[1024,128]{1,0:T(8,128)(2,1)S(1)}, bf16[1024,128]{1,0:T(8,128)(2,1)S(1)}, u32[]{:S(2)}, u32[]{:S(2)}) collective-permute-start(bf16[1024,128]{1,0:T(8,128)(2,1)S(1)} %collective-permute-done.13.refs_9_), channel_id=1, source_target_pairs={{0,4},{4,8},{8,12},{12,16},{16,20},{20,24},{24,28},{28,0},{32,36},... | collective-permute-start | bytes 786440 | tf_op jit(solution)/shard_map/ppermute | solution.py:394
  59.9 0.6 collective-permute-start.16
  60.5 2.7 %collective-permute-start.17 = (bf16[1024,128]{1,0:T(8,128)(2,1)}, bf16[1024,128]{1,0:T(8,128)(2,1)S(1)}, u32[]{:S(2)}, u32[]{:S(2)}) collective-permute-start(bf16[1024,128]{1,0:T(8,128)(2,1)} %collective-permute-done.14.refs_10_), channel_id=1, source_target_pairs={{0,24},{4,28},{8,0},{12,4},{16,8},{20,12},{24,16},{28,20},{32,56},... | collective-permute-start | bytes 786440 | tf_op jit(solution)/shard_map/ppermute | solution.py:394
  63.2 9.9 %all_to_all.15.in_ref = f32[4,32,128]{2,1,0:T(8,128)S(1)} all-to-all(f32[4,32,128]{2,1,0:T(8,128)S(1)} %add_spread.2), channel_id=1, replica_groups=mesh['expert'=2,'hidden'=32,'replica'=4] {'replica'}, dimensions={0} | all-to-all | bytes 131072 | tf_op jit(solution)/shard_map/all_to_all | solution.py:383
  73.0 0.9 add_spread.3
  74.0 8.6 %all-to-all-start.2 = ((f32[32,32,128]{2,1,0:T(8,128)}), f32[32,32,128]{2,1,0:T(8,128)S(1)}, u32[]{:S(2)}, u32[]{:S(2)}) async-start(f32[32,32,128]{2,1,0:T(8,128)} %add_spread.3), calls=%async_computation.2 | async-start | bytes 1048576 | tf_op jit(solution)/shard_map/all_to_all | solution.py:383
  82.6 1.5 %collective-permute-start.20 = (bf16[1024,128]{1,0:T(8,128)(2,1)S(1)}, bf16[1024,128]{1,0:T(8,128)(2,1)}, u32[]{:S(2)}, u32[]{:S(2)}) collective-permute-start(bf16[1024,128]{1,0:T(8,128)(2,1)S(1)} %copy-done.2), channel_id=1, source_target_pairs={{0,32},{4,36},{8,40},{12,44},{16,48},{20,52},{24,56},{28,60},{32,6... | collective-permute-start | bytes 786440 | tf_op jit(solution)/shard_map/ppermute | solution.py:394
  84.2 1.8 %collective-permute-start.21 = (bf16[1024,128]{1,0:T(8,128)(2,1)S(1)}, bf16[1024,128]{1,0:T(8,128)(2,1)}, u32[]{:S(2)}, u32[]{:S(2)}) collective-permute-start(bf16[1024,128]{1,0:T(8,128)(2,1)S(1)} %copy-done.2), channel_id=1, source_target_pairs={{0,96},{4,100},{8,104},{12,108},{16,112},{20,116},{24,120},{28,124... | collective-permute-start | bytes 786440 | tf_op jit(solution)/shard_map/ppermute | solution.py:394
  85.9 0.6 slice.14
  86.5 0.6 slice.15
  87.2 1.3 %concatenate.7.at_ref = s32[32]{0:T(128)S(1)} concatenate(s32[8]{0:T(128)S(1)} %get-tuple-element.76.at_ref, s32[7]{0:T(128)S(1)} %bitcast.46, s32[7]{0:T(128)S(1)} %bitcast.44, s32[1]{0:T(128)} %slice.14, s32[1]{0:T(128)} %slice.15, s32[8]{0:T(128)S(1)} %get-tuple-element.73), dimensions={0} | concatenate | bytes 256 | tf_op jit(solution)/shard_map/concatenate | solution.py:439
  88.6 6.4 %corrected.3.refs_1_ = bf16[14,448,128]{2,1,0:T(8,128)(2,1)S(1)} custom-call(s32[14]{0:T(128)S(1)} %pad_add_fusion.at_ref, bf16[448,1024]{1,0:T(8,128)(2,1)} %bitcast.41, bf16[448,4096]{1,0:T(8,128)(2,1)} %bitcast.37, bf16[7168,128]{1,0:T(8,128)(2,1)} %collective-permute-done.18.refs_0_, bf16[7168,128]{1,0:T(8,128)(2,1)} %collective-permute-done.19.refs_1_), custom_call_target="tpu_custom_call" | custom-call | tf_op jit(solution)/shard_map/corrected/pallas_call | solution.py:240
  95.0 1.0 all-to-all-done.2.p_ref
  96.0 6.9 %c_p.1 = (f32[32,448]{1,0:T(8,128)S(1)}, bf16[10,448,128]{2,1,0:T(8,128)(2,1)}) custom-call(s32[32]{0:T(128)S(1)} %concatenate.7.at_ref, f32[32,32,128]{2,1,0:T(8,128)S(1)} %all-to-all-done.2.p_ref, bf16[8,448,128]{2,1,0:T(8,128)(2,1)S(1)} %corrected.2.refs_0_, bf16[14,448,128]{2,1,0:T(8,128)(2,1)S(1)} %corrected.3.refs_1_, bf16[448,1024]{1,0:T(8,128)(2,1)} %bitcast.42, ...), custom_call_target="tpu_custom_call" | custom-call | tf_op jit(solution)/shard_map/c_p/pallas_call | solution.py:282
  102.9 1.7 %collective-permute-start.22 = (f32[32,448]{1,0:T(8,128)S(1)}, f32[32,448]{1,0:T(8,128)S(1)}, u32[]{:S(2)}, u32[]{:S(2)}) collective-permute-start(f32[32,448]{1,0:T(8,128)S(1)} %get-tuple-element.68.a_ref), channel_id=1, source_target_pairs={{0,1},{1,2},{2,3},{3,0},{4,5},{5,6},{6,7},{7,4},{8,9},{9,10},{10,1... | collective-permute-start | bytes 172040 | tf_op jit(solution)/shard_map/ppermute | solution.py:388
  104.6 1.7 %collective-permute-start.23 = (f32[32,448]{1,0:T(8,128)S(1)}, f32[32,448]{1,0:T(8,128)S(1)}, u32[]{:S(2)}, u32[]{:S(2)}) collective-permute-start(f32[32,448]{1,0:T(8,128)S(1)} %get-tuple-element.68.a_ref), channel_id=1, source_target_pairs={{0,3},{1,0},{2,1},{3,2},{4,7},{5,4},{6,5},{7,6},{8,11},{9,8},{10,9... | collective-permute-start | bytes 172040 | tf_op jit(solution)/shard_map/ppermute | solution.py:388
  106.3 2.0 %collective-permute-start.24 = (f32[32,448]{1,0:T(8,128)S(1)}, f32[32,448]{1,0:T(8,128)S(1)}, u32[]{:S(2)}, u32[]{:S(2)}) collective-permute-start(f32[32,448]{1,0:T(8,128)S(1)} %get-tuple-element.68.a_ref), channel_id=1, source_target_pairs={{0,2},{1,3},{2,0},{3,1},{4,6},{5,7},{6,4},{7,5},{8,10},{9,11},{10,... | collective-permute-start | bytes 172040 | tf_op jit(solution)/shard_map/ppermute | solution.py:388
  108.2 5.4 %factor.1 = (f32[32,32]{1,0:T(8,128)S(1)}, f32[32,4096]{1,0:T(8,128)}, bf16[32,4096]{1,0:T(8,128)(2,1)S(1)}) custom-call(f32[32,32,128]{2,1,0:T(8,128)S(1)} %all-to-all-done.2.p_ref), custom_call_target="tpu_custom_call" | custom-call | tf_op jit(solution)/shard_map/factor/pallas_call | solution.py:323
  113.7 5.4 %new_error.1 = (f32[32,448]{1,0:T(8,128)}, bf16[448,4096]{1,0:T(8,128)(2,1)}) custom-call(s32[32]{0:T(128)S(1)} %concatenate.7.at_ref, f32[32,32]{1,0:T(8,128)S(1)} %get-tuple-element.63.inv_ref, f32[32,448]{1,0:T(8,128)S(1)} %get-tuple-element.68.a_ref, f32[32,448]{1,0:T(8,128)S(1)} %collective-permute-done.22.b_ref, ...), custom_call_target="tpu_custom_call" | custom-call | tf_op jit(solution)/shard_map/new_error/pallas_call | solution.py:363
  (40 shorter events, 0.2 us)
Async XLA Ops:
  0.6 8.3 %collective-permute-start = (bf16[1024,128]{1,0:T(8,128)(2,1)}, bf16[1024,128]{1,0:T(8,128)(2,1)S(1)}, u32[]{:S(2)}, u32[]{:S(2)}) collective-permute-start(bf16[1024,128]{1,0:T(8,128)(2,1)} %bitcast.30), channel_id=1, source_target_pairs={{0,4},{4,8},{8,12},{12,16},{16,20},{20,24},{24,28},{28,0},{32,36},... | collective-permute-start | bytes 786440 | tf_op jit(solution)/shard_map/ppermute | solution.py:394
  2.6 8.2 %collective-permute-start.1 = (bf16[1024,128]{1,0:T(8,128)(2,1)}, bf16[1024,128]{1,0:T(8,128)(2,1)S(1)}, u32[]{:S(2)}, u32[]{:S(2)}) collective-permute-start(bf16[1024,128]{1,0:T(8,128)(2,1)} %bitcast.31), channel_id=1, source_target_pairs={{0,28},{4,0},{8,4},{12,8},{16,12},{20,16},{24,20},{28,24},{32,60},... | collective-permute-start | bytes 786440 | tf_op jit(solution)/shard_map/ppermute | solution.py:394
  2.7 11.2 %collective-permute-start.4 = (bf16[1024,128]{1,0:T(8,128)(2,1)}, bf16[1024,128]{1,0:T(8,128)(2,1)S(1)}, u32[]{:S(2)}, u32[]{:S(2)}) collective-permute-start(bf16[1024,128]{1,0:T(8,128)(2,1)} %bitcast.32), channel_id=1, source_target_pairs={{0,64},{4,68},{8,72},{12,76},{16,80},{20,84},{24,88},{28,92},{32,9... | collective-permute-start | bytes 786440 | tf_op jit(solution)/shard_map/ppermute | solution.py:394
  5.8 25.7 %copy-start = (bf16[1,1024,128]{2,1,0:T(8,128)(2,1)S(1)}, bf16[1,1024,128]{2,1,0:T(8,128)(2,1)}, u32[]{:S(2)}) copy-start(bf16[1,1024,128]{2,1,0:T(8,128)(2,1)} %param.4) | copy-start | bytes 786436
  10.8 8.1 %collective-permute-start.2 = (bf16[1024,128]{1,0:T(8,128)(2,1)S(1)}, bf16[1024,128]{1,0:T(8,128)(2,1)S(1)}, u32[]{:S(2)}, u32[]{:S(2)}) collective-permute-start(bf16[1024,128]{1,0:T(8,128)(2,1)S(1)} %collective-permute-done.refs_1_.refs_5_), channel_id=1, source_target_pairs={{0,4},{4,8},{8,12},{12,16},{16,20},{20,24},{24,28},{28,0},{32,36},... | collective-permute-start | bytes 786440 | tf_op jit(solution)/shard_map/ppermute | solution.py:394
  13.9 7.8 %collective-permute-start.3 = (bf16[1024,128]{1,0:T(8,128)(2,1)S(1)}, bf16[1024,128]{1,0:T(8,128)(2,1)S(1)}, u32[]{:S(2)}, u32[]{:S(2)}) collective-permute-start(bf16[1024,128]{1,0:T(8,128)(2,1)S(1)} %collective-permute-done.1.refs_2_.refs_6_), channel_id=1, source_target_pairs={{0,28},{4,0},{8,4},{12,8},{16,12},{20,16},{24,20},{28,24},{32,60},... | collective-permute-start | bytes 786440 | tf_op jit(solution)/shard_map/ppermute | solution.py:394
  13.9 18.8 %copy-start.3 = (bf16[1024,128]{1,0:T(8,128)(2,1)}, bf16[1024,128]{1,0:T(8,128)(2,1)S(1)}, u32[]{:S(2)}) copy-start(bf16[1024,128]{1,0:T(8,128)(2,1)S(1)} %collective-permute-done.4.refs_6_) | copy-start | bytes 786436
  21.7 7.7 %collective-permute-start.5 = (bf16[1024,128]{1,0:T(8,128)(2,1)S(1)}, bf16[1024,128]{1,0:T(8,128)(2,1)S(1)}, u32[]{:S(2)}, u32[]{:S(2)}) collective-permute-start(bf16[1024,128]{1,0:T(8,128)(2,1)S(1)} %collective-permute-done.2.refs_3_.refs_7_), channel_id=1, source_target_pairs={{0,4},{4,8},{8,12},{12,16},{16,20},{20,24},{24,28},{28,0},{32,36},... | collective-permute-start | bytes 786440 | tf_op jit(solution)/shard_map/ppermute | solution.py:394
  23.4 7.7 %collective-permute-start.6 = (bf16[1024,128]{1,0:T(8,128)(2,1)S(1)}, bf16[1024,128]{1,0:T(8,128)(2,1)S(1)}, u32[]{:S(2)}, u32[]{:S(2)}) collective-permute-start(bf16[1024,128]{1,0:T(8,128)(2,1)S(1)} %collective-permute-done.3.refs_4_.refs_8_), channel_id=1, source_target_pairs={{0,28},{4,0},{8,4},{12,8},{16,12},{20,16},{24,20},{28,24},{32,60},... | collective-permute-start | bytes 786440 | tf_op jit(solution)/shard_map/ppermute | solution.py:394
  23.7 9.0 %collective-permute-start.7 = (bf16[96,1024]{1,0:T(8,128)(2,1)S(1)}, bf16[96,1024]{1,0:T(8,128)(2,1)S(1)}, u32[]{:S(2)}, u32[]{:S(2)}) collective-permute-start(bf16[96,1024]{1,0:T(8,128)(2,1)S(1)} %get-tuple-element.44), channel_id=1, source_target_pairs={{0,32},{4,36},{8,40},{12,44},{16,48},{20,52},{24,56},{28,60},{32,6... | collective-permute-start | bytes 589832 | tf_op jit(solution)/shard_map/ppermute | solution.py:394
  25.2 8.9 %collective-permute-start.8 = (bf16[96,1024]{1,0:T(8,128)(2,1)S(1)}, bf16[96,1024]{1,0:T(8,128)(2,1)S(1)}, u32[]{:S(2)}, u32[]{:S(2)}) collective-permute-start(bf16[96,1024]{1,0:T(8,128)(2,1)S(1)} %get-tuple-element.45), channel_id=1, source_target_pairs={{0,64},{4,68},{8,72},{12,76},{16,80},{20,84},{24,88},{28,92},{32,9... | collective-permute-start | bytes 589832 | tf_op jit(solution)/shard_map/ppermute | solution.py:394
  27.9 6.2 %collective-permute-start.9 = (bf16[96,1024]{1,0:T(8,128)(2,1)S(1)}, bf16[96,1024]{1,0:T(8,128)(2,1)S(1)}, u32[]{:S(2)}, u32[]{:S(2)}) collective-permute-start(bf16[96,1024]{1,0:T(8,128)(2,1)S(1)} %get-tuple-element.46), channel_id=1, source_target_pairs={{0,96},{4,100},{8,104},{12,108},{16,112},{20,116},{24,120},{28,124... | collective-permute-start | bytes 589832 | tf_op jit(solution)/shard_map/ppermute | solution.py:394
  29.4 8.0 %collective-permute-start.10 = (bf16[1024,128]{1,0:T(8,128)(2,1)S(1)}, bf16[1024,128]{1,0:T(8,128)(2,1)}, u32[]{:S(2)}, u32[]{:S(2)}) collective-permute-start(bf16[1024,128]{1,0:T(8,128)(2,1)S(1)} %collective-permute-done.4.refs_6_), channel_id=1, source_target_pairs={{0,4},{4,8},{8,12},{12,16},{16,20},{20,24},{24,28},{28,0},{32,36},... | collective-permute-start | bytes 786440 | tf_op jit(solution)/shard_map/ppermute | solution.py:394
  31.1 6.5 %collective-permute-start.11 = (bf16[1024,128]{1,0:T(8,128)(2,1)S(1)}, bf16[1024,128]{1,0:T(8,128)(2,1)}, u32[]{:S(2)}, u32[]{:S(2)}) collective-permute-start(bf16[1024,128]{1,0:T(8,128)(2,1)S(1)} %collective-permute-done.4.refs_6_), channel_id=1, source_target_pairs={{0,28},{4,0},{8,4},{12,8},{16,12},{20,16},{24,20},{28,24},{32,60},... | collective-permute-start | bytes 786440 | tf_op jit(solution)/shard_map/ppermute | solution.py:394
  34.1 54.5 %collective-permute-start.18 = (bf16[7168,128]{1,0:T(8,128)(2,1)}, bf16[7168,128]{1,0:T(8,128)(2,1)}, u32[]{:S(2)}, u32[]{:S(2)}) collective-permute-start(bf16[7168,128]{1,0:T(8,128)(2,1)} %pack.1.refs_0_), channel_id=1, source_target_pairs={{0,32},{4,36},{8,40},{12,44},{16,48},{20,52},{24,56},{28,60},{32,6... | collective-permute-start | bytes 5505032 | tf_op jit(solution)/shard_map/ppermute | solution.py:394
  35.9 52.7 %collective-permute-start.19 = (bf16[7168,128]{1,0:T(8,128)(2,1)}, bf16[7168,128]{1,0:T(8,128)(2,1)}, u32[]{:S(2)}, u32[]{:S(2)}) collective-permute-start(bf16[7168,128]{1,0:T(8,128)(2,1)} %pack.1.refs_0_), channel_id=1, source_target_pairs={{0,96},{4,100},{8,104},{12,108},{16,112},{20,116},{24,120},{28,124... | collective-permute-start | bytes 5505032 | tf_op jit(solution)/shard_map/ppermute | solution.py:394
  37.6 7.1 %collective-permute-start.12 = (bf16[1024,128]{1,0:T(8,128)(2,1)S(1)}, bf16[1024,128]{1,0:T(8,128)(2,1)S(1)}, u32[]{:S(2)}, u32[]{:S(2)}) collective-permute-start(bf16[1024,128]{1,0:T(8,128)(2,1)S(1)} %collective-permute-done.5.refs_5_.refs_9_), channel_id=1, source_target_pairs={{0,4},{4,8},{8,12},{12,16},{16,20},{20,24},{24,28},{28,0},{32,36},... | collective-permute-start | bytes 786440 | tf_op jit(solution)/shard_map/ppermute | solution.py:394
  39.4 18.9 %collective-permute-start.13 = (bf16[1024,128]{1,0:T(8,128)(2,1)}, bf16[1024,128]{1,0:T(8,128)(2,1)S(1)}, u32[]{:S(2)}, u32[]{:S(2)}) collective-permute-start(bf16[1024,128]{1,0:T(8,128)(2,1)} %collective-permute-done.10.refs_7_), channel_id=1, source_target_pairs={{0,4},{4,8},{8,12},{12,16},{16,20},{20,24},{24,28},{28,0},{32,36},... | collective-permute-start | bytes 786440 | tf_op jit(solution)/shard_map/ppermute | solution.py:394
  42.1 16.2 %collective-permute-start.14 = (bf16[1024,128]{1,0:T(8,128)(2,1)}, bf16[1024,128]{1,0:T(8,128)(2,1)}, u32[]{:S(2)}, u32[]{:S(2)}) collective-permute-start(bf16[1024,128]{1,0:T(8,128)(2,1)} %collective-permute-done.11.refs_8_), channel_id=1, source_target_pairs={{0,28},{4,0},{8,4},{12,8},{16,12},{20,16},{24,20},{28,24},{32,60},... | collective-permute-start | bytes 786440 | tf_op jit(solution)/shard_map/ppermute | solution.py:394
  44.7 9.0 %copy-start.1 = (bf16[1024,128]{1,0:T(8,128)(2,1)}, bf16[1024,128]{1,0:T(8,128)(2,1)S(1)}, u32[]{:S(2)}) copy-start(bf16[1024,128]{1,0:T(8,128)(2,1)S(1)} %collective-permute-done.12.refs_0_.refs_1_) | copy-start | bytes 786436
  46.1 17.0 %all-to-all-start = ((f32[8,32,128]{2,1,0:T(8,128)}), f32[8,32,128]{2,1,0:T(8,128)S(1)}, u32[]{:S(2)}, u32[]{:S(2)}) async-start(f32[8,32,128]{2,1,0:T(8,128)} %p_column_rest.1), calls=%async_computation | async-start | bytes 262144 | tf_op jit(solution)/shard_map/all_to_all | solution.py:383
  58.3 24.3 %copy-start.2 = (bf16[1024,128]{1,0:T(8,128)(2,1)S(1)}, bf16[1024,128]{1,0:T(8,128)(2,1)}, u32[]{:S(2)}) copy-start(bf16[1024,128]{1,0:T(8,128)(2,1)} %copy-done.1) | copy-start | bytes 786436
  58.3 15.6 %copy-start.4 = (bf16[1024,128]{1,0:T(8,128)(2,1)}, bf16[1024,128]{1,0:T(8,128)(2,1)S(1)}, u32[]{:S(2)}) copy-start(bf16[1024,128]{1,0:T(8,128)(2,1)S(1)} %collective-permute-done.13.refs_9_) | copy-start | bytes 786436
  58.4 15.5 %collective-permute-start.15 = (bf16[1024,128]{1,0:T(8,128)(2,1)S(1)}, bf16[1024,128]{1,0:T(8,128)(2,1)S(1)}, u32[]{:S(2)}, u32[]{:S(2)}) collective-permute-start(bf16[1024,128]{1,0:T(8,128)(2,1)S(1)} %collective-permute-done.13.refs_9_), channel_id=1, source_target_pairs={{0,4},{4,8},{8,12},{12,16},{16,20},{20,24},{24,28},{28,0},{32,36},... | collective-permute-start | bytes 786440 | tf_op jit(solution)/shard_map/ppermute | solution.py:394
  59.9 14.0 %collective-permute-start.16 = (bf16[1024,128]{1,0:T(8,128)(2,1)}, bf16[1024,128]{1,0:T(8,128)(2,1)S(1)}, u32[]{:S(2)}, u32[]{:S(2)}) collective-permute-start(bf16[1024,128]{1,0:T(8,128)(2,1)} %collective-permute-done.14.refs_10_), channel_id=1, source_target_pairs={{0,28},{4,0},{8,4},{12,8},{16,12},{20,16},{24,20},{28,24},{32,60},... | collective-permute-start | bytes 786440 | tf_op jit(solution)/shard_map/ppermute | solution.py:394
  60.5 13.5 %collective-permute-start.17 = (bf16[1024,128]{1,0:T(8,128)(2,1)}, bf16[1024,128]{1,0:T(8,128)(2,1)S(1)}, u32[]{:S(2)}, u32[]{:S(2)}) collective-permute-start(bf16[1024,128]{1,0:T(8,128)(2,1)} %collective-permute-done.14.refs_10_), channel_id=1, source_target_pairs={{0,24},{4,28},{8,0},{12,4},{16,8},{20,12},{24,16},{28,20},{32,56},... | collective-permute-start | bytes 786440 | tf_op jit(solution)/shard_map/ppermute | solution.py:394
  73.9 14.7 %copy-start.5 = (bf16[1024,128]{1,0:T(8,128)(2,1)}, bf16[1024,128]{1,0:T(8,128)(2,1)S(1)}, u32[]{:S(2)}) copy-start(bf16[1024,128]{1,0:T(8,128)(2,1)S(1)} %collective-permute-done.15.refs_11_) | copy-start | bytes 786436
  73.9 14.7 %copy-start.6 = (bf16[1024,128]{1,0:T(8,128)(2,1)}, bf16[1024,128]{1,0:T(8,128)(2,1)S(1)}, u32[]{:S(2)}) copy-start(bf16[1024,128]{1,0:T(8,128)(2,1)S(1)} %collective-permute-done.16.refs_12_) | copy-start | bytes 786436
  73.9 14.7 %copy-start.7 = (bf16[1024,128]{1,0:T(8,128)(2,1)}, bf16[1024,128]{1,0:T(8,128)(2,1)S(1)}, u32[]{:S(2)}) copy-start(bf16[1024,128]{1,0:T(8,128)(2,1)S(1)} %collective-permute-done.17.refs_13_) | copy-start | bytes 786436
  74.0 22.1 %all-to-all-start.2 = ((f32[32,32,128]{2,1,0:T(8,128)}), f32[32,32,128]{2,1,0:T(8,128)S(1)}, u32[]{:S(2)}, u32[]{:S(2)}) async-start(f32[32,32,128]{2,1,0:T(8,128)} %add_spread.3), calls=%async_computation.2 | async-start | bytes 1048576 | tf_op jit(solution)/shard_map/all_to_all | solution.py:383
  82.6 12.4 %collective-permute-start.20 = (bf16[1024,128]{1,0:T(8,128)(2,1)S(1)}, bf16[1024,128]{1,0:T(8,128)(2,1)}, u32[]{:S(2)}, u32[]{:S(2)}) collective-permute-start(bf16[1024,128]{1,0:T(8,128)(2,1)S(1)} %copy-done.2), channel_id=1, source_target_pairs={{0,32},{4,36},{8,40},{12,44},{16,48},{20,52},{24,56},{28,60},{32,6... | collective-permute-start | bytes 786440 | tf_op jit(solution)/shard_map/ppermute | solution.py:394
  84.2 10.8 %collective-permute-start.21 = (bf16[1024,128]{1,0:T(8,128)(2,1)S(1)}, bf16[1024,128]{1,0:T(8,128)(2,1)}, u32[]{:S(2)}, u32[]{:S(2)}) collective-permute-start(bf16[1024,128]{1,0:T(8,128)(2,1)S(1)} %copy-done.2), channel_id=1, source_target_pairs={{0,96},{4,100},{8,104},{12,108},{16,112},{20,116},{24,120},{28,124... | collective-permute-start | bytes 786440 | tf_op jit(solution)/shard_map/ppermute | solution.py:394
  102.9 10.7 %collective-permute-start.22 = (f32[32,448]{1,0:T(8,128)S(1)}, f32[32,448]{1,0:T(8,128)S(1)}, u32[]{:S(2)}, u32[]{:S(2)}) collective-permute-start(f32[32,448]{1,0:T(8,128)S(1)} %get-tuple-element.68.a_ref), channel_id=1, source_target_pairs={{0,1},{1,2},{2,3},{3,0},{4,5},{5,6},{6,7},{7,4},{8,9},{9,10},{10,1... | collective-permute-start | bytes 172040 | tf_op jit(solution)/shard_map/ppermute | solution.py:388
  104.6 9.1 %collective-permute-start.23 = (f32[32,448]{1,0:T(8,128)S(1)}, f32[32,448]{1,0:T(8,128)S(1)}, u32[]{:S(2)}, u32[]{:S(2)}) collective-permute-start(f32[32,448]{1,0:T(8,128)S(1)} %get-tuple-element.68.a_ref), channel_id=1, source_target_pairs={{0,3},{1,0},{2,1},{3,2},{4,7},{5,4},{6,5},{7,6},{8,11},{9,8},{10,9... | collective-permute-start | bytes 172040 | tf_op jit(solution)/shard_map/ppermute | solution.py:388
  106.3 7.4 %collective-permute-start.24 = (f32[32,448]{1,0:T(8,128)S(1)}, f32[32,448]{1,0:T(8,128)S(1)}, u32[]{:S(2)}, u32[]{:S(2)}) collective-permute-start(f32[32,448]{1,0:T(8,128)S(1)} %get-tuple-element.68.a_ref), channel_id=1, source_target_pairs={{0,2},{1,3},{2,0},{3,1},{4,6},{5,7},{6,4},{7,5},{8,10},{9,11},{10,... | collective-permute-start | bytes 172040 | tf_op jit(solution)/shard_map/ppermute | solution.py:388

commit v4 on v3

--- a/solution.py
+++ b/solution.py
@@ -2,6 +2,7 @@
 
 import jax
 import jax.numpy as jnp
+import numpy as np
 from jax import lax
 from jax.experimental import pallas as pl
 from jax.experimental.pallas import tpu as pltpu
@@ -196,8 +197,8 @@
     )(*arrays)
 
 
-def slab_copies(at_ref, first, e_hbm, x_hbm, e_ref, x_ref):
-    slabs = [(r, i) for r in x_hbm for i in range(r.shape[0] // 1024)]
+def slab_copies(at_ref, first, e_hbm, x_hbm, parts_of, e_ref, x_ref):
+    slabs = [(r, first_of + i) for r, (first_of, n) in zip(x_hbm, parts_of) for i in range(n)]
     pairs = []
     for place, (r, i) in enumerate(slabs):
         cols = pl.ds(pl.multiple_of(at_ref[first + place] * 128, 128), 128)
@@ -217,9 +218,9 @@
         out_ref[place] = both.astype(BF16)
 
 
-def correct_kernel(at_ref, h_hbm, e_hbm, *refs):
+def correct_kernel(parts_of, at_ref, h_hbm, e_hbm, *refs):
     x_hbm, (out_ref, h_ref, e_ref, x_ref, sems) = refs[:-5], refs[-5:]
-    copies = slab_copies(at_ref, 0, e_hbm, x_hbm, e_ref, x_ref)
+    copies = slab_copies(at_ref, 0, e_hbm, x_hbm, parts_of, e_ref, x_ref)
     loads = load_all([(h_hbm, h_ref)] + copies, sems)
     loads[0].wait()
     for pair in range(at_ref.shape[0] // 2):
@@ -235,10 +236,10 @@
     ]
 
 
-def correct(places, h_t, e_t, arrays):
+def correct(places, h_t, e_t, arrays, parts_of):
     n = places.shape[0]
     return pl.pallas_call(
-        correct_kernel,
+        functools.partial(correct_kernel, parts_of),
         in_specs=[SMEM] + [HBM] * (2 + len(arrays)),
         out_specs=VMEM,
         out_shape=pltpu.VMEM((n, 448, 128), BF16),
@@ -256,7 +257,7 @@
     )
     x_hbm, (w_ref, out_hbm, h_ref, e_ref, x_ref, sems, out_ref, out_sem) = refs[:-8], refs[-8:]
     rest = len(x_hbm)
-    copies = slab_copies(at_ref, 32 - rest, e_hbm, x_hbm, e_ref, x_ref)
+    copies = slab_copies(at_ref, 32 - rest, e_hbm, x_hbm, [(0, 1)] * rest, e_ref, x_ref)
     loads = load_all([(h_hbm, h_ref)] + copies, sems)
     slabs = [(r, i) for r in [*kept_refs, out_ref] for i in range(r.shape[0])]
 
@@ -298,10 +299,9 @@
 
 
 def factor_kernel(p_ref, inv_ref, p_out_ref, low_ref):
-    p = jnp.concatenate([p_ref[i] for i in range(32)], axis=1)
-    gram = lax.dot_general(
-        p, p, NT, precision=lax.Precision.HIGHEST, preferred_element_type=F32
-    )
+    p = split3(jnp.concatenate([p_ref[i] for i in range(32)], axis=1))
+    gram = fold3(lax.dot_general(p, p, NT, preferred_element_type=F32))
+    gram = gram[:, 0:32] + gram[:, 32:64] + gram[:, 64:96]
     row = lax.broadcasted_iota(jnp.int32, (32, 128), 0)
     col = lax.broadcasted_iota(jnp.int32, (32, 128), 1)
     work = jnp.concatenate([gram, jnp.zeros((32, 96), F32)], axis=1)
@@ -314,7 +314,9 @@
         work = work - below * (work[j : j + 1, :] / pivot)
     inverse = work[:, 32:64] / jnp.sqrt(scale)
     inv_ref[...] = inverse
-    out = jnp.dot(inverse, p, precision=lax.Precision.HIGHEST, preferred_element_type=F32)
+    terms = split3(inverse)
+    terms = jnp.concatenate([terms, terms, terms], axis=1)
+    out = fold3(jnp.dot(terms, p, preferred_element_type=F32))
     p_out_ref[...] = out
     low_ref[...] = out.astype(BF16)
 
@@ -404,8 +406,10 @@
     x_index, z_index = me // 8, me % 8
     z_order = jnp.stack([(z_index + rz) % 8 for rz in SOURCE_Z]).astype(jnp.int32)
 
-    def places(rx):
-        return (x_index + rx) % 4 * 8 + z_order
+    def places(*columns):
+        rx = np.concatenate([np.full(len(rz), r) for r, rz in columns]).astype(np.int32)
+        rz = np.concatenate([rz for _, rz in columns]).astype(np.int32)
+        return ((x_index + rx) % 4 * 8 + (z_index + rz) % 8).astype(jnp.int32)
 
     e_t, h_t = error_buffer[0, 0].T, hidden_grad[0].T
     mine, *others = first(x_index.astype(jnp.int32)[None], q_previous[0].T, e_t, h_t)
@@ -425,20 +429,24 @@
     part, t = column(z_order, [mine, g1, g2, g3], [x, p1, m1, p2, m2, p3, m3])
     column_groups = [[8 * i + z for z in range(8)] for i in range(4)]
     p_parts = swap(column_rest(z_order, part, t, [end]), groups=column_groups)
-    kept_own = correct(places(0), h_t, e_t, [bundle, end])
+    own_early, own_late = (0, SOURCE_Z[:4]), (0, SOURCE_Z[4:])
+    kept_own = correct(places(own_early), h_t, e_t, [bundle], [(0, 4)])
     fp2, fm2 = move(fp1, 0, 1), move(fm1, 0, -1)
     fp2, fm2, kept_own = together(fp2, fm2, kept_own)
     fp3, fm3, f_end = move(fp2, 0, 1), move(fm2, 0, -1), move(fm2, 0, -2)
     p_parts, kept_own = together(add_spread(p_parts, 4, 1.0), kept_own)
     p_parts = add_spread(swap(p_parts, "replica"), 32, 0.25)
-    p_parts, fp3, fm3, f_end = together(p_parts, fp3, fm3, f_end)
+    kept_late = correct(places(own_late), h_t, e_t, [bundle, end], [(4, 3), (0, 1)])
+    p_parts, fp3, fm3, f_end, kept_late = together(p_parts, fp3, fm3, f_end, kept_late)
     far = [f0, fp1, fm1, fp2, fm2, fp3, fm3, f_end]
     p_blocks = swap(p_parts)
-    at_near = jnp.concatenate([places(-1)[:7], places(1)[:7]])
-    at_rest = jnp.concatenate([places(-1)[7:], places(1)[7:], places(2)])
-    at = jnp.concatenate([places(0), at_near, at_rest])
-    kept = [kept_own, correct(at_near, h_t, e_t, near)]
-    w_part, piece = finish(at, p_blocks, kept, h_t, e_t, [*near_end, *far])
+    middle = [(-1, SOURCE_Z[:7]), (1, SOURCE_Z[:7]), (2, SOURCE_Z[:4])]
+    rest = [(-1, SOURCE_Z[7:]), (1, SOURCE_Z[7:]), (2, SOURCE_Z[4:])]
+    at = places(own_early, own_late, *middle, *rest)
+    parts_of = [(0, 7), (0, 7)] + [(0, 1)] * 4
+    kept_middle = correct(places(*middle), h_t, e_t, [*near, *far[:4]], parts_of)
+    kept = [kept_own, kept_late, kept_middle]
+    w_part, piece = finish(at, p_blocks, kept, h_t, e_t, [*near_end, *far[4:]])
     parts = replicas(w_part)
     inverse, p_factor, p_low = factor(p_blocks)
     q_factor, new_error = final(at, inverse, parts, p_low, kept, piece)

time: 120 us -> 117 us (0.975)
  blocking collectives: 9.89 us -> 0 us
  waiting for transfers between devices: 12.9 us -> 16.7 us
  starting transfers between devices: 55.3 us -> 59 us
  local copies, waits for them, and re-layouts: 2.69 us -> 0.84 us
  Pallas kernels: 37.4 us -> 39.1 us
    all_to_all x1 -> x0, blocking collectives: 9.89 us -> none  [swap(): return lax.all_to_all(v, axis, 0, 0, axis_index_groups=groups)]
    all_to_all x2 -> x3, waiting for transfers between devices: 1.04 us -> 4.73 us  [swap(): return lax.all_to_all(v, axis, 0, 0, axis_index_groups=groups)]
    all_to_all x2 -> x3, starting transfers between devices: 16.2 us -> 19.9 us  [swap(): return lax.all_to_all(v, axis, 0, 0, axis_index_groups=groups)]
    pallas_call x2 -> x3, Pallas kernels: 10.9 us -> 14.2 us  [correct(): pl.pallas_call(functools.partial(correct_kernel, parts_of), in_specs=[SME...]
    concatenate x1 -> x0, local copies, waits for them, and re-layouts: 1.35 us -> none  [shards(): at = jnp.concatenate([places(0), at_near, at_rest])]
    pallas_call x1, Pallas kernels: 6.91 us -> 5.57 us  [finish(): pl.pallas_call(functools.partial(finish_kernel, len(kept)), in_specs=[SME...]
    slice x2 -> x0, local copies, waits for them, and re-layouts: 1.22 us -> none  [shards(): at_rest = jnp.concatenate([places(-1)[7:], places(1)[7:], places(2)])]
  transfers between devices with their start and end apart: 27 -> 28, of which waited for: 8 -> 10; matrix products, arithmetic and copies ran while one was open for 2% -> 0% of each run, Pallas kernels for 21% -> 24%
where the time goes in v4:
time: 117 us
  starting transfers between devices  59 us (50%)
  Pallas kernels  39.1 us (33%)
  waiting for transfers between devices  16.7 us (14%)
    ppermute x22, starting transfers between devices, move(): return lax.ppermute(v, 'hidden', pairs)  33.8 us
    all_to_all x3, starting transfers between devices, swap(): return lax.all_to_all(v, axis, 0, 0, axis_index_groups=groups)  19.9 us
    pallas_call x3, Pallas kernels, correct(): pl.pallas_call(functools.partial(correct_kernel, parts_of), in_specs=[SME...  14.2 us
    ppermute x22, waiting for transfers between devices, move(): return lax.ppermute(v, 'hidden', pairs)  12 us
    pallas_call x1, Pallas kernels, finish(): pl.pallas_call(functools.partial(finish_kernel, len(kept)), in_specs=[SME...  5.57 us
    pallas_call x1, Pallas kernels, final(): pl.pallas_call(final_kernel, in_specs=[SMEM] + [VMEM] * (6 + len(kept)) +...  5.31 us
    ppermute x3, starting transfers between devices, replicas(): lax.ppermute(v, 'replica', [(i, (i + s) % 4) for i in range(4)])  5.3 us
    pallas_call x1, Pallas kernels, factor(): pl.pallas_call(factor_kernel, in_specs=[VMEM], out_specs=[VMEM] * 3, out_...  4.8 us
  transfers between devices with their start and end apart: 28, of which 10 were waited for; matrix products, arithmetic and copies ran while one was open for 0% of the time, Pallas kernels for 24%

profile of v4, /device:TPU:32, one launch (start us, length us, event | category | flops | bytes accessed | tf_op | source)
XLA Modules:
  0.0 116.8 jit_solution(2754046070495489195)
XLA Ops:
  0.6 2.0 %collective-permute-start = (bf16[1024,128]{1,0:T(8,128)(2,1)}, bf16[1024,128]{1,0:T(8,128)(2,1)S(1)}, u32[]{:S(2)}, u32[]{:S(2)}) collective-permute-start(bf16[1024,128]{1,0:T(8,128)(2,1)} %bitcast.28), channel_id=1, source_target_pairs={{0,4},{4,8},{8,12},{12,16},{16,20},{20,24},{24,28},{28,0},{32,36},... | collective-permute-start | bytes 786440 | tf_op jit(solution)/shard_map/ppermute | solution.py:396
  2.7 3.0 %collective-permute-start.4 = (bf16[1024,128]{1,0:T(8,128)(2,1)}, bf16[1024,128]{1,0:T(8,128)(2,1)S(1)}, u32[]{:S(2)}, u32[]{:S(2)}) collective-permute-start(bf16[1024,128]{1,0:T(8,128)(2,1)} %bitcast.30), channel_id=1, source_target_pairs={{0,64},{4,68},{8,72},{12,76},{16,80},{20,84},{24,88},{28,92},{32,9... | collective-permute-start | bytes 786440 | tf_op jit(solution)/shard_map/ppermute | solution.py:396
  5.8 2.7 %eq_hq.1 = (bf16[96,1024]{1,0:T(8,128)(2,1)S(1)}, bf16[96,1024]{1,0:T(8,128)(2,1)S(1)}, bf16[96,1024]{1,0:T(8,128)(2,1)S(1)}, bf16[96,1024]{1,0:T(8,128)(2,1)S(1)}) custom-call(s32[1]{0:T(128)} %bitcast.9.x_ref, f32[32,448]{1,0:T(8,128)} %bitcast.43, bf16[448,4096]{1,0:T(8,128)(2,1)} %bitcast.33, bf16[448,1024]{1,0:T(8,128)(2,1)} %bitcast.38), custom_call_target="tpu_custom_call" | custom-call | tf_op jit(solution)/shard_map/eq_hq/pallas_call | solution.py:78
  8.5 0.5 collective-permute-done.refs_1_.refs_5_
  9.0 1.8 %collective-permute-done.1.refs_2_.refs_6_ = bf16[1024,128]{1,0:T(8,128)(2,1)S(1)} collective-permute-done((bf16[1024,128]{1,0:T(8,128)(2,1)}, bf16[1024,128]{1,0:T(8,128)(2,1)S(1)}, u32[]{:S(2)}, u32[]{:S(2)}) %collective-permute-start.1) | collective-permute-done | bytes 262176 | tf_op jit(solution)/shard_map/ppermute | solution.py:396
  10.8 3.1 %collective-permute-start.2 = (bf16[1024,128]{1,0:T(8,128)(2,1)S(1)}, bf16[1024,128]{1,0:T(8,128)(2,1)S(1)}, u32[]{:S(2)}, u32[]{:S(2)}) collective-permute-start(bf16[1024,128]{1,0:T(8,128)(2,1)S(1)} %collective-permute-done.refs_1_.refs_5_), channel_id=1, source_target_pairs={{0,4},{4,8},{8,12},{12,16},{16,20},{20,24},{24,28},{28,0},{32,36},... | collective-permute-start | bytes 786440 | tf_op jit(solution)/shard_map/ppermute | solution.py:396
  13.9 5.0 %collective-permute-done.2.refs_3_.refs_7_ = bf16[1024,128]{1,0:T(8,128)(2,1)S(1)} collective-permute-done((bf16[1024,128]{1,0:T(8,128)(2,1)S(1)}, bf16[1024,128]{1,0:T(8,128)(2,1)S(1)}, u32[]{:S(2)}, u32[]{:S(2)}) %collective-permute-start.2) | collective-permute-done | bytes 262176 | tf_op jit(solution)/shard_map/ppermute | solution.py:396
  18.9 2.8 %collective-permute-done.3.refs_4_.refs_8_ = bf16[1024,128]{1,0:T(8,128)(2,1)S(1)} collective-permute-done((bf16[1024,128]{1,0:T(8,128)(2,1)S(1)}, bf16[1024,128]{1,0:T(8,128)(2,1)S(1)}, u32[]{:S(2)}, u32[]{:S(2)}) %collective-permute-start.3) | collective-permute-done | bytes 262176 | tf_op jit(solution)/shard_map/ppermute | solution.py:396
  21.7 1.7 %collective-permute-start.5 = (bf16[1024,128]{1,0:T(8,128)(2,1)S(1)}, bf16[1024,128]{1,0:T(8,128)(2,1)S(1)}, u32[]{:S(2)}, u32[]{:S(2)}) collective-permute-start(bf16[1024,128]{1,0:T(8,128)(2,1)S(1)} %collective-permute-done.2.refs_3_.refs_7_), channel_id=1, source_target_pairs={{0,4},{4,8},{8,12},{12,16},{16,20},{20,24},{24,28},{28,0},{32,36},... | collective-permute-start | bytes 786440 | tf_op jit(solution)/shard_map/ppermute | solution.py:396
  23.4 0.3 collective-permute-start.6
  23.7 1.5 %collective-permute-start.7 = (bf16[96,1024]{1,0:T(8,128)(2,1)S(1)}, bf16[96,1024]{1,0:T(8,128)(2,1)S(1)}, u32[]{:S(2)}, u32[]{:S(2)}) collective-permute-start(bf16[96,1024]{1,0:T(8,128)(2,1)S(1)} %get-tuple-element.45), channel_id=1, source_target_pairs={{0,32},{4,36},{8,40},{12,44},{16,48},{20,52},{24,56},{28,60},{32,6... | collective-permute-start | bytes 589832 | tf_op jit(solution)/shard_map/ppermute | solution.py:396
  25.2 2.7 %collective-permute-start.8 = (bf16[96,1024]{1,0:T(8,128)(2,1)S(1)}, bf16[96,1024]{1,0:T(8,128)(2,1)S(1)}, u32[]{:S(2)}, u32[]{:S(2)}) collective-permute-start(bf16[96,1024]{1,0:T(8,128)(2,1)S(1)} %get-tuple-element.46), channel_id=1, source_target_pairs={{0,64},{4,68},{8,72},{12,76},{16,80},{20,84},{24,88},{28,92},{32,9... | collective-permute-start | bytes 589832 | tf_op jit(solution)/shard_map/ppermute | solution.py:396
  27.9 1.4 %collective-permute-start.9 = (bf16[96,1024]{1,0:T(8,128)(2,1)S(1)}, bf16[96,1024]{1,0:T(8,128)(2,1)S(1)}, u32[]{:S(2)}, u32[]{:S(2)}) collective-permute-start(bf16[96,1024]{1,0:T(8,128)(2,1)S(1)} %get-tuple-element.47), channel_id=1, source_target_pairs={{0,96},{4,100},{8,104},{12,108},{16,112},{20,116},{24,120},{28,124... | collective-permute-start | bytes 589832 | tf_op jit(solution)/shard_map/ppermute | solution.py:396
  29.4 1.7 %collective-permute-start.10 = (bf16[1024,128]{1,0:T(8,128)(2,1)S(1)}, bf16[1024,128]{1,0:T(8,128)(2,1)}, u32[]{:S(2)}, u32[]{:S(2)}) collective-permute-start(bf16[1024,128]{1,0:T(8,128)(2,1)S(1)} %collective-permute-done.4.refs_2_), channel_id=1, source_target_pairs={{0,4},{4,8},{8,12},{12,16},{16,20},{20,24},{24,28},{28,0},{32,36},... | collective-permute-start | bytes 786440 | tf_op jit(solution)/shard_map/ppermute | solution.py:396
  31.1 0.3 collective-permute-start.11
  31.4 1.3 %pack.1.refs_0_ = bf16[7168,128]{1,0:T(8,128)(2,1)} custom-call(bf16[1024,128]{1,0:T(8,128)(2,1)S(1)} %bitcast.31, bf16[1024,128]{1,0:T(8,128)(2,1)S(1)} %collective-permute-done.refs_1_.refs_5_, bf16[1024,128]{1,0:T(8,128)(2,1)S(1)} %collective-permute-done.1.refs_2_.refs_6_, bf16[1024,128]{1,0:T(8,128)(2,1)S(1)} %collective-permute-done.2.refs_3_.refs_7_, ...), custom_call_target="tpu_custom_call" | custom-call | tf_op jit(solution)/shard_map/pack/pallas_call | solution.py:189
  32.7 1.4 %collective-permute-done.8.refs_2_ = bf16[96,1024]{1,0:T(8,128)(2,1)S(1)} collective-permute-done((bf16[96,1024]{1,0:T(8,128)(2,1)S(1)}, bf16[96,1024]{1,0:T(8,128)(2,1)S(1)}, u32[]{:S(2)}, u32[]{:S(2)}) %collective-permute-start.8) | collective-permute-done | bytes 196640 | tf_op jit(solution)/shard_map/ppermute | solution.py:396
  34.1 1.8 %collective-permute-start.18 = (bf16[7168,128]{1,0:T(8,128)(2,1)}, bf16[7168,128]{1,0:T(8,128)(2,1)}, u32[]{:S(2)}, u32[]{:S(2)}) collective-permute-start(bf16[7168,128]{1,0:T(8,128)(2,1)} %pack.1.refs_0_), channel_id=1, source_target_pairs={{0,32},{4,36},{8,40},{12,44},{16,48},{20,52},{24,56},{28,60},{32,6... | collective-permute-start | bytes 5505032 | tf_op jit(solution)/shard_map/ppermute | solution.py:396
  35.9 1.5 %collective-permute-start.19 = (bf16[7168,128]{1,0:T(8,128)(2,1)}, bf16[7168,128]{1,0:T(8,128)(2,1)}, u32[]{:S(2)}, u32[]{:S(2)}) collective-permute-start(bf16[7168,128]{1,0:T(8,128)(2,1)} %pack.1.refs_0_), channel_id=1, source_target_pairs={{0,96},{4,100},{8,104},{12,108},{16,112},{20,116},{24,120},{28,124... | collective-permute-start | bytes 5505032 | tf_op jit(solution)/shard_map/ppermute | solution.py:396
  37.3 0.3 collective-permute-done.11.refs_4_
  37.6 1.8 %collective-permute-start.12 = (bf16[1024,128]{1,0:T(8,128)(2,1)S(1)}, bf16[1024,128]{1,0:T(8,128)(2,1)S(1)}, u32[]{:S(2)}, u32[]{:S(2)}) collective-permute-start(bf16[1024,128]{1,0:T(8,128)(2,1)S(1)} %collective-permute-done.5.refs_5_.refs_9_), channel_id=1, source_target_pairs={{0,4},{4,8},{8,12},{12,16},{16,20},{20,24},{24,28},{28,0},{32,36},... | collective-permute-start | bytes 786440 | tf_op jit(solution)/shard_map/ppermute | solution.py:396
  39.4 2.7 %collective-permute-start.13 = (bf16[1024,128]{1,0:T(8,128)(2,1)}, bf16[1024,128]{1,0:T(8,128)(2,1)}, u32[]{:S(2)}, u32[]{:S(2)}) collective-permute-start(bf16[1024,128]{1,0:T(8,128)(2,1)} %collective-permute-done.10.refs_3_), channel_id=1, source_target_pairs={{0,4},{4,8},{8,12},{12,16},{16,20},{20,24},{24,28},{28,0},{32,36},... | collective-permute-start | bytes 786440 | tf_op jit(solution)/shard_map/ppermute | solution.py:396
  42.2 2.4 %p_column.1 = (f32[8,32,128]{2,1,0:T(8,128)S(1)}, bf16[96,1024]{1,0:T(8,128)(2,1)S(1)}) custom-call(s32[8]{0:T(128)S(1)} %stack.35.z_ref, bf16[96,1024]{1,0:T(8,128)(2,1)S(1)} %get-tuple-element.40.refs_0_, bf16[96,1024]{1,0:T(8,128)(2,1)S(1)} %collective-permute-done.7.refs_1_, bf16[96,1024]{1,0:T(8,128)(2,1)S(1)} %collective-permute-done.8.refs_2_, ...), custom_call_target="tpu_custom_call" | custom-call | tf_op jit(solution)/shard_map/p_column/pallas_call | solution.py:124
  44.6 0.2 collective-permute-done.12.refs_0_.refs_1_
  44.8 1.4 %p_column_rest.1 = f32[8,32,128]{2,1,0:T(8,128)} custom-call(s32[8]{0:T(128)S(1)} %stack.35.z_ref, f32[8,32,128]{2,1,0:T(8,128)S(1)} %get-tuple-element.53.part_ref, bf16[96,1024]{1,0:T(8,128)(2,1)S(1)} %get-tuple-element.54.t_ref, bf16[1024,128]{1,0:T(8,128)(2,1)S(1)} %collective-permute-done.12.refs_0_.refs_1_), custom_call_target="tpu_custom_call" | custom-call | tf_op jit(solution)/shard_map/p_column_rest/pallas_call | solution.py:154
  46.2 7.6 %all-to-all-start = ((f32[8,32,128]{2,1,0:T(8,128)}), f32[8,32,128]{2,1,0:T(8,128)S(1)}, u32[]{:S(2)}, u32[]{:S(2)}) async-start(f32[8,32,128]{2,1,0:T(8,128)} %p_column_rest.1), calls=%async_computation | async-start | bytes 262144 | tf_op jit(solution)/shard_map/all_to_all | solution.py:385
  53.8 3.2 %corrected.3.refs_0_ = bf16[4,448,128]{2,1,0:T(8,128)(2,1)S(1)} custom-call(s32[4]{0:T(128)S(1)} %fusion.3.at_ref, bf16[448,1024]{1,0:T(8,128)(2,1)} %bitcast.39, bf16[448,4096]{1,0:T(8,128)(2,1)} %bitcast.34, bf16[7168,128]{1,0:T(8,128)(2,1)} %pack.1.refs_0_), custom_call_target="tpu_custom_call" | custom-call | tf_op jit(solution)/shard_map/corrected/pallas_call | solution.py:241
  57.1 1.5 %collective-permute-start.15 = (bf16[1024,128]{1,0:T(8,128)(2,1)}, bf16[1024,128]{1,0:T(8,128)(2,1)S(1)}, u32[]{:S(2)}, u32[]{:S(2)}) collective-permute-start(bf16[1024,128]{1,0:T(8,128)(2,1)} %collective-permute-done.13.refs_5_), channel_id=1, source_target_pairs={{0,4},{4,8},{8,12},{12,16},{16,20},{20,24},{24,28},{28,0},{32,36},... | collective-permute-start | bytes 786440 | tf_op jit(solution)/shard_map/ppermute | solution.py:396
  58.6 0.6 collective-permute-start.16
  59.2 2.7 %collective-permute-start.17 = (bf16[1024,128]{1,0:T(8,128)(2,1)}, bf16[1024,128]{1,0:T(8,128)(2,1)S(1)}, u32[]{:S(2)}, u32[]{:S(2)}) collective-permute-start(bf16[1024,128]{1,0:T(8,128)(2,1)} %collective-permute-done.14.refs_7_), channel_id=1, source_target_pairs={{0,24},{4,28},{8,0},{12,4},{16,8},{20,12},{24,16},{28,20},{32,56},... | collective-permute-start | bytes 786440 | tf_op jit(solution)/shard_map/ppermute | solution.py:396
  61.9 0.3 all-to-all-done.in_ref
  62.2 0.6 add_spread.2
  62.8 4.5 %all-to-all-start.1 = ((f32[4,32,128]{2,1,0:T(8,128)}), f32[4,32,128]{2,1,0:T(8,128)S(1)}, u32[]{:S(2)}, u32[]{:S(2)}) async-start(f32[4,32,128]{2,1,0:T(8,128)} %add_spread.2), calls=%async_computation.1 | async-start | bytes 131072 | tf_op jit(solution)/shard_map/all_to_all | solution.py:385
  67.4 3.2 %corrected.4.refs_1_ = bf16[4,448,128]{2,1,0:T(8,128)(2,1)S(1)} custom-call(s32[4]{0:T(128)S(1)} %fusion.5.at_ref, bf16[448,1024]{1,0:T(8,128)(2,1)} %bitcast.40, bf16[448,4096]{1,0:T(8,128)(2,1)} %bitcast.35, bf16[7168,128]{1,0:T(8,128)(2,1)} %pack.1.refs_0_, bf16[1024,128]{1,0:T(8,128)(2,1)} %copy-done), custom_call_target="tpu_custom_call" | custom-call | tf_op jit(solution)/shard_map/corrected/pallas_call | solution.py:241
  70.6 2.3 %all-to-all-done.1.in_ref = f32[4,32,128]{2,1,0:T(8,128)S(1)} async-done(((f32[4,32,128]{2,1,0:T(8,128)}), f32[4,32,128]{2,1,0:T(8,128)S(1)}, u32[]{:S(2)}, u32[]{:S(2)}) %all-to-all-start.1) | async-done | bytes 65568 | tf_op jit(solution)/shard_map/all_to_all | solution.py:385
  72.9 0.9 add_spread.3
  73.8 7.9 %all-to-all-start.2 = ((f32[32,32,128]{2,1,0:T(8,128)}), f32[32,32,128]{2,1,0:T(8,128)S(1)}, u32[]{:S(2)}, u32[]{:S(2)}) async-start(f32[32,32,128]{2,1,0:T(8,128)} %add_spread.3), calls=%async_computation.2 | async-start | bytes 1048576 | tf_op jit(solution)/shard_map/all_to_all | solution.py:385
  81.7 1.5 %collective-permute-start.20 = (bf16[1024,128]{1,0:T(8,128)(2,1)}, bf16[1024,128]{1,0:T(8,128)(2,1)S(1)}, u32[]{:S(2)}, u32[]{:S(2)}) collective-permute-start(bf16[1024,128]{1,0:T(8,128)(2,1)} %copy-done), channel_id=1, source_target_pairs={{0,32},{4,36},{8,40},{12,44},{16,48},{20,52},{24,56},{28,60},{32,6... | collective-permute-start | bytes 786440 | tf_op jit(solution)/shard_map/ppermute | solution.py:396
  83.2 1.8 %collective-permute-start.21 = (bf16[1024,128]{1,0:T(8,128)(2,1)}, bf16[1024,128]{1,0:T(8,128)(2,1)}, u32[]{:S(2)}, u32[]{:S(2)}) collective-permute-start(bf16[1024,128]{1,0:T(8,128)(2,1)} %copy-done), channel_id=1, source_target_pairs={{0,96},{4,100},{8,104},{12,108},{16,112},{20,116},{24,120},{28,124... | collective-permute-start | bytes 786440 | tf_op jit(solution)/shard_map/ppermute | solution.py:396
  85.1 7.7 %corrected.5.refs_2_ = bf16[18,448,128]{2,1,0:T(8,128)(2,1)S(1)} custom-call(s32[18]{0:T(128)S(1)} %fusion.1.at_ref, bf16[448,1024]{1,0:T(8,128)(2,1)} %bitcast.41, bf16[448,4096]{1,0:T(8,128)(2,1)} %bitcast.36, bf16[7168,128]{1,0:T(8,128)(2,1)} %collective-permute-done.18.refs_0_, bf16[7168,128]{1,0:T(8,128)(2,1)} %collective-permute-done.19.refs_1_, ...), custom_call_target="tpu_custom_call" | custom-call | tf_op jit(solution)/shard_map/corrected/pallas_call | solution.py:241
  92.8 0.7 copy-done.6
  93.5 2.1 %all-to-all-done.2.p_ref = f32[32,32,128]{2,1,0:T(8,128)S(1)} async-done(((f32[32,32,128]{2,1,0:T(8,128)}), f32[32,32,128]{2,1,0:T(8,128)S(1)}, u32[]{:S(2)}, u32[]{:S(2)}) %all-to-all-start.2) | async-done | bytes 524320 | tf_op jit(solution)/shard_map/all_to_all | solution.py:385
  95.7 5.6 %c_p.1 = (f32[32,448]{1,0:T(8,128)S(1)}, bf16[6,448,128]{2,1,0:T(8,128)(2,1)}) custom-call(s32[32]{0:T(128)S(1)} %fusion.at_ref, f32[32,32,128]{2,1,0:T(8,128)S(1)} %all-to-all-done.2.p_ref, bf16[4,448,128]{2,1,0:T(8,128)(2,1)S(1)} %corrected.3.refs_0_, bf16[4,448,128]{2,1,0:T(8,128)(2,1)S(1)} %corrected.4.refs_1_, ...), custom_call_target="tpu_custom_call" | custom-call | tf_op jit(solution)/shard_map/c_p/pallas_call | solution.py:283
  101.2 1.7 %collective-permute-start.22 = (f32[32,448]{1,0:T(8,128)S(1)}, f32[32,448]{1,0:T(8,128)S(1)}, u32[]{:S(2)}, u32[]{:S(2)}) collective-permute-start(f32[32,448]{1,0:T(8,128)S(1)} %get-tuple-element.70.a_ref), channel_id=1, source_target_pairs={{0,1},{1,2},{2,3},{3,0},{4,5},{5,6},{6,7},{7,4},{8,9},{9,10},{10,1... | collective-permute-start | bytes 172040 | tf_op jit(solution)/shard_map/ppermute | solution.py:390
  102.9 1.7 %collective-permute-start.23 = (f32[32,448]{1,0:T(8,128)S(1)}, f32[32,448]{1,0:T(8,128)S(1)}, u32[]{:S(2)}, u32[]{:S(2)}) collective-permute-start(f32[32,448]{1,0:T(8,128)S(1)} %get-tuple-element.70.a_ref), channel_id=1, source_target_pairs={{0,3},{1,0},{2,1},{3,2},{4,7},{5,4},{6,5},{7,6},{8,11},{9,8},{10,9... | collective-permute-start | bytes 172040 | tf_op jit(solution)/shard_map/ppermute | solution.py:390
  104.6 2.0 %collective-permute-start.24 = (f32[32,448]{1,0:T(8,128)S(1)}, f32[32,448]{1,0:T(8,128)S(1)}, u32[]{:S(2)}, u32[]{:S(2)}) collective-permute-start(f32[32,448]{1,0:T(8,128)S(1)} %get-tuple-element.70.a_ref), channel_id=1, source_target_pairs={{0,2},{1,3},{2,0},{3,1},{4,6},{5,7},{6,4},{7,5},{8,10},{9,11},{10,... | collective-permute-start | bytes 172040 | tf_op jit(solution)/shard_map/ppermute | solution.py:390
  106.5 4.8 %factor.1 = (f32[32,32]{1,0:T(8,128)S(1)}, f32[32,4096]{1,0:T(8,128)}, bf16[32,4096]{1,0:T(8,128)(2,1)S(1)}) custom-call(f32[32,32,128]{2,1,0:T(8,128)S(1)} %all-to-all-done.2.p_ref), custom_call_target="tpu_custom_call" | custom-call | tf_op jit(solution)/shard_map/factor/pallas_call | solution.py:325
  111.3 5.3 %new_error.1 = (f32[32,448]{1,0:T(8,128)}, bf16[448,4096]{1,0:T(8,128)(2,1)}) custom-call(s32[32]{0:T(128)S(1)} %fusion.at_ref, f32[32,32]{1,0:T(8,128)S(1)} %get-tuple-element.64.inv_ref, f32[32,448]{1,0:T(8,128)S(1)} %get-tuple-element.70.a_ref, f32[32,448]{1,0:T(8,128)S(1)} %collective-permute-done.22.b_ref, f32[32,448]{1,0:T(8,128)S(1)} %collective-permute-done.23.c_ref, ...), custom_call_target="tpu_custom_call" | custom-call | tf_op jit(solution)/shard_map/new_error/pallas_call | solution.py:365
  (51 shorter events, 0.4 us)
Async XLA Ops:
  0.6 8.3 %collective-permute-start = (bf16[1024,128]{1,0:T(8,128)(2,1)}, bf16[1024,128]{1,0:T(8,128)(2,1)S(1)}, u32[]{:S(2)}, u32[]{:S(2)}) collective-permute-start(bf16[1024,128]{1,0:T(8,128)(2,1)} %bitcast.28), channel_id=1, source_target_pairs={{0,4},{4,8},{8,12},{12,16},{16,20},{20,24},{24,28},{28,0},{32,36},... | collective-permute-start | bytes 786440 | tf_op jit(solution)/shard_map/ppermute | solution.py:396
  2.6 8.2 %collective-permute-start.1 = (bf16[1024,128]{1,0:T(8,128)(2,1)}, bf16[1024,128]{1,0:T(8,128)(2,1)S(1)}, u32[]{:S(2)}, u32[]{:S(2)}) collective-permute-start(bf16[1024,128]{1,0:T(8,128)(2,1)} %bitcast.29), channel_id=1, source_target_pairs={{0,28},{4,0},{8,4},{12,8},{16,12},{20,16},{24,20},{28,24},{32,60},... | collective-permute-start | bytes 786440 | tf_op jit(solution)/shard_map/ppermute | solution.py:396
  2.7 11.2 %collective-permute-start.4 = (bf16[1024,128]{1,0:T(8,128)(2,1)}, bf16[1024,128]{1,0:T(8,128)(2,1)S(1)}, u32[]{:S(2)}, u32[]{:S(2)}) collective-permute-start(bf16[1024,128]{1,0:T(8,128)(2,1)} %bitcast.30), channel_id=1, source_target_pairs={{0,64},{4,68},{8,72},{12,76},{16,80},{20,84},{24,88},{28,92},{32,9... | collective-permute-start | bytes 786440 | tf_op jit(solution)/shard_map/ppermute | solution.py:396
  5.8 25.7 %copy-start.1 = (bf16[1,1024,128]{2,1,0:T(8,128)(2,1)S(1)}, bf16[1,1024,128]{2,1,0:T(8,128)(2,1)}, u32[]{:S(2)}) copy-start(bf16[1,1024,128]{2,1,0:T(8,128)(2,1)} %param.12) | copy-start | bytes 786436
  10.8 8.1 %collective-permute-start.2 = (bf16[1024,128]{1,0:T(8,128)(2,1)S(1)}, bf16[1024,128]{1,0:T(8,128)(2,1)S(1)}, u32[]{:S(2)}, u32[]{:S(2)}) collective-permute-start(bf16[1024,128]{1,0:T(8,128)(2,1)S(1)} %collective-permute-done.refs_1_.refs_5_), channel_id=1, source_target_pairs={{0,4},{4,8},{8,12},{12,16},{16,20},{20,24},{24,28},{28,0},{32,36},... | collective-permute-start | bytes 786440 | tf_op jit(solution)/shard_map/ppermute | solution.py:396
  13.9 7.8 %collective-permute-start.3 = (bf16[1024,128]{1,0:T(8,128)(2,1)S(1)}, bf16[1024,128]{1,0:T(8,128)(2,1)S(1)}, u32[]{:S(2)}, u32[]{:S(2)}) collective-permute-start(bf16[1024,128]{1,0:T(8,128)(2,1)S(1)} %collective-permute-done.1.refs_2_.refs_6_), channel_id=1, source_target_pairs={{0,28},{4,0},{8,4},{12,8},{16,12},{20,16},{24,20},{28,24},{32,60},... | collective-permute-start | bytes 786440 | tf_op jit(solution)/shard_map/ppermute | solution.py:396
  13.9 23.4 %copy-start.2 = (bf16[1024,128]{1,0:T(8,128)(2,1)}, bf16[1024,128]{1,0:T(8,128)(2,1)S(1)}, u32[]{:S(2)}) copy-start(bf16[1024,128]{1,0:T(8,128)(2,1)S(1)} %collective-permute-done.4.refs_2_) | copy-start | bytes 786436
  21.7 7.7 %collective-permute-start.5 = (bf16[1024,128]{1,0:T(8,128)(2,1)S(1)}, bf16[1024,128]{1,0:T(8,128)(2,1)S(1)}, u32[]{:S(2)}, u32[]{:S(2)}) collective-permute-start(bf16[1024,128]{1,0:T(8,128)(2,1)S(1)} %collective-permute-done.2.refs_3_.refs_7_), channel_id=1, source_target_pairs={{0,4},{4,8},{8,12},{12,16},{16,20},{20,24},{24,28},{28,0},{32,36},... | collective-permute-start | bytes 786440 | tf_op jit(solution)/shard_map/ppermute | solution.py:396
  23.4 7.7 %collective-permute-start.6 = (bf16[1024,128]{1,0:T(8,128)(2,1)S(1)}, bf16[1024,128]{1,0:T(8,128)(2,1)S(1)}, u32[]{:S(2)}, u32[]{:S(2)}) collective-permute-start(bf16[1024,128]{1,0:T(8,128)(2,1)S(1)} %collective-permute-done.3.refs_4_.refs_8_), channel_id=1, source_target_pairs={{0,28},{4,0},{8,4},{12,8},{16,12},{20,16},{24,20},{28,24},{32,60},... | collective-permute-start | bytes 786440 | tf_op jit(solution)/shard_map/ppermute | solution.py:396
  23.7 9.0 %collective-permute-start.7 = (bf16[96,1024]{1,0:T(8,128)(2,1)S(1)}, bf16[96,1024]{1,0:T(8,128)(2,1)S(1)}, u32[]{:S(2)}, u32[]{:S(2)}) collective-permute-start(bf16[96,1024]{1,0:T(8,128)(2,1)S(1)} %get-tuple-element.45), channel_id=1, source_target_pairs={{0,32},{4,36},{8,40},{12,44},{16,48},{20,52},{24,56},{28,60},{32,6... | collective-permute-start | bytes 589832 | tf_op jit(solution)/shard_map/ppermute | solution.py:396
  25.2 8.9 %collective-permute-start.8 = (bf16[96,1024]{1,0:T(8,128)(2,1)S(1)}, bf16[96,1024]{1,0:T(8,128)(2,1)S(1)}, u32[]{:S(2)}, u32[]{:S(2)}) collective-permute-start(bf16[96,1024]{1,0:T(8,128)(2,1)S(1)} %get-tuple-element.46), channel_id=1, source_target_pairs={{0,64},{4,68},{8,72},{12,76},{16,80},{20,84},{24,88},{28,92},{32,9... | collective-permute-start | bytes 589832 | tf_op jit(solution)/shard_map/ppermute | solution.py:396
  27.9 6.2 %collective-permute-start.9 = (bf16[96,1024]{1,0:T(8,128)(2,1)S(1)}, bf16[96,1024]{1,0:T(8,128)(2,1)S(1)}, u32[]{:S(2)}, u32[]{:S(2)}) collective-permute-start(bf16[96,1024]{1,0:T(8,128)(2,1)S(1)} %get-tuple-element.47), channel_id=1, source_target_pairs={{0,96},{4,100},{8,104},{12,108},{16,112},{20,116},{24,120},{28,124... | collective-permute-start | bytes 589832 | tf_op jit(solution)/shard_map/ppermute | solution.py:396
  29.4 8.0 %collective-permute-start.10 = (bf16[1024,128]{1,0:T(8,128)(2,1)S(1)}, bf16[1024,128]{1,0:T(8,128)(2,1)}, u32[]{:S(2)}, u32[]{:S(2)}) collective-permute-start(bf16[1024,128]{1,0:T(8,128)(2,1)S(1)} %collective-permute-done.4.refs_2_), channel_id=1, source_target_pairs={{0,4},{4,8},{8,12},{12,16},{16,20},{20,24},{24,28},{28,0},{32,36},... | collective-permute-start | bytes 786440 | tf_op jit(solution)/shard_map/ppermute | solution.py:396
  31.1 6.5 %collective-permute-start.11 = (bf16[1024,128]{1,0:T(8,128)(2,1)S(1)}, bf16[1024,128]{1,0:T(8,128)(2,1)}, u32[]{:S(2)}, u32[]{:S(2)}) collective-permute-start(bf16[1024,128]{1,0:T(8,128)(2,1)S(1)} %collective-permute-done.4.refs_2_), channel_id=1, source_target_pairs={{0,28},{4,0},{8,4},{12,8},{16,12},{20,16},{24,20},{28,24},{32,60},... | collective-permute-start | bytes 786440 | tf_op jit(solution)/shard_map/ppermute | solution.py:396
  32.7 21.1 %copy-start.12 = (s32[4]{0:T(128)S(1)}, s32[4]{0:T(128)}, u32[]{:S(2)}) copy-start(s32[4]{0:T(128)} %constant.145.clone) | copy-start | bytes 52
  34.1 51.0 %collective-permute-start.18 = (bf16[7168,128]{1,0:T(8,128)(2,1)}, bf16[7168,128]{1,0:T(8,128)(2,1)}, u32[]{:S(2)}, u32[]{:S(2)}) collective-permute-start(bf16[7168,128]{1,0:T(8,128)(2,1)} %pack.1.refs_0_), channel_id=1, source_target_pairs={{0,32},{4,36},{8,40},{12,44},{16,48},{20,52},{24,56},{28,60},{32,6... | collective-permute-start | bytes 5505032 | tf_op jit(solution)/shard_map/ppermute | solution.py:396
  35.9 49.2 %collective-permute-start.19 = (bf16[7168,128]{1,0:T(8,128)(2,1)}, bf16[7168,128]{1,0:T(8,128)(2,1)}, u32[]{:S(2)}, u32[]{:S(2)}) collective-permute-start(bf16[7168,128]{1,0:T(8,128)(2,1)} %pack.1.refs_0_), channel_id=1, source_target_pairs={{0,96},{4,100},{8,104},{12,108},{16,112},{20,116},{24,120},{28,124... | collective-permute-start | bytes 5505032 | tf_op jit(solution)/shard_map/ppermute | solution.py:396
  37.6 7.2 %collective-permute-start.12 = (bf16[1024,128]{1,0:T(8,128)(2,1)S(1)}, bf16[1024,128]{1,0:T(8,128)(2,1)S(1)}, u32[]{:S(2)}, u32[]{:S(2)}) collective-permute-start(bf16[1024,128]{1,0:T(8,128)(2,1)S(1)} %collective-permute-done.5.refs_5_.refs_9_), channel_id=1, source_target_pairs={{0,4},{4,8},{8,12},{12,16},{16,20},{20,24},{24,28},{28,0},{32,36},... | collective-permute-start | bytes 786440 | tf_op jit(solution)/shard_map/ppermute | solution.py:396
  39.4 17.7 %collective-permute-start.13 = (bf16[1024,128]{1,0:T(8,128)(2,1)}, bf16[1024,128]{1,0:T(8,128)(2,1)}, u32[]{:S(2)}, u32[]{:S(2)}) collective-permute-start(bf16[1024,128]{1,0:T(8,128)(2,1)} %collective-permute-done.10.refs_3_), channel_id=1, source_target_pairs={{0,4},{4,8},{8,12},{12,16},{16,20},{20,24},{24,28},{28,0},{32,36},... | collective-permute-start | bytes 786440 | tf_op jit(solution)/shard_map/ppermute | solution.py:396
  42.1 15.0 %collective-permute-start.14 = (bf16[1024,128]{1,0:T(8,128)(2,1)}, bf16[1024,128]{1,0:T(8,128)(2,1)}, u32[]{:S(2)}, u32[]{:S(2)}) collective-permute-start(bf16[1024,128]{1,0:T(8,128)(2,1)} %collective-permute-done.11.refs_4_), channel_id=1, source_target_pairs={{0,28},{4,0},{8,4},{12,8},{16,12},{20,16},{24,20},{28,24},{32,60},... | collective-permute-start | bytes 786440 | tf_op jit(solution)/shard_map/ppermute | solution.py:396
  44.8 22.5 %copy-start = (bf16[1024,128]{1,0:T(8,128)(2,1)}, bf16[1024,128]{1,0:T(8,128)(2,1)S(1)}, u32[]{:S(2)}) copy-start(bf16[1024,128]{1,0:T(8,128)(2,1)S(1)} %collective-permute-done.12.refs_0_.refs_1_) | copy-start | bytes 786436
  46.2 16.0 %all-to-all-start = ((f32[8,32,128]{2,1,0:T(8,128)}), f32[8,32,128]{2,1,0:T(8,128)S(1)}, u32[]{:S(2)}, u32[]{:S(2)}) async-start(f32[8,32,128]{2,1,0:T(8,128)} %p_column_rest.1), calls=%async_computation | async-start | bytes 262144 | tf_op jit(solution)/shard_map/all_to_all | solution.py:385
  53.8 13.5 %copy-start.11 = (s32[4]{0:T(128)S(1)}, s32[4]{0:T(128)}, u32[]{:S(2)}) copy-start(s32[4]{0:T(128)} %constant.146.clone) | copy-start | bytes 52
  57.1 16.7 %collective-permute-start.15 = (bf16[1024,128]{1,0:T(8,128)(2,1)}, bf16[1024,128]{1,0:T(8,128)(2,1)S(1)}, u32[]{:S(2)}, u32[]{:S(2)}) collective-permute-start(bf16[1024,128]{1,0:T(8,128)(2,1)} %collective-permute-done.13.refs_5_), channel_id=1, source_target_pairs={{0,4},{4,8},{8,12},{12,16},{16,20},{20,24},{24,28},{28,0},{32,36},... | collective-permute-start | bytes 786440 | tf_op jit(solution)/shard_map/ppermute | solution.py:396
  58.6 15.2 %collective-permute-start.16 = (bf16[1024,128]{1,0:T(8,128)(2,1)}, bf16[1024,128]{1,0:T(8,128)(2,1)S(1)}, u32[]{:S(2)}, u32[]{:S(2)}) collective-permute-start(bf16[1024,128]{1,0:T(8,128)(2,1)} %collective-permute-done.14.refs_7_), channel_id=1, source_target_pairs={{0,28},{4,0},{8,4},{12,8},{16,12},{20,16},{24,20},{28,24},{32,60},... | collective-permute-start | bytes 786440 | tf_op jit(solution)/shard_map/ppermute | solution.py:396
  59.2 14.6 %collective-permute-start.17 = (bf16[1024,128]{1,0:T(8,128)(2,1)}, bf16[1024,128]{1,0:T(8,128)(2,1)S(1)}, u32[]{:S(2)}, u32[]{:S(2)}) collective-permute-start(bf16[1024,128]{1,0:T(8,128)(2,1)} %collective-permute-done.14.refs_7_), channel_id=1, source_target_pairs={{0,24},{4,28},{8,0},{12,4},{16,8},{20,12},{24,16},{28,20},{32,56},... | collective-permute-start | bytes 786440 | tf_op jit(solution)/shard_map/ppermute | solution.py:396
  62.8 10.1 %all-to-all-start.1 = ((f32[4,32,128]{2,1,0:T(8,128)}), f32[4,32,128]{2,1,0:T(8,128)S(1)}, u32[]{:S(2)}, u32[]{:S(2)}) async-start(f32[4,32,128]{2,1,0:T(8,128)} %add_spread.2), calls=%async_computation.1 | async-start | bytes 131072 | tf_op jit(solution)/shard_map/all_to_all | solution.py:385
  67.3 17.7 %copy-start.9 = (s32[32]{0:T(128)S(1)}, s32[32]{0:T(128)}, u32[]{:S(2)}) copy-start(s32[32]{0:T(128)} %constant.147.clone) | copy-start | bytes 388
  67.3 17.7 %copy-start.10 = (s32[32]{0:T(128)S(1)}, s32[32]{0:T(128)}, u32[]{:S(2)}) copy-start(s32[32]{0:T(128)} %constant.148.clone) | copy-start | bytes 388
  67.3 17.7 %copy-start.7 = (s32[18]{0:T(128)S(1)}, s32[18]{0:T(128)}, u32[]{:S(2)}) copy-start(s32[18]{0:T(128)} %constant.149.clone) | copy-start | bytes 220
  67.4 17.7 %copy-start.8 = (s32[18]{0:T(128)S(1)}, s32[18]{0:T(128)}, u32[]{:S(2)}) copy-start(s32[18]{0:T(128)} %constant.150.clone) | copy-start | bytes 220
  73.8 11.3 %copy-start.3 = (bf16[1024,128]{1,0:T(8,128)(2,1)}, bf16[1024,128]{1,0:T(8,128)(2,1)S(1)}, u32[]{:S(2)}) copy-start(bf16[1024,128]{1,0:T(8,128)(2,1)S(1)} %collective-permute-done.15.refs_8_) | copy-start | bytes 786436
  73.8 11.3 %copy-start.4 = (bf16[1024,128]{1,0:T(8,128)(2,1)}, bf16[1024,128]{1,0:T(8,128)(2,1)S(1)}, u32[]{:S(2)}) copy-start(bf16[1024,128]{1,0:T(8,128)(2,1)S(1)} %collective-permute-done.16.refs_9_) | copy-start | bytes 786436
  73.8 11.3 %copy-start.5 = (bf16[1024,128]{1,0:T(8,128)(2,1)}, bf16[1024,128]{1,0:T(8,128)(2,1)S(1)}, u32[]{:S(2)}) copy-start(bf16[1024,128]{1,0:T(8,128)(2,1)S(1)} %collective-permute-done.17.refs_10_) | copy-start | bytes 786436
  73.8 21.8 %all-to-all-start.2 = ((f32[32,32,128]{2,1,0:T(8,128)}), f32[32,32,128]{2,1,0:T(8,128)S(1)}, u32[]{:S(2)}, u32[]{:S(2)}) async-start(f32[32,32,128]{2,1,0:T(8,128)} %add_spread.3), calls=%async_computation.2 | async-start | bytes 1048576 | tf_op jit(solution)/shard_map/all_to_all | solution.py:385
  81.7 11.1 %collective-permute-start.20 = (bf16[1024,128]{1,0:T(8,128)(2,1)}, bf16[1024,128]{1,0:T(8,128)(2,1)S(1)}, u32[]{:S(2)}, u32[]{:S(2)}) collective-permute-start(bf16[1024,128]{1,0:T(8,128)(2,1)} %copy-done), channel_id=1, source_target_pairs={{0,32},{4,36},{8,40},{12,44},{16,48},{20,52},{24,56},{28,60},{32,6... | collective-permute-start | bytes 786440 | tf_op jit(solution)/shard_map/ppermute | solution.py:396
  83.2 10.3 %collective-permute-start.21 = (bf16[1024,128]{1,0:T(8,128)(2,1)}, bf16[1024,128]{1,0:T(8,128)(2,1)}, u32[]{:S(2)}, u32[]{:S(2)}) collective-permute-start(bf16[1024,128]{1,0:T(8,128)(2,1)} %copy-done), channel_id=1, source_target_pairs={{0,96},{4,100},{8,104},{12,108},{16,112},{20,116},{24,120},{28,124... | collective-permute-start | bytes 786440 | tf_op jit(solution)/shard_map/ppermute | solution.py:396
  92.8 0.7 copy-start.6
  101.2 10.1 %collective-permute-start.22 = (f32[32,448]{1,0:T(8,128)S(1)}, f32[32,448]{1,0:T(8,128)S(1)}, u32[]{:S(2)}, u32[]{:S(2)}) collective-permute-start(f32[32,448]{1,0:T(8,128)S(1)} %get-tuple-element.70.a_ref), channel_id=1, source_target_pairs={{0,1},{1,2},{2,3},{3,0},{4,5},{5,6},{6,7},{7,4},{8,9},{9,10},{10,1... | collective-permute-start | bytes 172040 | tf_op jit(solution)/shard_map/ppermute | solution.py:390
  102.9 8.5 %collective-permute-start.23 = (f32[32,448]{1,0:T(8,128)S(1)}, f32[32,448]{1,0:T(8,128)S(1)}, u32[]{:S(2)}, u32[]{:S(2)}) collective-permute-start(f32[32,448]{1,0:T(8,128)S(1)} %get-tuple-element.70.a_ref), channel_id=1, source_target_pairs={{0,3},{1,0},{2,1},{3,2},{4,7},{5,4},{6,5},{7,6},{8,11},{9,8},{10,9... | collective-permute-start | bytes 172040 | tf_op jit(solution)/shard_map/ppermute | solution.py:390
  104.6 6.8 %collective-permute-start.24 = (f32[32,448]{1,0:T(8,128)S(1)}, f32[32,448]{1,0:T(8,128)S(1)}, u32[]{:S(2)}, u32[]{:S(2)}) collective-permute-start(f32[32,448]{1,0:T(8,128)S(1)} %get-tuple-element.70.a_ref), channel_id=1, source_target_pairs={{0,2},{1,3},{2,0},{3,1},{4,6},{5,7},{6,4},{7,5},{8,10},{9,11},{10,... | collective-permute-start | bytes 172040 | tf_op jit(solution)/shard_map/ppermute | solution.py:390

commit v5 on v4

--- a/solution.py
+++ b/solution.py
@@ -306,13 +306,18 @@
     col = lax.broadcasted_iota(jnp.int32, (32, 128), 1)
     work = jnp.concatenate([gram, jnp.zeros((32, 96), F32)], axis=1)
     work = jnp.where(col == row + 32, 1.0, work)
-    scale = jnp.zeros((32, 1), F32)
-    for j in range(32):
-        pivot = work[j : j + 1, j : j + 1]
-        below = jnp.where(row[:, :1] > j, work[:, j : j + 1], 0.0)
-        scale = jnp.where(row[:, :1] == j, pivot, scale)
-        work = work - below * (work[j : j + 1, :] / pivot)
-    inverse = work[:, 32:64] / jnp.sqrt(scale)
+    scale = jnp.zeros((32, 128), F32)
+    for start in range(0, 32, 8):
+        block = range(start, start + 8)
+        columns = {j: jnp.broadcast_to(work[:, j : j + 1], (32, 128)) for j in block}
+        for j in block:
+            pivot = columns[j][j : j + 1, :]
+            scale = jnp.where(row == j, pivot, scale)
+            below = jnp.where(row > j, columns[j], 0.0) * (1.0 / pivot)
+            work = work - below * work[j : j + 1, :]
+            for k in range(j + 1, start + 8):
+                columns[k] = columns[k] - below * columns[k][j : j + 1, :]
+    inverse = (work / jnp.sqrt(scale))[:, 32:64]
     inv_ref[...] = inverse
     terms = split3(inverse)
     terms = jnp.concatenate([terms, terms, terms], axis=1)

time: 117 us -> 116 us (level)
  Pallas kernels: 39.1 us -> 37.2 us
    pallas_call x1, Pallas kernels: 4.8 us -> 2.83 us  [factor(): pl.pallas_call(factor_kernel, in_specs=[VMEM], out_specs=[VMEM] * 3, out_...]
  transfers between devices with their start and end apart: 28 -> 28, of which waited for: 10 -> 11; matrix products, arithmetic and copies ran while one was open for 0% -> 0% of each run, Pallas kernels for 24% -> 23%
where the time goes in v5:
time: 116 us
  starting transfers between devices  59 us (51%)
  Pallas kernels  37.2 us (32%)
  waiting for transfers between devices  17.6 us (15%)
    ppermute x22, starting transfers between devices, move(): return lax.ppermute(v, 'hidden', pairs)  33.8 us
    all_to_all x3, starting transfers between devices, swap(): return lax.all_to_all(v, axis, 0, 0, axis_index_groups=groups)  19.9 us
    pallas_call x3, Pallas kernels, correct(): pl.pallas_call(functools.partial(correct_kernel, parts_of), in_specs=[SME...  14.2 us
    ppermute x22, waiting for transfers between devices, move(): return lax.ppermute(v, 'hidden', pairs)  12 us
    pallas_call x1, Pallas kernels, finish(): pl.pallas_call(functools.partial(finish_kernel, len(kept)), in_specs=[SME...  5.57 us
    pallas_call x1, Pallas kernels, final(): pl.pallas_call(final_kernel, in_specs=[SMEM] + [VMEM] * (6 + len(kept)) +...  5.31 us
    ppermute x3, starting transfers between devices, replicas(): lax.ppermute(v, 'replica', [(i, (i + s) % 4) for i in range(4)])  5.3 us
    all_to_all x3, waiting for transfers between devices, swap(): return lax.all_to_all(v, axis, 0, 0, axis_index_groups=groups)  4.73 us
  transfers between devices with their start and end apart: 28, of which 11 were waited for; matrix products, arithmetic and copies ran while one was open for 0% of the time, Pallas kernels for 23%

profile of v5, /device:TPU:32, one launch (start us, length us, event | category | flops | bytes accessed | tf_op | source)
XLA Modules:
  0.0 115.8 jit_solution(9119216480122402145)
XLA Ops:
  0.6 2.0 %collective-permute-start = (bf16[1024,128]{1,0:T(8,128)(2,1)}, bf16[1024,128]{1,0:T(8,128)(2,1)S(1)}, u32[]{:S(2)}, u32[]{:S(2)}) collective-permute-start(bf16[1024,128]{1,0:T(8,128)(2,1)} %bitcast.28), channel_id=1, source_target_pairs={{0,4},{4,8},{8,12},{12,16},{16,20},{20,24},{24,28},{28,0},{32,36},... | collective-permute-start | bytes 786440 | tf_op jit(solution)/shard_map/ppermute | solution.py:401
  2.7 3.0 %collective-permute-start.4 = (bf16[1024,128]{1,0:T(8,128)(2,1)}, bf16[1024,128]{1,0:T(8,128)(2,1)S(1)}, u32[]{:S(2)}, u32[]{:S(2)}) collective-permute-start(bf16[1024,128]{1,0:T(8,128)(2,1)} %bitcast.30), channel_id=1, source_target_pairs={{0,64},{4,68},{8,72},{12,76},{16,80},{20,84},{24,88},{28,92},{32,9... | collective-permute-start | bytes 786440 | tf_op jit(solution)/shard_map/ppermute | solution.py:401
  5.8 2.7 %eq_hq.1 = (bf16[96,1024]{1,0:T(8,128)(2,1)S(1)}, bf16[96,1024]{1,0:T(8,128)(2,1)S(1)}, bf16[96,1024]{1,0:T(8,128)(2,1)S(1)}, bf16[96,1024]{1,0:T(8,128)(2,1)S(1)}) custom-call(s32[1]{0:T(128)} %bitcast.9.x_ref, f32[32,448]{1,0:T(8,128)} %bitcast.43, bf16[448,4096]{1,0:T(8,128)(2,1)} %bitcast.33, bf16[448,1024]{1,0:T(8,128)(2,1)} %bitcast.38), custom_call_target="tpu_custom_call" | custom-call | tf_op jit(solution)/shard_map/eq_hq/pallas_call | solution.py:78
  8.5 0.5 collective-permute-done.refs_1_.refs_5_
  9.0 1.8 %collective-permute-done.1.refs_2_.refs_6_ = bf16[1024,128]{1,0:T(8,128)(2,1)S(1)} collective-permute-done((bf16[1024,128]{1,0:T(8,128)(2,1)}, bf16[1024,128]{1,0:T(8,128)(2,1)S(1)}, u32[]{:S(2)}, u32[]{:S(2)}) %collective-permute-start.1) | collective-permute-done | bytes 262176 | tf_op jit(solution)/shard_map/ppermute | solution.py:401
  10.8 3.1 %collective-permute-start.2 = (bf16[1024,128]{1,0:T(8,128)(2,1)S(1)}, bf16[1024,128]{1,0:T(8,128)(2,1)S(1)}, u32[]{:S(2)}, u32[]{:S(2)}) collective-permute-start(bf16[1024,128]{1,0:T(8,128)(2,1)S(1)} %collective-permute-done.refs_1_.refs_5_), channel_id=1, source_target_pairs={{0,4},{4,8},{8,12},{12,16},{16,20},{20,24},{24,28},{28,0},{32,36},... | collective-permute-start | bytes 786440 | tf_op jit(solution)/shard_map/ppermute | solution.py:401
  13.9 5.0 %collective-permute-done.2.refs_3_.refs_7_ = bf16[1024,128]{1,0:T(8,128)(2,1)S(1)} collective-permute-done((bf16[1024,128]{1,0:T(8,128)(2,1)S(1)}, bf16[1024,128]{1,0:T(8,128)(2,1)S(1)}, u32[]{:S(2)}, u32[]{:S(2)}) %collective-permute-start.2) | collective-permute-done | bytes 262176 | tf_op jit(solution)/shard_map/ppermute | solution.py:401
  18.9 2.8 %collective-permute-done.3.refs_4_.refs_8_ = bf16[1024,128]{1,0:T(8,128)(2,1)S(1)} collective-permute-done((bf16[1024,128]{1,0:T(8,128)(2,1)S(1)}, bf16[1024,128]{1,0:T(8,128)(2,1)S(1)}, u32[]{:S(2)}, u32[]{:S(2)}) %collective-permute-start.3) | collective-permute-done | bytes 262176 | tf_op jit(solution)/shard_map/ppermute | solution.py:401
  21.7 1.7 %collective-permute-start.5 = (bf16[1024,128]{1,0:T(8,128)(2,1)S(1)}, bf16[1024,128]{1,0:T(8,128)(2,1)S(1)}, u32[]{:S(2)}, u32[]{:S(2)}) collective-permute-start(bf16[1024,128]{1,0:T(8,128)(2,1)S(1)} %collective-permute-done.2.refs_3_.refs_7_), channel_id=1, source_target_pairs={{0,4},{4,8},{8,12},{12,16},{16,20},{20,24},{24,28},{28,0},{32,36},... | collective-permute-start | bytes 786440 | tf_op jit(solution)/shard_map/ppermute | solution.py:401
  23.4 0.3 collective-permute-start.6
  23.7 1.5 %collective-permute-start.7 = (bf16[96,1024]{1,0:T(8,128)(2,1)S(1)}, bf16[96,1024]{1,0:T(8,128)(2,1)S(1)}, u32[]{:S(2)}, u32[]{:S(2)}) collective-permute-start(bf16[96,1024]{1,0:T(8,128)(2,1)S(1)} %get-tuple-element.45), channel_id=1, source_target_pairs={{0,32},{4,36},{8,40},{12,44},{16,48},{20,52},{24,56},{28,60},{32,6... | collective-permute-start | bytes 589832 | tf_op jit(solution)/shard_map/ppermute | solution.py:401
  25.2 2.7 %collective-permute-start.8 = (bf16[96,1024]{1,0:T(8,128)(2,1)S(1)}, bf16[96,1024]{1,0:T(8,128)(2,1)S(1)}, u32[]{:S(2)}, u32[]{:S(2)}) collective-permute-start(bf16[96,1024]{1,0:T(8,128)(2,1)S(1)} %get-tuple-element.46), channel_id=1, source_target_pairs={{0,64},{4,68},{8,72},{12,76},{16,80},{20,84},{24,88},{28,92},{32,9... | collective-permute-start | bytes 589832 | tf_op jit(solution)/shard_map/ppermute | solution.py:401
  27.9 1.4 %collective-permute-start.9 = (bf16[96,1024]{1,0:T(8,128)(2,1)S(1)}, bf16[96,1024]{1,0:T(8,128)(2,1)S(1)}, u32[]{:S(2)}, u32[]{:S(2)}) collective-permute-start(bf16[96,1024]{1,0:T(8,128)(2,1)S(1)} %get-tuple-element.47), channel_id=1, source_target_pairs={{0,96},{4,100},{8,104},{12,108},{16,112},{20,116},{24,120},{28,124... | collective-permute-start | bytes 589832 | tf_op jit(solution)/shard_map/ppermute | solution.py:401
  29.4 1.7 %collective-permute-start.10 = (bf16[1024,128]{1,0:T(8,128)(2,1)S(1)}, bf16[1024,128]{1,0:T(8,128)(2,1)}, u32[]{:S(2)}, u32[]{:S(2)}) collective-permute-start(bf16[1024,128]{1,0:T(8,128)(2,1)S(1)} %collective-permute-done.4.refs_2_), channel_id=1, source_target_pairs={{0,4},{4,8},{8,12},{12,16},{16,20},{20,24},{24,28},{28,0},{32,36},... | collective-permute-start | bytes 786440 | tf_op jit(solution)/shard_map/ppermute | solution.py:401
  31.1 0.3 collective-permute-start.11
  31.4 1.3 %pack.1.refs_0_ = bf16[7168,128]{1,0:T(8,128)(2,1)} custom-call(bf16[1024,128]{1,0:T(8,128)(2,1)S(1)} %bitcast.31, bf16[1024,128]{1,0:T(8,128)(2,1)S(1)} %collective-permute-done.refs_1_.refs_5_, bf16[1024,128]{1,0:T(8,128)(2,1)S(1)} %collective-permute-done.1.refs_2_.refs_6_, bf16[1024,128]{1,0:T(8,128)(2,1)S(1)} %collective-permute-done.2.refs_3_.refs_7_, ...), custom_call_target="tpu_custom_call" | custom-call | tf_op jit(solution)/shard_map/pack/pallas_call | solution.py:189
  32.7 1.4 %collective-permute-done.8.refs_2_ = bf16[96,1024]{1,0:T(8,128)(2,1)S(1)} collective-permute-done((bf16[96,1024]{1,0:T(8,128)(2,1)S(1)}, bf16[96,1024]{1,0:T(8,128)(2,1)S(1)}, u32[]{:S(2)}, u32[]{:S(2)}) %collective-permute-start.8) | collective-permute-done | bytes 196640 | tf_op jit(solution)/shard_map/ppermute | solution.py:401
  34.1 1.8 %collective-permute-start.18 = (bf16[7168,128]{1,0:T(8,128)(2,1)}, bf16[7168,128]{1,0:T(8,128)(2,1)}, u32[]{:S(2)}, u32[]{:S(2)}) collective-permute-start(bf16[7168,128]{1,0:T(8,128)(2,1)} %pack.1.refs_0_), channel_id=1, source_target_pairs={{0,32},{4,36},{8,40},{12,44},{16,48},{20,52},{24,56},{28,60},{32,6... | collective-permute-start | bytes 5505032 | tf_op jit(solution)/shard_map/ppermute | solution.py:401
  35.9 1.5 %collective-permute-start.19 = (bf16[7168,128]{1,0:T(8,128)(2,1)}, bf16[7168,128]{1,0:T(8,128)(2,1)}, u32[]{:S(2)}, u32[]{:S(2)}) collective-permute-start(bf16[7168,128]{1,0:T(8,128)(2,1)} %pack.1.refs_0_), channel_id=1, source_target_pairs={{0,96},{4,100},{8,104},{12,108},{16,112},{20,116},{24,120},{28,124... | collective-permute-start | bytes 5505032 | tf_op jit(solution)/shard_map/ppermute | solution.py:401
  37.3 0.3 collective-permute-done.11.refs_4_
  37.6 1.8 %collective-permute-start.12 = (bf16[1024,128]{1,0:T(8,128)(2,1)S(1)}, bf16[1024,128]{1,0:T(8,128)(2,1)S(1)}, u32[]{:S(2)}, u32[]{:S(2)}) collective-permute-start(bf16[1024,128]{1,0:T(8,128)(2,1)S(1)} %collective-permute-done.5.refs_5_.refs_9_), channel_id=1, source_target_pairs={{0,4},{4,8},{8,12},{12,16},{16,20},{20,24},{24,28},{28,0},{32,36},... | collective-permute-start | bytes 786440 | tf_op jit(solution)/shard_map/ppermute | solution.py:401
  39.4 2.7 %collective-permute-start.13 = (bf16[1024,128]{1,0:T(8,128)(2,1)}, bf16[1024,128]{1,0:T(8,128)(2,1)}, u32[]{:S(2)}, u32[]{:S(2)}) collective-permute-start(bf16[1024,128]{1,0:T(8,128)(2,1)} %collective-permute-done.10.refs_3_), channel_id=1, source_target_pairs={{0,4},{4,8},{8,12},{12,16},{16,20},{20,24},{24,28},{28,0},{32,36},... | collective-permute-start | bytes 786440 | tf_op jit(solution)/shard_map/ppermute | solution.py:401
  42.2 2.4 %p_column.1 = (f32[8,32,128]{2,1,0:T(8,128)S(1)}, bf16[96,1024]{1,0:T(8,128)(2,1)S(1)}) custom-call(s32[8]{0:T(128)S(1)} %stack.35.z_ref, bf16[96,1024]{1,0:T(8,128)(2,1)S(1)} %get-tuple-element.40.refs_0_, bf16[96,1024]{1,0:T(8,128)(2,1)S(1)} %collective-permute-done.7.refs_1_, bf16[96,1024]{1,0:T(8,128)(2,1)S(1)} %collective-permute-done.8.refs_2_, ...), custom_call_target="tpu_custom_call" | custom-call | tf_op jit(solution)/shard_map/p_column/pallas_call | solution.py:124
  44.8 1.4 %p_column_rest.1 = f32[8,32,128]{2,1,0:T(8,128)} custom-call(s32[8]{0:T(128)S(1)} %stack.35.z_ref, f32[8,32,128]{2,1,0:T(8,128)S(1)} %get-tuple-element.53.part_ref, bf16[96,1024]{1,0:T(8,128)(2,1)S(1)} %get-tuple-element.54.t_ref, bf16[1024,128]{1,0:T(8,128)(2,1)S(1)} %collective-permute-done.12.refs_0_.refs_1_), custom_call_target="tpu_custom_call" | custom-call | tf_op jit(solution)/shard_map/p_column_rest/pallas_call | solution.py:154
  46.2 7.6 %all-to-all-start = ((f32[8,32,128]{2,1,0:T(8,128)}), f32[8,32,128]{2,1,0:T(8,128)S(1)}, u32[]{:S(2)}, u32[]{:S(2)}) async-start(f32[8,32,128]{2,1,0:T(8,128)} %p_column_rest.1), calls=%async_computation | async-start | bytes 262144 | tf_op jit(solution)/shard_map/all_to_all | solution.py:390
  53.8 3.2 %corrected.3.refs_0_ = bf16[4,448,128]{2,1,0:T(8,128)(2,1)S(1)} custom-call(s32[4]{0:T(128)S(1)} %fusion.3.at_ref, bf16[448,1024]{1,0:T(8,128)(2,1)} %bitcast.39, bf16[448,4096]{1,0:T(8,128)(2,1)} %bitcast.34, bf16[7168,128]{1,0:T(8,128)(2,1)} %pack.1.refs_0_), custom_call_target="tpu_custom_call" | custom-call | tf_op jit(solution)/shard_map/corrected/pallas_call | solution.py:241
  57.1 1.5 %collective-permute-start.15 = (bf16[1024,128]{1,0:T(8,128)(2,1)}, bf16[1024,128]{1,0:T(8,128)(2,1)S(1)}, u32[]{:S(2)}, u32[]{:S(2)}) collective-permute-start(bf16[1024,128]{1,0:T(8,128)(2,1)} %collective-permute-done.13.refs_5_), channel_id=1, source_target_pairs={{0,4},{4,8},{8,12},{12,16},{16,20},{20,24},{24,28},{28,0},{32,36},... | collective-permute-start | bytes 786440 | tf_op jit(solution)/shard_map/ppermute | solution.py:401
  58.6 0.6 collective-permute-start.16
  59.2 2.7 %collective-permute-start.17 = (bf16[1024,128]{1,0:T(8,128)(2,1)}, bf16[1024,128]{1,0:T(8,128)(2,1)S(1)}, u32[]{:S(2)}, u32[]{:S(2)}) collective-permute-start(bf16[1024,128]{1,0:T(8,128)(2,1)} %collective-permute-done.14.refs_7_), channel_id=1, source_target_pairs={{0,24},{4,28},{8,0},{12,4},{16,8},{20,12},{24,16},{28,20},{32,56},... | collective-permute-start | bytes 786440 | tf_op jit(solution)/shard_map/ppermute | solution.py:401
  61.9 0.3 all-to-all-done.in_ref
  62.2 0.6 add_spread.2
  62.8 4.5 %all-to-all-start.1 = ((f32[4,32,128]{2,1,0:T(8,128)}), f32[4,32,128]{2,1,0:T(8,128)S(1)}, u32[]{:S(2)}, u32[]{:S(2)}) async-start(f32[4,32,128]{2,1,0:T(8,128)} %add_spread.2), calls=%async_computation.1 | async-start | bytes 131072 | tf_op jit(solution)/shard_map/all_to_all | solution.py:390
  67.4 3.2 %corrected.4.refs_1_ = bf16[4,448,128]{2,1,0:T(8,128)(2,1)S(1)} custom-call(s32[4]{0:T(128)S(1)} %fusion.5.at_ref, bf16[448,1024]{1,0:T(8,128)(2,1)} %bitcast.40, bf16[448,4096]{1,0:T(8,128)(2,1)} %bitcast.35, bf16[7168,128]{1,0:T(8,128)(2,1)} %pack.1.refs_0_, bf16[1024,128]{1,0:T(8,128)(2,1)} %copy-done), custom_call_target="tpu_custom_call" | custom-call | tf_op jit(solution)/shard_map/corrected/pallas_call | solution.py:241
  70.6 2.3 %all-to-all-done.1.in_ref = f32[4,32,128]{2,1,0:T(8,128)S(1)} async-done(((f32[4,32,128]{2,1,0:T(8,128)}), f32[4,32,128]{2,1,0:T(8,128)S(1)}, u32[]{:S(2)}, u32[]{:S(2)}) %all-to-all-start.1) | async-done | bytes 65568 | tf_op jit(solution)/shard_map/all_to_all | solution.py:390
  72.9 0.9 add_spread.3
  73.8 7.9 %all-to-all-start.2 = ((f32[32,32,128]{2,1,0:T(8,128)}), f32[32,32,128]{2,1,0:T(8,128)S(1)}, u32[]{:S(2)}, u32[]{:S(2)}) async-start(f32[32,32,128]{2,1,0:T(8,128)} %add_spread.3), calls=%async_computation.2 | async-start | bytes 1048576 | tf_op jit(solution)/shard_map/all_to_all | solution.py:390
  81.7 1.5 %collective-permute-start.20 = (bf16[1024,128]{1,0:T(8,128)(2,1)}, bf16[1024,128]{1,0:T(8,128)(2,1)S(1)}, u32[]{:S(2)}, u32[]{:S(2)}) collective-permute-start(bf16[1024,128]{1,0:T(8,128)(2,1)} %copy-done), channel_id=1, source_target_pairs={{0,32},{4,36},{8,40},{12,44},{16,48},{20,52},{24,56},{28,60},{32,6... | collective-permute-start | bytes 786440 | tf_op jit(solution)/shard_map/ppermute | solution.py:401
  83.2 1.8 %collective-permute-start.21 = (bf16[1024,128]{1,0:T(8,128)(2,1)}, bf16[1024,128]{1,0:T(8,128)(2,1)}, u32[]{:S(2)}, u32[]{:S(2)}) collective-permute-start(bf16[1024,128]{1,0:T(8,128)(2,1)} %copy-done), channel_id=1, source_target_pairs={{0,96},{4,100},{8,104},{12,108},{16,112},{20,116},{24,120},{28,124... | collective-permute-start | bytes 786440 | tf_op jit(solution)/shard_map/ppermute | solution.py:401
  85.1 7.7 %corrected.5.refs_2_ = bf16[18,448,128]{2,1,0:T(8,128)(2,1)S(1)} custom-call(s32[18]{0:T(128)S(1)} %fusion.1.at_ref, bf16[448,1024]{1,0:T(8,128)(2,1)} %bitcast.41, bf16[448,4096]{1,0:T(8,128)(2,1)} %bitcast.36, bf16[7168,128]{1,0:T(8,128)(2,1)} %collective-permute-done.18.refs_0_, bf16[7168,128]{1,0:T(8,128)(2,1)} %collective-permute-done.19.refs_1_, ...), custom_call_target="tpu_custom_call" | custom-call | tf_op jit(solution)/shard_map/corrected/pallas_call | solution.py:241
  92.8 0.7 copy-done.6
  93.5 2.1 %all-to-all-done.2.p_ref = f32[32,32,128]{2,1,0:T(8,128)S(1)} async-done(((f32[32,32,128]{2,1,0:T(8,128)}), f32[32,32,128]{2,1,0:T(8,128)S(1)}, u32[]{:S(2)}, u32[]{:S(2)}) %all-to-all-start.2) | async-done | bytes 524320 | tf_op jit(solution)/shard_map/all_to_all | solution.py:390
  95.7 5.6 %c_p.1 = (f32[32,448]{1,0:T(8,128)S(1)}, bf16[6,448,128]{2,1,0:T(8,128)(2,1)}) custom-call(s32[32]{0:T(128)S(1)} %fusion.at_ref, f32[32,32,128]{2,1,0:T(8,128)S(1)} %all-to-all-done.2.p_ref, bf16[4,448,128]{2,1,0:T(8,128)(2,1)S(1)} %corrected.3.refs_0_, bf16[4,448,128]{2,1,0:T(8,128)(2,1)S(1)} %corrected.4.refs_1_, ...), custom_call_target="tpu_custom_call" | custom-call | tf_op jit(solution)/shard_map/c_p/pallas_call | solution.py:283
  101.2 1.7 %collective-permute-start.22 = (f32[32,448]{1,0:T(8,128)S(1)}, f32[32,448]{1,0:T(8,128)S(1)}, u32[]{:S(2)}, u32[]{:S(2)}) collective-permute-start(f32[32,448]{1,0:T(8,128)S(1)} %get-tuple-element.70.a_ref), channel_id=1, source_target_pairs={{0,1},{1,2},{2,3},{3,0},{4,5},{5,6},{6,7},{7,4},{8,9},{9,10},{10,1... | collective-permute-start | bytes 172040 | tf_op jit(solution)/shard_map/ppermute | solution.py:395
  102.9 1.7 %collective-permute-start.23 = (f32[32,448]{1,0:T(8,128)S(1)}, f32[32,448]{1,0:T(8,128)S(1)}, u32[]{:S(2)}, u32[]{:S(2)}) collective-permute-start(f32[32,448]{1,0:T(8,128)S(1)} %get-tuple-element.70.a_ref), channel_id=1, source_target_pairs={{0,3},{1,0},{2,1},{3,2},{4,7},{5,4},{6,5},{7,6},{8,11},{9,8},{10,9... | collective-permute-start | bytes 172040 | tf_op jit(solution)/shard_map/ppermute | solution.py:395
  104.6 2.0 %collective-permute-start.24 = (f32[32,448]{1,0:T(8,128)S(1)}, f32[32,448]{1,0:T(8,128)S(1)}, u32[]{:S(2)}, u32[]{:S(2)}) collective-permute-start(f32[32,448]{1,0:T(8,128)S(1)} %get-tuple-element.70.a_ref), channel_id=1, source_target_pairs={{0,2},{1,3},{2,0},{3,1},{4,6},{5,7},{6,4},{7,5},{8,10},{9,11},{10,... | collective-permute-start | bytes 172040 | tf_op jit(solution)/shard_map/ppermute | solution.py:395
  106.5 2.8 %factor.1 = (f32[32,32]{1,0:T(8,128)S(1)}, f32[32,4096]{1,0:T(8,128)}, bf16[32,4096]{1,0:T(8,128)(2,1)S(1)}) custom-call(f32[32,32,128]{2,1,0:T(8,128)S(1)} %all-to-all-done.2.p_ref), custom_call_target="tpu_custom_call" | custom-call | tf_op jit(solution)/shard_map/factor/pallas_call | solution.py:330
  109.4 0.9 collective-permute-done.24.d_ref
  110.3 5.3 %new_error.1 = (f32[32,448]{1,0:T(8,128)}, bf16[448,4096]{1,0:T(8,128)(2,1)}) custom-call(s32[32]{0:T(128)S(1)} %fusion.at_ref, f32[32,32]{1,0:T(8,128)S(1)} %get-tuple-element.64.inv_ref, f32[32,448]{1,0:T(8,128)S(1)} %get-tuple-element.70.a_ref, f32[32,448]{1,0:T(8,128)S(1)} %collective-permute-done.22.b_ref, f32[32,448]{1,0:T(8,128)S(1)} %collective-permute-done.23.c_ref, ...), custom_call_target="tpu_custom_call" | custom-call | tf_op jit(solution)/shard_map/new_error/pallas_call | solution.py:370
  (51 shorter events, 0.6 us)
Async XLA Ops:
  0.6 8.3 %collective-permute-start = (bf16[1024,128]{1,0:T(8,128)(2,1)}, bf16[1024,128]{1,0:T(8,128)(2,1)S(1)}, u32[]{:S(2)}, u32[]{:S(2)}) collective-permute-start(bf16[1024,128]{1,0:T(8,128)(2,1)} %bitcast.28), channel_id=1, source_target_pairs={{0,4},{4,8},{8,12},{12,16},{16,20},{20,24},{24,28},{28,0},{32,36},... | collective-permute-start | bytes 786440 | tf_op jit(solution)/shard_map/ppermute | solution.py:401
  2.6 8.2 %collective-permute-start.1 = (bf16[1024,128]{1,0:T(8,128)(2,1)}, bf16[1024,128]{1,0:T(8,128)(2,1)S(1)}, u32[]{:S(2)}, u32[]{:S(2)}) collective-permute-start(bf16[1024,128]{1,0:T(8,128)(2,1)} %bitcast.29), channel_id=1, source_target_pairs={{0,28},{4,0},{8,4},{12,8},{16,12},{20,16},{24,20},{28,24},{32,60},... | collective-permute-start | bytes 786440 | tf_op jit(solution)/shard_map/ppermute | solution.py:401
  2.7 11.2 %collective-permute-start.4 = (bf16[1024,128]{1,0:T(8,128)(2,1)}, bf16[1024,128]{1,0:T(8,128)(2,1)S(1)}, u32[]{:S(2)}, u32[]{:S(2)}) collective-permute-start(bf16[1024,128]{1,0:T(8,128)(2,1)} %bitcast.30), channel_id=1, source_target_pairs={{0,64},{4,68},{8,72},{12,76},{16,80},{20,84},{24,88},{28,92},{32,9... | collective-permute-start | bytes 786440 | tf_op jit(solution)/shard_map/ppermute | solution.py:401
  5.8 25.7 %copy-start.1 = (bf16[1,1024,128]{2,1,0:T(8,128)(2,1)S(1)}, bf16[1,1024,128]{2,1,0:T(8,128)(2,1)}, u32[]{:S(2)}) copy-start(bf16[1,1024,128]{2,1,0:T(8,128)(2,1)} %param.12) | copy-start | bytes 786436
  10.8 8.1 %collective-permute-start.2 = (bf16[1024,128]{1,0:T(8,128)(2,1)S(1)}, bf16[1024,128]{1,0:T(8,128)(2,1)S(1)}, u32[]{:S(2)}, u32[]{:S(2)}) collective-permute-start(bf16[1024,128]{1,0:T(8,128)(2,1)S(1)} %collective-permute-done.refs_1_.refs_5_), channel_id=1, source_target_pairs={{0,4},{4,8},{8,12},{12,16},{16,20},{20,24},{24,28},{28,0},{32,36},... | collective-permute-start | bytes 786440 | tf_op jit(solution)/shard_map/ppermute | solution.py:401
  13.9 7.8 %collective-permute-start.3 = (bf16[1024,128]{1,0:T(8,128)(2,1)S(1)}, bf16[1024,128]{1,0:T(8,128)(2,1)S(1)}, u32[]{:S(2)}, u32[]{:S(2)}) collective-permute-start(bf16[1024,128]{1,0:T(8,128)(2,1)S(1)} %collective-permute-done.1.refs_2_.refs_6_), channel_id=1, source_target_pairs={{0,28},{4,0},{8,4},{12,8},{16,12},{20,16},{24,20},{28,24},{32,60},... | collective-permute-start | bytes 786440 | tf_op jit(solution)/shard_map/ppermute | solution.py:401
  13.9 23.4 %copy-start.2 = (bf16[1024,128]{1,0:T(8,128)(2,1)}, bf16[1024,128]{1,0:T(8,128)(2,1)S(1)}, u32[]{:S(2)}) copy-start(bf16[1024,128]{1,0:T(8,128)(2,1)S(1)} %collective-permute-done.4.refs_2_) | copy-start | bytes 786436
  21.7 7.7 %collective-permute-start.5 = (bf16[1024,128]{1,0:T(8,128)(2,1)S(1)}, bf16[1024,128]{1,0:T(8,128)(2,1)S(1)}, u32[]{:S(2)}, u32[]{:S(2)}) collective-permute-start(bf16[1024,128]{1,0:T(8,128)(2,1)S(1)} %collective-permute-done.2.refs_3_.refs_7_), channel_id=1, source_target_pairs={{0,4},{4,8},{8,12},{12,16},{16,20},{20,24},{24,28},{28,0},{32,36},... | collective-permute-start | bytes 786440 | tf_op jit(solution)/shard_map/ppermute | solution.py:401
  23.4 7.7 %collective-permute-start.6 = (bf16[1024,128]{1,0:T(8,128)(2,1)S(1)}, bf16[1024,128]{1,0:T(8,128)(2,1)S(1)}, u32[]{:S(2)}, u32[]{:S(2)}) collective-permute-start(bf16[1024,128]{1,0:T(8,128)(2,1)S(1)} %collective-permute-done.3.refs_4_.refs_8_), channel_id=1, source_target_pairs={{0,28},{4,0},{8,4},{12,8},{16,12},{20,16},{24,20},{28,24},{32,60},... | collective-permute-start | bytes 786440 | tf_op jit(solution)/shard_map/ppermute | solution.py:401
  23.7 9.0 %collective-permute-start.7 = (bf16[96,1024]{1,0:T(8,128)(2,1)S(1)}, bf16[96,1024]{1,0:T(8,128)(2,1)S(1)}, u32[]{:S(2)}, u32[]{:S(2)}) collective-permute-start(bf16[96,1024]{1,0:T(8,128)(2,1)S(1)} %get-tuple-element.45), channel_id=1, source_target_pairs={{0,32},{4,36},{8,40},{12,44},{16,48},{20,52},{24,56},{28,60},{32,6... | collective-permute-start | bytes 589832 | tf_op jit(solution)/shard_map/ppermute | solution.py:401
  25.2 8.9 %collective-permute-start.8 = (bf16[96,1024]{1,0:T(8,128)(2,1)S(1)}, bf16[96,1024]{1,0:T(8,128)(2,1)S(1)}, u32[]{:S(2)}, u32[]{:S(2)}) collective-permute-start(bf16[96,1024]{1,0:T(8,128)(2,1)S(1)} %get-tuple-element.46), channel_id=1, source_target_pairs={{0,64},{4,68},{8,72},{12,76},{16,80},{20,84},{24,88},{28,92},{32,9... | collective-permute-start | bytes 589832 | tf_op jit(solution)/shard_map/ppermute | solution.py:401
  27.9 6.2 %collective-permute-start.9 = (bf16[96,1024]{1,0:T(8,128)(2,1)S(1)}, bf16[96,1024]{1,0:T(8,128)(2,1)S(1)}, u32[]{:S(2)}, u32[]{:S(2)}) collective-permute-start(bf16[96,1024]{1,0:T(8,128)(2,1)S(1)} %get-tuple-element.47), channel_id=1, source_target_pairs={{0,96},{4,100},{8,104},{12,108},{16,112},{20,116},{24,120},{28,124... | collective-permute-start | bytes 589832 | tf_op jit(solution)/shard_map/ppermute | solution.py:401
  29.4 8.0 %collective-permute-start.10 = (bf16[1024,128]{1,0:T(8,128)(2,1)S(1)}, bf16[1024,128]{1,0:T(8,128)(2,1)}, u32[]{:S(2)}, u32[]{:S(2)}) collective-permute-start(bf16[1024,128]{1,0:T(8,128)(2,1)S(1)} %collective-permute-done.4.refs_2_), channel_id=1, source_target_pairs={{0,4},{4,8},{8,12},{12,16},{16,20},{20,24},{24,28},{28,0},{32,36},... | collective-permute-start | bytes 786440 | tf_op jit(solution)/shard_map/ppermute | solution.py:401
  31.1 6.5 %collective-permute-start.11 = (bf16[1024,128]{1,0:T(8,128)(2,1)S(1)}, bf16[1024,128]{1,0:T(8,128)(2,1)}, u32[]{:S(2)}, u32[]{:S(2)}) collective-permute-start(bf16[1024,128]{1,0:T(8,128)(2,1)S(1)} %collective-permute-done.4.refs_2_), channel_id=1, source_target_pairs={{0,28},{4,0},{8,4},{12,8},{16,12},{20,16},{24,20},{28,24},{32,60},... | collective-permute-start | bytes 786440 | tf_op jit(solution)/shard_map/ppermute | solution.py:401
  32.7 21.1 %copy-start.12 = (s32[4]{0:T(128)S(1)}, s32[4]{0:T(128)}, u32[]{:S(2)}) copy-start(s32[4]{0:T(128)} %constant.145.clone) | copy-start | bytes 52
  34.1 51.0 %collective-permute-start.18 = (bf16[7168,128]{1,0:T(8,128)(2,1)}, bf16[7168,128]{1,0:T(8,128)(2,1)}, u32[]{:S(2)}, u32[]{:S(2)}) collective-permute-start(bf16[7168,128]{1,0:T(8,128)(2,1)} %pack.1.refs_0_), channel_id=1, source_target_pairs={{0,32},{4,36},{8,40},{12,44},{16,48},{20,52},{24,56},{28,60},{32,6... | collective-permute-start | bytes 5505032 | tf_op jit(solution)/shard_map/ppermute | solution.py:401
  35.9 49.2 %collective-permute-start.19 = (bf16[7168,128]{1,0:T(8,128)(2,1)}, bf16[7168,128]{1,0:T(8,128)(2,1)}, u32[]{:S(2)}, u32[]{:S(2)}) collective-permute-start(bf16[7168,128]{1,0:T(8,128)(2,1)} %pack.1.refs_0_), channel_id=1, source_target_pairs={{0,96},{4,100},{8,104},{12,108},{16,112},{20,116},{24,120},{28,124... | collective-permute-start | bytes 5505032 | tf_op jit(solution)/shard_map/ppermute | solution.py:401
  37.6 7.2 %collective-permute-start.12 = (bf16[1024,128]{1,0:T(8,128)(2,1)S(1)}, bf16[1024,128]{1,0:T(8,128)(2,1)S(1)}, u32[]{:S(2)}, u32[]{:S(2)}) collective-permute-start(bf16[1024,128]{1,0:T(8,128)(2,1)S(1)} %collective-permute-done.5.refs_5_.refs_9_), channel_id=1, source_target_pairs={{0,4},{4,8},{8,12},{12,16},{16,20},{20,24},{24,28},{28,0},{32,36},... | collective-permute-start | bytes 786440 | tf_op jit(solution)/shard_map/ppermute | solution.py:401
  39.4 17.7 %collective-permute-start.13 = (bf16[1024,128]{1,0:T(8,128)(2,1)}, bf16[1024,128]{1,0:T(8,128)(2,1)}, u32[]{:S(2)}, u32[]{:S(2)}) collective-permute-start(bf16[1024,128]{1,0:T(8,128)(2,1)} %collective-permute-done.10.refs_3_), channel_id=1, source_target_pairs={{0,4},{4,8},{8,12},{12,16},{16,20},{20,24},{24,28},{28,0},{32,36},... | collective-permute-start | bytes 786440 | tf_op jit(solution)/shard_map/ppermute | solution.py:401
  42.1 15.0 %collective-permute-start.14 = (bf16[1024,128]{1,0:T(8,128)(2,1)}, bf16[1024,128]{1,0:T(8,128)(2,1)}, u32[]{:S(2)}, u32[]{:S(2)}) collective-permute-start(bf16[1024,128]{1,0:T(8,128)(2,1)} %collective-permute-done.11.refs_4_), channel_id=1, source_target_pairs={{0,28},{4,0},{8,4},{12,8},{16,12},{20,16},{24,20},{28,24},{32,60},... | collective-permute-start | bytes 786440 | tf_op jit(solution)/shard_map/ppermute | solution.py:401
  44.8 22.5 %copy-start = (bf16[1024,128]{1,0:T(8,128)(2,1)}, bf16[1024,128]{1,0:T(8,128)(2,1)S(1)}, u32[]{:S(2)}) copy-start(bf16[1024,128]{1,0:T(8,128)(2,1)S(1)} %collective-permute-done.12.refs_0_.refs_1_) | copy-start | bytes 786436
  46.2 16.0 %all-to-all-start = ((f32[8,32,128]{2,1,0:T(8,128)}), f32[8,32,128]{2,1,0:T(8,128)S(1)}, u32[]{:S(2)}, u32[]{:S(2)}) async-start(f32[8,32,128]{2,1,0:T(8,128)} %p_column_rest.1), calls=%async_computation | async-start | bytes 262144 | tf_op jit(solution)/shard_map/all_to_all | solution.py:390
  53.8 13.5 %copy-start.11 = (s32[4]{0:T(128)S(1)}, s32[4]{0:T(128)}, u32[]{:S(2)}) copy-start(s32[4]{0:T(128)} %constant.146.clone) | copy-start | bytes 52
  57.1 16.7 %collective-permute-start.15 = (bf16[1024,128]{1,0:T(8,128)(2,1)}, bf16[1024,128]{1,0:T(8,128)(2,1)S(1)}, u32[]{:S(2)}, u32[]{:S(2)}) collective-permute-start(bf16[1024,128]{1,0:T(8,128)(2,1)} %collective-permute-done.13.refs_5_), channel_id=1, source_target_pairs={{0,4},{4,8},{8,12},{12,16},{16,20},{20,24},{24,28},{28,0},{32,36},... | collective-permute-start | bytes 786440 | tf_op jit(solution)/shard_map/ppermute | solution.py:401
  58.6 15.2 %collective-permute-start.16 = (bf16[1024,128]{1,0:T(8,128)(2,1)}, bf16[1024,128]{1,0:T(8,128)(2,1)S(1)}, u32[]{:S(2)}, u32[]{:S(2)}) collective-permute-start(bf16[1024,128]{1,0:T(8,128)(2,1)} %collective-permute-done.14.refs_7_), channel_id=1, source_target_pairs={{0,28},{4,0},{8,4},{12,8},{16,12},{20,16},{24,20},{28,24},{32,60},... | collective-permute-start | bytes 786440 | tf_op jit(solution)/shard_map/ppermute | solution.py:401
  59.2 14.6 %collective-permute-start.17 = (bf16[1024,128]{1,0:T(8,128)(2,1)}, bf16[1024,128]{1,0:T(8,128)(2,1)S(1)}, u32[]{:S(2)}, u32[]{:S(2)}) collective-permute-start(bf16[1024,128]{1,0:T(8,128)(2,1)} %collective-permute-done.14.refs_7_), channel_id=1, source_target_pairs={{0,24},{4,28},{8,0},{12,4},{16,8},{20,12},{24,16},{28,20},{32,56},... | collective-permute-start | bytes 786440 | tf_op jit(solution)/shard_map/ppermute | solution.py:401
  62.8 10.1 %all-to-all-start.1 = ((f32[4,32,128]{2,1,0:T(8,128)}), f32[4,32,128]{2,1,0:T(8,128)S(1)}, u32[]{:S(2)}, u32[]{:S(2)}) async-start(f32[4,32,128]{2,1,0:T(8,128)} %add_spread.2), calls=%async_computation.1 | async-start | bytes 131072 | tf_op jit(solution)/shard_map/all_to_all | solution.py:390
  67.3 17.7 %copy-start.9 = (s32[32]{0:T(128)S(1)}, s32[32]{0:T(128)}, u32[]{:S(2)}) copy-start(s32[32]{0:T(128)} %constant.147.clone) | copy-start | bytes 388
  67.3 17.7 %copy-start.10 = (s32[32]{0:T(128)S(1)}, s32[32]{0:T(128)}, u32[]{:S(2)}) copy-start(s32[32]{0:T(128)} %constant.148.clone) | copy-start | bytes 388
  67.3 17.7 %copy-start.7 = (s32[18]{0:T(128)S(1)}, s32[18]{0:T(128)}, u32[]{:S(2)}) copy-start(s32[18]{0:T(128)} %constant.149.clone) | copy-start | bytes 220
  67.4 17.7 %copy-start.8 = (s32[18]{0:T(128)S(1)}, s32[18]{0:T(128)}, u32[]{:S(2)}) copy-start(s32[18]{0:T(128)} %constant.150.clone) | copy-start | bytes 220
  73.8 11.3 %copy-start.3 = (bf16[1024,128]{1,0:T(8,128)(2,1)}, bf16[1024,128]{1,0:T(8,128)(2,1)S(1)}, u32[]{:S(2)}) copy-start(bf16[1024,128]{1,0:T(8,128)(2,1)S(1)} %collective-permute-done.15.refs_8_) | copy-start | bytes 786436
  73.8 11.3 %copy-start.4 = (bf16[1024,128]{1,0:T(8,128)(2,1)}, bf16[1024,128]{1,0:T(8,128)(2,1)S(1)}, u32[]{:S(2)}) copy-start(bf16[1024,128]{1,0:T(8,128)(2,1)S(1)} %collective-permute-done.16.refs_9_) | copy-start | bytes 786436
  73.8 11.3 %copy-start.5 = (bf16[1024,128]{1,0:T(8,128)(2,1)}, bf16[1024,128]{1,0:T(8,128)(2,1)S(1)}, u32[]{:S(2)}) copy-start(bf16[1024,128]{1,0:T(8,128)(2,1)S(1)} %collective-permute-done.17.refs_10_) | copy-start | bytes 786436
  73.8 21.8 %all-to-all-start.2 = ((f32[32,32,128]{2,1,0:T(8,128)}), f32[32,32,128]{2,1,0:T(8,128)S(1)}, u32[]{:S(2)}, u32[]{:S(2)}) async-start(f32[32,32,128]{2,1,0:T(8,128)} %add_spread.3), calls=%async_computation.2 | async-start | bytes 1048576 | tf_op jit(solution)/shard_map/all_to_all | solution.py:390
  81.7 11.1 %collective-permute-start.20 = (bf16[1024,128]{1,0:T(8,128)(2,1)}, bf16[1024,128]{1,0:T(8,128)(2,1)S(1)}, u32[]{:S(2)}, u32[]{:S(2)}) collective-permute-start(bf16[1024,128]{1,0:T(8,128)(2,1)} %copy-done), channel_id=1, source_target_pairs={{0,32},{4,36},{8,40},{12,44},{16,48},{20,52},{24,56},{28,60},{32,6... | collective-permute-start | bytes 786440 | tf_op jit(solution)/shard_map/ppermute | solution.py:401
  83.2 10.3 %collective-permute-start.21 = (bf16[1024,128]{1,0:T(8,128)(2,1)}, bf16[1024,128]{1,0:T(8,128)(2,1)}, u32[]{:S(2)}, u32[]{:S(2)}) collective-permute-start(bf16[1024,128]{1,0:T(8,128)(2,1)} %copy-done), channel_id=1, source_target_pairs={{0,96},{4,100},{8,104},{12,108},{16,112},{20,116},{24,120},{28,124... | collective-permute-start | bytes 786440 | tf_op jit(solution)/shard_map/ppermute | solution.py:401
  92.8 0.7 copy-start.6
  101.2 8.1 %collective-permute-start.22 = (f32[32,448]{1,0:T(8,128)S(1)}, f32[32,448]{1,0:T(8,128)S(1)}, u32[]{:S(2)}, u32[]{:S(2)}) collective-permute-start(f32[32,448]{1,0:T(8,128)S(1)} %get-tuple-element.70.a_ref), channel_id=1, source_target_pairs={{0,1},{1,2},{2,3},{3,0},{4,5},{5,6},{6,7},{7,4},{8,9},{9,10},{10,1... | collective-permute-start | bytes 172040 | tf_op jit(solution)/shard_map/ppermute | solution.py:395
  102.9 6.5 %collective-permute-start.23 = (f32[32,448]{1,0:T(8,128)S(1)}, f32[32,448]{1,0:T(8,128)S(1)}, u32[]{:S(2)}, u32[]{:S(2)}) collective-permute-start(f32[32,448]{1,0:T(8,128)S(1)} %get-tuple-element.70.a_ref), channel_id=1, source_target_pairs={{0,3},{1,0},{2,1},{3,2},{4,7},{5,4},{6,5},{7,6},{8,11},{9,8},{10,9... | collective-permute-start | bytes 172040 | tf_op jit(solution)/shard_map/ppermute | solution.py:395
  104.6 5.8 %collective-permute-start.24 = (f32[32,448]{1,0:T(8,128)S(1)}, f32[32,448]{1,0:T(8,128)S(1)}, u32[]{:S(2)}, u32[]{:S(2)}) collective-permute-start(f32[32,448]{1,0:T(8,128)S(1)} %get-tuple-element.70.a_ref), channel_id=1, source_target_pairs={{0,2},{1,3},{2,0},{3,1},{4,6},{5,7},{6,4},{7,5},{8,10},{9,11},{10,... | collective-permute-start | bytes 172040 | tf_op jit(solution)/shard_map/ppermute | solution.py:395

commit v6 on v5

--- a/solution.py
+++ b/solution.py
@@ -434,23 +434,20 @@
     part, t = column(z_order, [mine, g1, g2, g3], [x, p1, m1, p2, m2, p3, m3])
     column_groups = [[8 * i + z for z in range(8)] for i in range(4)]
     p_parts = swap(column_rest(z_order, part, t, [end]), groups=column_groups)
-    own_early, own_late = (0, SOURCE_Z[:4]), (0, SOURCE_Z[4:])
-    kept_own = correct(places(own_early), h_t, e_t, [bundle], [(0, 4)])
     fp2, fm2 = move(fp1, 0, 1), move(fm1, 0, -1)
-    fp2, fm2, kept_own = together(fp2, fm2, kept_own)
     fp3, fm3, f_end = move(fp2, 0, 1), move(fm2, 0, -1), move(fm2, 0, -2)
-    p_parts, kept_own = together(add_spread(p_parts, 4, 1.0), kept_own)
+    p_parts = add_spread(p_parts, 4, 1.0)
     p_parts = add_spread(swap(p_parts, "replica"), 32, 0.25)
-    kept_late = correct(places(own_late), h_t, e_t, [bundle, end], [(4, 3), (0, 1)])
-    p_parts, fp3, fm3, f_end, kept_late = together(p_parts, fp3, fm3, f_end, kept_late)
+    kept_own = correct(places((0, SOURCE_Z)), h_t, e_t, [bundle, end], [(0, 7), (0, 1)])
+    p_parts, fp3, fm3, f_end, kept_own = together(p_parts, fp3, fm3, f_end, kept_own)
     far = [f0, fp1, fm1, fp2, fm2, fp3, fm3, f_end]
     p_blocks = swap(p_parts)
     middle = [(-1, SOURCE_Z[:7]), (1, SOURCE_Z[:7]), (2, SOURCE_Z[:4])]
     rest = [(-1, SOURCE_Z[7:]), (1, SOURCE_Z[7:]), (2, SOURCE_Z[4:])]
-    at = places(own_early, own_late, *middle, *rest)
+    at = places((0, SOURCE_Z), *middle, *rest)
     parts_of = [(0, 7), (0, 7)] + [(0, 1)] * 4
     kept_middle = correct(places(*middle), h_t, e_t, [*near, *far[:4]], parts_of)
-    kept = [kept_own, kept_late, kept_middle]
+    kept = [kept_own, kept_middle]
     w_part, piece = finish(at, p_blocks, kept, h_t, e_t, [*near_end, *far[4:]])
     parts = replicas(w_part)
     inverse, p_factor, p_low = factor(p_blocks)

time: 116 us -> 114 us (0.983)
  starting transfers between devices: 59 us -> 55.1 us
  waiting for transfers between devices: 17.6 us -> 21.3 us
  Pallas kernels: 37.2 us -> 35.3 us
    all_to_all x3, starting transfers between devices: 19.9 us -> 16.7 us  [swap(): return lax.all_to_all(v, axis, 0, 0, axis_index_groups=groups)]
    all_to_all x3, waiting for transfers between devices: 4.73 us -> 7.8 us  [swap(): return lax.all_to_all(v, axis, 0, 0, axis_index_groups=groups)]
    pallas_call x3 -> x2, Pallas kernels: 14.2 us -> 12.3 us  [correct(): pl.pallas_call(functools.partial(correct_kernel, parts_of), in_specs=[SME...]
  transfers between devices with their start and end apart: 28 -> 28, of which waited for: 11 -> 11; matrix products, arithmetic and copies ran while one was open for 0% -> 0% of each run, Pallas kernels for 23% -> 21%
where the time goes in v6:
time: 114 us
  starting transfers between devices  55.1 us (48%)
  Pallas kernels  35.3 us (31%)
  waiting for transfers between devices  21.3 us (19%)
    ppermute x22, starting transfers between devices, move(): return lax.ppermute(v, 'hidden', pairs)  33.7 us
    all_to_all x3, starting transfers between devices, swap(): return lax.all_to_all(v, axis, 0, 0, axis_index_groups=groups)  16.7 us
    pallas_call x2, Pallas kernels, correct(): pl.pallas_call(functools.partial(correct_kernel, parts_of), in_specs=[SME...  12.3 us
    ppermute x22, waiting for transfers between devices, move(): return lax.ppermute(v, 'hidden', pairs)  12 us
    all_to_all x3, waiting for transfers between devices, swap(): return lax.all_to_all(v, axis, 0, 0, axis_index_groups=groups)  7.8 us
    pallas_call x1, Pallas kernels, finish(): pl.pallas_call(functools.partial(finish_kernel, len(kept)), in_specs=[SME...  5.57 us
    pallas_call x1, Pallas kernels, final(): pl.pallas_call(final_kernel, in_specs=[SMEM] + [VMEM] * (6 + len(kept)) +...  5.31 us
    ppermute x3, starting transfers between devices, replicas(): lax.ppermute(v, 'replica', [(i, (i + s) % 4) for i in range(4)])  4.72 us
  transfers between devices with their start and end apart: 28, of which 11 were waited for; matrix products, arithmetic and copies ran while one was open for 0% of the time, Pallas kernels for 21%

profile of v6, /device:TPU:32, one launch (start us, length us, event | category | flops | bytes accessed | tf_op | source)
XLA Modules:
  0.0 113.6 jit_solution(8847993395795230498)
XLA Ops:
  0.6 2.0 %collective-permute-start = (bf16[1024,128]{1,0:T(8,128)(2,1)}, bf16[1024,128]{1,0:T(8,128)(2,1)S(1)}, u32[]{:S(2)}, u32[]{:S(2)}) collective-permute-start(bf16[1024,128]{1,0:T(8,128)(2,1)} %bitcast.28), channel_id=1, source_target_pairs={{0,4},{4,8},{8,12},{12,16},{16,20},{20,24},{24,28},{28,0},{32,36},... | collective-permute-start | bytes 786440 | tf_op jit(solution)/shard_map/ppermute | solution.py:401
  2.7 3.0 %collective-permute-start.4 = (bf16[1024,128]{1,0:T(8,128)(2,1)}, bf16[1024,128]{1,0:T(8,128)(2,1)S(1)}, u32[]{:S(2)}, u32[]{:S(2)}) collective-permute-start(bf16[1024,128]{1,0:T(8,128)(2,1)} %bitcast.30), channel_id=1, source_target_pairs={{0,64},{4,68},{8,72},{12,76},{16,80},{20,84},{24,88},{28,92},{32,9... | collective-permute-start | bytes 786440 | tf_op jit(solution)/shard_map/ppermute | solution.py:401
  5.8 2.7 %eq_hq.1 = (bf16[96,1024]{1,0:T(8,128)(2,1)S(1)}, bf16[96,1024]{1,0:T(8,128)(2,1)S(1)}, bf16[96,1024]{1,0:T(8,128)(2,1)S(1)}, bf16[96,1024]{1,0:T(8,128)(2,1)S(1)}) custom-call(s32[1]{0:T(128)} %bitcast.9.x_ref, f32[32,448]{1,0:T(8,128)} %bitcast.41, bf16[448,4096]{1,0:T(8,128)(2,1)} %bitcast.33, bf16[448,1024]{1,0:T(8,128)(2,1)} %bitcast.37), custom_call_target="tpu_custom_call" | custom-call | tf_op jit(solution)/shard_map/eq_hq/pallas_call | solution.py:78
  8.5 0.5 collective-permute-done.refs_1_.refs_5_
  9.0 1.8 %collective-permute-done.1.refs_2_.refs_6_ = bf16[1024,128]{1,0:T(8,128)(2,1)S(1)} collective-permute-done((bf16[1024,128]{1,0:T(8,128)(2,1)}, bf16[1024,128]{1,0:T(8,128)(2,1)S(1)}, u32[]{:S(2)}, u32[]{:S(2)}) %collective-permute-start.1) | collective-permute-done | bytes 262176 | tf_op jit(solution)/shard_map/ppermute | solution.py:401
  10.8 3.1 %collective-permute-start.2 = (bf16[1024,128]{1,0:T(8,128)(2,1)S(1)}, bf16[1024,128]{1,0:T(8,128)(2,1)S(1)}, u32[]{:S(2)}, u32[]{:S(2)}) collective-permute-start(bf16[1024,128]{1,0:T(8,128)(2,1)S(1)} %collective-permute-done.refs_1_.refs_5_), channel_id=1, source_target_pairs={{0,4},{4,8},{8,12},{12,16},{16,20},{20,24},{24,28},{28,0},{32,36},... | collective-permute-start | bytes 786440 | tf_op jit(solution)/shard_map/ppermute | solution.py:401
  13.9 5.0 %collective-permute-done.2.refs_3_.refs_7_ = bf16[1024,128]{1,0:T(8,128)(2,1)S(1)} collective-permute-done((bf16[1024,128]{1,0:T(8,128)(2,1)S(1)}, bf16[1024,128]{1,0:T(8,128)(2,1)S(1)}, u32[]{:S(2)}, u32[]{:S(2)}) %collective-permute-start.2) | collective-permute-done | bytes 262176 | tf_op jit(solution)/shard_map/ppermute | solution.py:401
  18.9 2.8 %collective-permute-done.3.refs_4_.refs_8_ = bf16[1024,128]{1,0:T(8,128)(2,1)S(1)} collective-permute-done((bf16[1024,128]{1,0:T(8,128)(2,1)S(1)}, bf16[1024,128]{1,0:T(8,128)(2,1)S(1)}, u32[]{:S(2)}, u32[]{:S(2)}) %collective-permute-start.3) | collective-permute-done | bytes 262176 | tf_op jit(solution)/shard_map/ppermute | solution.py:401
  21.7 1.7 %collective-permute-start.5 = (bf16[1024,128]{1,0:T(8,128)(2,1)S(1)}, bf16[1024,128]{1,0:T(8,128)(2,1)S(1)}, u32[]{:S(2)}, u32[]{:S(2)}) collective-permute-start(bf16[1024,128]{1,0:T(8,128)(2,1)S(1)} %collective-permute-done.2.refs_3_.refs_7_), channel_id=1, source_target_pairs={{0,4},{4,8},{8,12},{12,16},{16,20},{20,24},{24,28},{28,0},{32,36},... | collective-permute-start | bytes 786440 | tf_op jit(solution)/shard_map/ppermute | solution.py:401
  23.4 0.3 collective-permute-start.6
  23.7 1.5 %collective-permute-start.7 = (bf16[96,1024]{1,0:T(8,128)(2,1)S(1)}, bf16[96,1024]{1,0:T(8,128)(2,1)S(1)}, u32[]{:S(2)}, u32[]{:S(2)}) collective-permute-start(bf16[96,1024]{1,0:T(8,128)(2,1)S(1)} %get-tuple-element.40), channel_id=1, source_target_pairs={{0,32},{4,36},{8,40},{12,44},{16,48},{20,52},{24,56},{28,60},{32,6... | collective-permute-start | bytes 589832 | tf_op jit(solution)/shard_map/ppermute | solution.py:401
  25.2 2.7 %collective-permute-start.8 = (bf16[96,1024]{1,0:T(8,128)(2,1)S(1)}, bf16[96,1024]{1,0:T(8,128)(2,1)S(1)}, u32[]{:S(2)}, u32[]{:S(2)}) collective-permute-start(bf16[96,1024]{1,0:T(8,128)(2,1)S(1)} %get-tuple-element.41), channel_id=1, source_target_pairs={{0,64},{4,68},{8,72},{12,76},{16,80},{20,84},{24,88},{28,92},{32,9... | collective-permute-start | bytes 589832 | tf_op jit(solution)/shard_map/ppermute | solution.py:401
  27.9 1.4 %collective-permute-start.9 = (bf16[96,1024]{1,0:T(8,128)(2,1)S(1)}, bf16[96,1024]{1,0:T(8,128)(2,1)S(1)}, u32[]{:S(2)}, u32[]{:S(2)}) collective-permute-start(bf16[96,1024]{1,0:T(8,128)(2,1)S(1)} %get-tuple-element.42), channel_id=1, source_target_pairs={{0,96},{4,100},{8,104},{12,108},{16,112},{20,116},{24,120},{28,124... | collective-permute-start | bytes 589832 | tf_op jit(solution)/shard_map/ppermute | solution.py:401
  29.4 1.7 %collective-permute-start.10 = (bf16[1024,128]{1,0:T(8,128)(2,1)S(1)}, bf16[1024,128]{1,0:T(8,128)(2,1)S(1)}, u32[]{:S(2)}, u32[]{:S(2)}) collective-permute-start(bf16[1024,128]{1,0:T(8,128)(2,1)S(1)} %collective-permute-done.4.refs_2_), channel_id=1, source_target_pairs={{0,4},{4,8},{8,12},{12,16},{16,20},{20,24},{24,28},{28,0},{32,36},... | collective-permute-start | bytes 786440 | tf_op jit(solution)/shard_map/ppermute | solution.py:401
  31.1 0.3 collective-permute-start.11
  31.4 1.3 %pack.1.refs_0_ = bf16[7168,128]{1,0:T(8,128)(2,1)} custom-call(bf16[1024,128]{1,0:T(8,128)(2,1)S(1)} %bitcast.31, bf16[1024,128]{1,0:T(8,128)(2,1)S(1)} %collective-permute-done.refs_1_.refs_5_, bf16[1024,128]{1,0:T(8,128)(2,1)S(1)} %collective-permute-done.1.refs_2_.refs_6_, bf16[1024,128]{1,0:T(8,128)(2,1)S(1)} %collective-permute-done.2.refs_3_.refs_7_, ...), custom_call_target="tpu_custom_call" | custom-call | tf_op jit(solution)/shard_map/pack/pallas_call | solution.py:189
  32.7 1.4 %collective-permute-done.8.refs_2_ = bf16[96,1024]{1,0:T(8,128)(2,1)S(1)} collective-permute-done((bf16[96,1024]{1,0:T(8,128)(2,1)S(1)}, bf16[96,1024]{1,0:T(8,128)(2,1)S(1)}, u32[]{:S(2)}, u32[]{:S(2)}) %collective-permute-start.8) | collective-permute-done | bytes 196640 | tf_op jit(solution)/shard_map/ppermute | solution.py:401
  34.1 1.8 %collective-permute-start.18 = (bf16[7168,128]{1,0:T(8,128)(2,1)}, bf16[7168,128]{1,0:T(8,128)(2,1)}, u32[]{:S(2)}, u32[]{:S(2)}) collective-permute-start(bf16[7168,128]{1,0:T(8,128)(2,1)} %pack.1.refs_0_), channel_id=1, source_target_pairs={{0,32},{4,36},{8,40},{12,44},{16,48},{20,52},{24,56},{28,60},{32,6... | collective-permute-start | bytes 5505032 | tf_op jit(solution)/shard_map/ppermute | solution.py:401
  35.9 1.5 %collective-permute-start.19 = (bf16[7168,128]{1,0:T(8,128)(2,1)}, bf16[7168,128]{1,0:T(8,128)(2,1)}, u32[]{:S(2)}, u32[]{:S(2)}) collective-permute-start(bf16[7168,128]{1,0:T(8,128)(2,1)} %pack.1.refs_0_), channel_id=1, source_target_pairs={{0,96},{4,100},{8,104},{12,108},{16,112},{20,116},{24,120},{28,124... | collective-permute-start | bytes 5505032 | tf_op jit(solution)/shard_map/ppermute | solution.py:401
  37.3 0.3 collective-permute-done.11.refs_4_
  37.6 1.8 %collective-permute-start.12 = (bf16[1024,128]{1,0:T(8,128)(2,1)S(1)}, bf16[1024,128]{1,0:T(8,128)(2,1)S(1)}, u32[]{:S(2)}, u32[]{:S(2)}) collective-permute-start(bf16[1024,128]{1,0:T(8,128)(2,1)S(1)} %collective-permute-done.5.refs_5_.refs_9_), channel_id=1, source_target_pairs={{0,4},{4,8},{8,12},{12,16},{16,20},{20,24},{24,28},{28,0},{32,36},... | collective-permute-start | bytes 786440 | tf_op jit(solution)/shard_map/ppermute | solution.py:401
  39.4 2.7 %collective-permute-start.13 = (bf16[1024,128]{1,0:T(8,128)(2,1)S(1)}, bf16[1024,128]{1,0:T(8,128)(2,1)}, u32[]{:S(2)}, u32[]{:S(2)}) collective-permute-start(bf16[1024,128]{1,0:T(8,128)(2,1)S(1)} %collective-permute-done.10.refs_3_), channel_id=1, source_target_pairs={{0,4},{4,8},{8,12},{12,16},{16,20},{20,24},{24,28},{28,0},{32,36},... | collective-permute-start | bytes 786440 | tf_op jit(solution)/shard_map/ppermute | solution.py:401
  42.2 2.4 %p_column.1 = (f32[8,32,128]{2,1,0:T(8,128)S(1)}, bf16[96,1024]{1,0:T(8,128)(2,1)S(1)}) custom-call(s32[8]{0:T(128)S(1)} %stack.35.z_ref, bf16[96,1024]{1,0:T(8,128)(2,1)S(1)} %get-tuple-element.35.refs_0_, bf16[96,1024]{1,0:T(8,128)(2,1)S(1)} %collective-permute-done.7.refs_1_, bf16[96,1024]{1,0:T(8,128)(2,1)S(1)} %collective-permute-done.8.refs_2_, ...), custom_call_target="tpu_custom_call" | custom-call | tf_op jit(solution)/shard_map/p_column/pallas_call | solution.py:124
  44.6 0.2 collective-permute-done.12.refs_0_.refs_1_
  44.8 1.4 %p_column_rest.1 = f32[8,32,128]{2,1,0:T(8,128)} custom-call(s32[8]{0:T(128)S(1)} %stack.35.z_ref, f32[8,32,128]{2,1,0:T(8,128)S(1)} %get-tuple-element.48.part_ref, bf16[96,1024]{1,0:T(8,128)(2,1)S(1)} %get-tuple-element.49.t_ref, bf16[1024,128]{1,0:T(8,128)(2,1)S(1)} %collective-permute-done.12.refs_0_.refs_1_), custom_call_target="tpu_custom_call" | custom-call | tf_op jit(solution)/shard_map/p_column_rest/pallas_call | solution.py:154
  46.2 7.6 %all-to-all-start = ((f32[8,32,128]{2,1,0:T(8,128)}), f32[8,32,128]{2,1,0:T(8,128)S(1)}, u32[]{:S(2)}, u32[]{:S(2)}) async-start(f32[8,32,128]{2,1,0:T(8,128)} %p_column_rest.1), calls=%async_computation | async-start | bytes 262144 | tf_op jit(solution)/shard_map/all_to_all | solution.py:390
  53.8 1.5 %collective-permute-start.14 = (bf16[1024,128]{1,0:T(8,128)(2,1)}, bf16[1024,128]{1,0:T(8,128)(2,1)S(1)}, u32[]{:S(2)}, u32[]{:S(2)}) collective-permute-start(bf16[1024,128]{1,0:T(8,128)(2,1)} %collective-permute-done.13.refs_5_), channel_id=1, source_target_pairs={{0,4},{4,8},{8,12},{12,16},{16,20},{20,24},{24,28},{28,0},{32,36},... | collective-permute-start | bytes 786440 | tf_op jit(solution)/shard_map/ppermute | solution.py:401
  55.3 0.6 collective-permute-start.16
  55.8 2.7 %collective-permute-start.17 = (bf16[1024,128]{1,0:T(8,128)(2,1)}, bf16[1024,128]{1,0:T(8,128)(2,1)S(1)}, u32[]{:S(2)}, u32[]{:S(2)}) collective-permute-start(bf16[1024,128]{1,0:T(8,128)(2,1)} %collective-permute-done.15.refs_6_), channel_id=1, source_target_pairs={{0,24},{4,28},{8,0},{12,4},{16,8},{20,12},{24,16},{28,20},{32,56},... | collective-permute-start | bytes 786440 | tf_op jit(solution)/shard_map/ppermute | solution.py:401
  58.5 4.8 %all-to-all-done.in_ref = f32[8,32,128]{2,1,0:T(8,128)S(1)} async-done(((f32[8,32,128]{2,1,0:T(8,128)}), f32[8,32,128]{2,1,0:T(8,128)S(1)}, u32[]{:S(2)}, u32[]{:S(2)}) %all-to-all-start) | async-done | bytes 131104 | tf_op jit(solution)/shard_map/all_to_all | solution.py:390
  63.3 0.6 add_spread.2
  63.9 4.5 %all-to-all-start.1 = ((f32[4,32,128]{2,1,0:T(8,128)}), f32[4,32,128]{2,1,0:T(8,128)S(1)}, u32[]{:S(2)}, u32[]{:S(2)}) async-start(f32[4,32,128]{2,1,0:T(8,128)} %add_spread.2), calls=%async_computation.1 | async-start | bytes 131072 | tf_op jit(solution)/shard_map/all_to_all | solution.py:390
  68.4 4.6 %corrected.2.refs_0_ = bf16[8,448,128]{2,1,0:T(8,128)(2,1)S(1)} custom-call(s32[8]{0:T(128)S(1)} %fusion.3.at_ref, bf16[448,1024]{1,0:T(8,128)(2,1)} %bitcast.38, bf16[448,4096]{1,0:T(8,128)(2,1)} %bitcast.34, bf16[7168,128]{1,0:T(8,128)(2,1)} %pack.1.refs_0_, bf16[1024,128]{1,0:T(8,128)(2,1)} %copy-done.1), custom_call_target="tpu_custom_call" | custom-call | tf_op jit(solution)/shard_map/corrected/pallas_call | solution.py:241
  73.0 1.0 all-to-all-done.1.in_ref
  74.0 0.9 add_spread.3
  74.9 4.7 %all-to-all-start.2 = ((f32[32,32,128]{2,1,0:T(8,128)}), f32[32,32,128]{2,1,0:T(8,128)S(1)}, u32[]{:S(2)}, u32[]{:S(2)}) async-start(f32[32,32,128]{2,1,0:T(8,128)} %add_spread.3), calls=%async_computation.2 | async-start | bytes 1048576 | tf_op jit(solution)/shard_map/all_to_all | solution.py:390
  79.6 1.5 %collective-permute-start.20 = (bf16[1024,128]{1,0:T(8,128)(2,1)}, bf16[1024,128]{1,0:T(8,128)(2,1)S(1)}, u32[]{:S(2)}, u32[]{:S(2)}) collective-permute-start(bf16[1024,128]{1,0:T(8,128)(2,1)} %copy-done.1), channel_id=1, source_target_pairs={{0,32},{4,36},{8,40},{12,44},{16,48},{20,52},{24,56},{28,60},{32,6... | collective-permute-start | bytes 786440 | tf_op jit(solution)/shard_map/ppermute | solution.py:401
  81.1 1.8 %collective-permute-start.21 = (bf16[1024,128]{1,0:T(8,128)(2,1)}, bf16[1024,128]{1,0:T(8,128)(2,1)}, u32[]{:S(2)}, u32[]{:S(2)}) collective-permute-start(bf16[1024,128]{1,0:T(8,128)(2,1)} %copy-done.1), channel_id=1, source_target_pairs={{0,96},{4,100},{8,104},{12,108},{16,112},{20,116},{24,120},{28,124... | collective-permute-start | bytes 786440 | tf_op jit(solution)/shard_map/ppermute | solution.py:401
  83.0 7.7 %corrected.3.refs_1_ = bf16[18,448,128]{2,1,0:T(8,128)(2,1)S(1)} custom-call(s32[18]{0:T(128)S(1)} %fusion.1.at_ref, bf16[448,1024]{1,0:T(8,128)(2,1)} %bitcast.39, bf16[448,4096]{1,0:T(8,128)(2,1)} %bitcast.35, bf16[7168,128]{1,0:T(8,128)(2,1)} %collective-permute-done.18.refs_0_, bf16[7168,128]{1,0:T(8,128)(2,1)} %collective-permute-done.19.refs_1_, ...), custom_call_target="tpu_custom_call" | custom-call | tf_op jit(solution)/shard_map/corrected/pallas_call | solution.py:241
  90.7 0.7 copy-done.7
  91.4 2.1 %all-to-all-done.2.p_ref = f32[32,32,128]{2,1,0:T(8,128)S(1)} async-done(((f32[32,32,128]{2,1,0:T(8,128)}), f32[32,32,128]{2,1,0:T(8,128)S(1)}, u32[]{:S(2)}, u32[]{:S(2)}) %all-to-all-start.2) | async-done | bytes 524320 | tf_op jit(solution)/shard_map/all_to_all | solution.py:390
  93.5 5.6 %c_p.1 = (f32[32,448]{1,0:T(8,128)S(1)}, bf16[6,448,128]{2,1,0:T(8,128)(2,1)}) custom-call(s32[32]{0:T(128)S(1)} %fusion.at_ref, f32[32,32,128]{2,1,0:T(8,128)S(1)} %all-to-all-done.2.p_ref, bf16[8,448,128]{2,1,0:T(8,128)(2,1)S(1)} %corrected.2.refs_0_, bf16[18,448,128]{2,1,0:T(8,128)(2,1)S(1)} %corrected.3.refs_1_, bf16[448,1024]{1,0:T(8,128)(2,1)} %bitcast.40, ...), custom_call_target="tpu_custom_call" | custom-call | tf_op jit(solution)/shard_map/c_p/pallas_call | solution.py:283
  99.1 1.2 %collective-permute-start.22 = (f32[32,448]{1,0:T(8,128)S(1)}, f32[32,448]{1,0:T(8,128)S(1)}, u32[]{:S(2)}, u32[]{:S(2)}) collective-permute-start(f32[32,448]{1,0:T(8,128)S(1)} %get-tuple-element.60.a_ref), channel_id=1, source_target_pairs={{0,1},{1,2},{2,3},{3,0},{4,5},{5,6},{6,7},{7,4},{8,9},{9,10},{10,1... | collective-permute-start | bytes 172040 | tf_op jit(solution)/shard_map/ppermute | solution.py:395
  100.2 2.1 %collective-permute-start.23 = (f32[32,448]{1,0:T(8,128)S(1)}, f32[32,448]{1,0:T(8,128)S(1)}, u32[]{:S(2)}, u32[]{:S(2)}) collective-permute-start(f32[32,448]{1,0:T(8,128)S(1)} %get-tuple-element.60.a_ref), channel_id=1, source_target_pairs={{0,3},{1,0},{2,1},{3,2},{4,7},{5,4},{6,5},{7,6},{8,11},{9,8},{10,9... | collective-permute-start | bytes 172040 | tf_op jit(solution)/shard_map/ppermute | solution.py:395
  102.4 1.4 %collective-permute-start.24 = (f32[32,448]{1,0:T(8,128)S(1)}, f32[32,448]{1,0:T(8,128)S(1)}, u32[]{:S(2)}, u32[]{:S(2)}) collective-permute-start(f32[32,448]{1,0:T(8,128)S(1)} %get-tuple-element.60.a_ref), channel_id=1, source_target_pairs={{0,2},{1,3},{2,0},{3,1},{4,6},{5,7},{6,4},{7,5},{8,10},{9,11},{10,... | collective-permute-start | bytes 172040 | tf_op jit(solution)/shard_map/ppermute | solution.py:395
  103.8 2.8 %factor.1 = (f32[32,32]{1,0:T(8,128)S(1)}, f32[32,4096]{1,0:T(8,128)}, bf16[32,4096]{1,0:T(8,128)(2,1)S(1)}) custom-call(f32[32,32,128]{2,1,0:T(8,128)S(1)} %all-to-all-done.2.p_ref), custom_call_target="tpu_custom_call" | custom-call | tf_op jit(solution)/shard_map/factor/pallas_call | solution.py:330
  106.6 1.5 %collective-permute-done.24.d_ref = f32[32,448]{1,0:T(8,128)S(1)} collective-permute-done((f32[32,448]{1,0:T(8,128)S(1)}, f32[32,448]{1,0:T(8,128)S(1)}, u32[]{:S(2)}, u32[]{:S(2)}) %collective-permute-start.24) | collective-permute-done | bytes 57376 | tf_op jit(solution)/shard_map/ppermute | solution.py:395
  108.1 5.3 %new_error.1 = (f32[32,448]{1,0:T(8,128)}, bf16[448,4096]{1,0:T(8,128)(2,1)}) custom-call(s32[32]{0:T(128)S(1)} %fusion.at_ref, f32[32,32]{1,0:T(8,128)S(1)} %get-tuple-element.55.inv_ref, f32[32,448]{1,0:T(8,128)S(1)} %get-tuple-element.60.a_ref, f32[32,448]{1,0:T(8,128)S(1)} %collective-permute-done.22.b_ref, f32[32,448]{1,0:T(8,128)S(1)} %collective-permute-done.23.c_ref, ...), custom_call_target="tpu_custom_call" | custom-call | tf_op jit(solution)/shard_map/new_error/pallas_call | solution.py:370
  (49 shorter events, 0.3 us)
Async XLA Ops:
  0.6 8.3 %collective-permute-start = (bf16[1024,128]{1,0:T(8,128)(2,1)}, bf16[1024,128]{1,0:T(8,128)(2,1)S(1)}, u32[]{:S(2)}, u32[]{:S(2)}) collective-permute-start(bf16[1024,128]{1,0:T(8,128)(2,1)} %bitcast.28), channel_id=1, source_target_pairs={{0,4},{4,8},{8,12},{12,16},{16,20},{20,24},{24,28},{28,0},{32,36},... | collective-permute-start | bytes 786440 | tf_op jit(solution)/shard_map/ppermute | solution.py:401
  2.6 8.2 %collective-permute-start.1 = (bf16[1024,128]{1,0:T(8,128)(2,1)}, bf16[1024,128]{1,0:T(8,128)(2,1)S(1)}, u32[]{:S(2)}, u32[]{:S(2)}) collective-permute-start(bf16[1024,128]{1,0:T(8,128)(2,1)} %bitcast.29), channel_id=1, source_target_pairs={{0,28},{4,0},{8,4},{12,8},{16,12},{20,16},{24,20},{28,24},{32,60},... | collective-permute-start | bytes 786440 | tf_op jit(solution)/shard_map/ppermute | solution.py:401
  2.7 11.2 %collective-permute-start.4 = (bf16[1024,128]{1,0:T(8,128)(2,1)}, bf16[1024,128]{1,0:T(8,128)(2,1)S(1)}, u32[]{:S(2)}, u32[]{:S(2)}) collective-permute-start(bf16[1024,128]{1,0:T(8,128)(2,1)} %bitcast.30), channel_id=1, source_target_pairs={{0,64},{4,68},{8,72},{12,76},{16,80},{20,84},{24,88},{28,92},{32,9... | collective-permute-start | bytes 786440 | tf_op jit(solution)/shard_map/ppermute | solution.py:401
  5.8 25.7 %copy-start = (bf16[1,1024,128]{2,1,0:T(8,128)(2,1)S(1)}, bf16[1,1024,128]{2,1,0:T(8,128)(2,1)}, u32[]{:S(2)}) copy-start(bf16[1,1024,128]{2,1,0:T(8,128)(2,1)} %param.10) | copy-start | bytes 786436
  10.8 8.1 %collective-permute-start.2 = (bf16[1024,128]{1,0:T(8,128)(2,1)S(1)}, bf16[1024,128]{1,0:T(8,128)(2,1)S(1)}, u32[]{:S(2)}, u32[]{:S(2)}) collective-permute-start(bf16[1024,128]{1,0:T(8,128)(2,1)S(1)} %collective-permute-done.refs_1_.refs_5_), channel_id=1, source_target_pairs={{0,4},{4,8},{8,12},{12,16},{16,20},{20,24},{24,28},{28,0},{32,36},... | collective-permute-start | bytes 786440 | tf_op jit(solution)/shard_map/ppermute | solution.py:401
  13.9 7.8 %collective-permute-start.3 = (bf16[1024,128]{1,0:T(8,128)(2,1)S(1)}, bf16[1024,128]{1,0:T(8,128)(2,1)S(1)}, u32[]{:S(2)}, u32[]{:S(2)}) collective-permute-start(bf16[1024,128]{1,0:T(8,128)(2,1)S(1)} %collective-permute-done.1.refs_2_.refs_6_), channel_id=1, source_target_pairs={{0,28},{4,0},{8,4},{12,8},{16,12},{20,16},{24,20},{28,24},{32,60},... | collective-permute-start | bytes 786440 | tf_op jit(solution)/shard_map/ppermute | solution.py:401
  13.9 28.2 %copy-start.2 = (bf16[1024,128]{1,0:T(8,128)(2,1)}, bf16[1024,128]{1,0:T(8,128)(2,1)S(1)}, u32[]{:S(2)}) copy-start(bf16[1024,128]{1,0:T(8,128)(2,1)S(1)} %collective-permute-done.4.refs_2_) | copy-start | bytes 786436
  21.7 7.7 %collective-permute-start.5 = (bf16[1024,128]{1,0:T(8,128)(2,1)S(1)}, bf16[1024,128]{1,0:T(8,128)(2,1)S(1)}, u32[]{:S(2)}, u32[]{:S(2)}) collective-permute-start(bf16[1024,128]{1,0:T(8,128)(2,1)S(1)} %collective-permute-done.2.refs_3_.refs_7_), channel_id=1, source_target_pairs={{0,4},{4,8},{8,12},{12,16},{16,20},{20,24},{24,28},{28,0},{32,36},... | collective-permute-start | bytes 786440 | tf_op jit(solution)/shard_map/ppermute | solution.py:401
  23.4 7.7 %collective-permute-start.6 = (bf16[1024,128]{1,0:T(8,128)(2,1)S(1)}, bf16[1024,128]{1,0:T(8,128)(2,1)S(1)}, u32[]{:S(2)}, u32[]{:S(2)}) collective-permute-start(bf16[1024,128]{1,0:T(8,128)(2,1)S(1)} %collective-permute-done.3.refs_4_.refs_8_), channel_id=1, source_target_pairs={{0,28},{4,0},{8,4},{12,8},{16,12},{20,16},{24,20},{28,24},{32,60},... | collective-permute-start | bytes 786440 | tf_op jit(solution)/shard_map/ppermute | solution.py:401
  23.7 9.0 %collective-permute-start.7 = (bf16[96,1024]{1,0:T(8,128)(2,1)S(1)}, bf16[96,1024]{1,0:T(8,128)(2,1)S(1)}, u32[]{:S(2)}, u32[]{:S(2)}) collective-permute-start(bf16[96,1024]{1,0:T(8,128)(2,1)S(1)} %get-tuple-element.40), channel_id=1, source_target_pairs={{0,32},{4,36},{8,40},{12,44},{16,48},{20,52},{24,56},{28,60},{32,6... | collective-permute-start | bytes 589832 | tf_op jit(solution)/shard_map/ppermute | solution.py:401
  25.2 8.9 %collective-permute-start.8 = (bf16[96,1024]{1,0:T(8,128)(2,1)S(1)}, bf16[96,1024]{1,0:T(8,128)(2,1)S(1)}, u32[]{:S(2)}, u32[]{:S(2)}) collective-permute-start(bf16[96,1024]{1,0:T(8,128)(2,1)S(1)} %get-tuple-element.41), channel_id=1, source_target_pairs={{0,64},{4,68},{8,72},{12,76},{16,80},{20,84},{24,88},{28,92},{32,9... | collective-permute-start | bytes 589832 | tf_op jit(solution)/shard_map/ppermute | solution.py:401
  27.9 6.2 %collective-permute-start.9 = (bf16[96,1024]{1,0:T(8,128)(2,1)S(1)}, bf16[96,1024]{1,0:T(8,128)(2,1)S(1)}, u32[]{:S(2)}, u32[]{:S(2)}) collective-permute-start(bf16[96,1024]{1,0:T(8,128)(2,1)S(1)} %get-tuple-element.42), channel_id=1, source_target_pairs={{0,96},{4,100},{8,104},{12,108},{16,112},{20,116},{24,120},{28,124... | collective-permute-start | bytes 589832 | tf_op jit(solution)/shard_map/ppermute | solution.py:401
  29.4 8.0 %collective-permute-start.10 = (bf16[1024,128]{1,0:T(8,128)(2,1)S(1)}, bf16[1024,128]{1,0:T(8,128)(2,1)S(1)}, u32[]{:S(2)}, u32[]{:S(2)}) collective-permute-start(bf16[1024,128]{1,0:T(8,128)(2,1)S(1)} %collective-permute-done.4.refs_2_), channel_id=1, source_target_pairs={{0,4},{4,8},{8,12},{12,16},{16,20},{20,24},{24,28},{28,0},{32,36},... | collective-permute-start | bytes 786440 | tf_op jit(solution)/shard_map/ppermute | solution.py:401
  31.1 6.5 %collective-permute-start.11 = (bf16[1024,128]{1,0:T(8,128)(2,1)S(1)}, bf16[1024,128]{1,0:T(8,128)(2,1)}, u32[]{:S(2)}, u32[]{:S(2)}) collective-permute-start(bf16[1024,128]{1,0:T(8,128)(2,1)S(1)} %collective-permute-done.4.refs_2_), channel_id=1, source_target_pairs={{0,28},{4,0},{8,4},{12,8},{16,12},{20,16},{24,20},{28,24},{32,60},... | collective-permute-start | bytes 786440 | tf_op jit(solution)/shard_map/ppermute | solution.py:401
  34.1 48.8 %collective-permute-start.18 = (bf16[7168,128]{1,0:T(8,128)(2,1)}, bf16[7168,128]{1,0:T(8,128)(2,1)}, u32[]{:S(2)}, u32[]{:S(2)}) collective-permute-start(bf16[7168,128]{1,0:T(8,128)(2,1)} %pack.1.refs_0_), channel_id=1, source_target_pairs={{0,32},{4,36},{8,40},{12,44},{16,48},{20,52},{24,56},{28,60},{32,6... | collective-permute-start | bytes 5505032 | tf_op jit(solution)/shard_map/ppermute | solution.py:401
  35.9 47.1 %collective-permute-start.19 = (bf16[7168,128]{1,0:T(8,128)(2,1)}, bf16[7168,128]{1,0:T(8,128)(2,1)}, u32[]{:S(2)}, u32[]{:S(2)}) collective-permute-start(bf16[7168,128]{1,0:T(8,128)(2,1)} %pack.1.refs_0_), channel_id=1, source_target_pairs={{0,96},{4,100},{8,104},{12,108},{16,112},{20,116},{24,120},{28,124... | collective-permute-start | bytes 5505032 | tf_op jit(solution)/shard_map/ppermute | solution.py:401
  37.3 26.6 %copy-start.3 = (bf16[1024,128]{1,0:T(8,128)(2,1)}, bf16[1024,128]{1,0:T(8,128)(2,1)S(1)}, u32[]{:S(2)}) copy-start(bf16[1024,128]{1,0:T(8,128)(2,1)S(1)} %collective-permute-done.10.refs_3_) | copy-start | bytes 786436
  37.6 7.2 %collective-permute-start.12 = (bf16[1024,128]{1,0:T(8,128)(2,1)S(1)}, bf16[1024,128]{1,0:T(8,128)(2,1)S(1)}, u32[]{:S(2)}, u32[]{:S(2)}) collective-permute-start(bf16[1024,128]{1,0:T(8,128)(2,1)S(1)} %collective-permute-done.5.refs_5_.refs_9_), channel_id=1, source_target_pairs={{0,4},{4,8},{8,12},{12,16},{16,20},{20,24},{24,28},{28,0},{32,36},... | collective-permute-start | bytes 786440 | tf_op jit(solution)/shard_map/ppermute | solution.py:401
  39.4 14.4 %collective-permute-start.13 = (bf16[1024,128]{1,0:T(8,128)(2,1)S(1)}, bf16[1024,128]{1,0:T(8,128)(2,1)}, u32[]{:S(2)}, u32[]{:S(2)}) collective-permute-start(bf16[1024,128]{1,0:T(8,128)(2,1)S(1)} %collective-permute-done.10.refs_3_), channel_id=1, source_target_pairs={{0,4},{4,8},{8,12},{12,16},{16,20},{20,24},{24,28},{28,0},{32,36},... | collective-permute-start | bytes 786440 | tf_op jit(solution)/shard_map/ppermute | solution.py:401
  42.1 13.1 %collective-permute-start.15 = (bf16[1024,128]{1,0:T(8,128)(2,1)}, bf16[1024,128]{1,0:T(8,128)(2,1)}, u32[]{:S(2)}, u32[]{:S(2)}) collective-permute-start(bf16[1024,128]{1,0:T(8,128)(2,1)} %collective-permute-done.11.refs_4_), channel_id=1, source_target_pairs={{0,28},{4,0},{8,4},{12,8},{16,12},{20,16},{24,20},{28,24},{32,60},... | collective-permute-start | bytes 786440 | tf_op jit(solution)/shard_map/ppermute | solution.py:401
  42.1 26.2 %copy-start.12 = (s32[8]{0:T(128)S(1)}, s32[8]{0:T(128)}, u32[]{:S(2)}) copy-start(s32[8]{0:T(128)} %constant.133.clone) | copy-start | bytes 100
  44.8 23.6 %copy-start.1 = (bf16[1024,128]{1,0:T(8,128)(2,1)}, bf16[1024,128]{1,0:T(8,128)(2,1)S(1)}, u32[]{:S(2)}) copy-start(bf16[1024,128]{1,0:T(8,128)(2,1)S(1)} %collective-permute-done.12.refs_0_.refs_1_) | copy-start | bytes 786436
  46.2 17.0 %all-to-all-start = ((f32[8,32,128]{2,1,0:T(8,128)}), f32[8,32,128]{2,1,0:T(8,128)S(1)}, u32[]{:S(2)}, u32[]{:S(2)}) async-start(f32[8,32,128]{2,1,0:T(8,128)} %p_column_rest.1), calls=%async_computation | async-start | bytes 262144 | tf_op jit(solution)/shard_map/all_to_all | solution.py:390
  53.8 21.1 %collective-permute-start.14 = (bf16[1024,128]{1,0:T(8,128)(2,1)}, bf16[1024,128]{1,0:T(8,128)(2,1)S(1)}, u32[]{:S(2)}, u32[]{:S(2)}) collective-permute-start(bf16[1024,128]{1,0:T(8,128)(2,1)} %collective-permute-done.13.refs_5_), channel_id=1, source_target_pairs={{0,4},{4,8},{8,12},{12,16},{16,20},{20,24},{24,28},{28,0},{32,36},... | collective-permute-start | bytes 786440 | tf_op jit(solution)/shard_map/ppermute | solution.py:401
  55.3 19.6 %collective-permute-start.16 = (bf16[1024,128]{1,0:T(8,128)(2,1)}, bf16[1024,128]{1,0:T(8,128)(2,1)S(1)}, u32[]{:S(2)}, u32[]{:S(2)}) collective-permute-start(bf16[1024,128]{1,0:T(8,128)(2,1)} %collective-permute-done.15.refs_6_), channel_id=1, source_target_pairs={{0,28},{4,0},{8,4},{12,8},{16,12},{20,16},{24,20},{28,24},{32,60},... | collective-permute-start | bytes 786440 | tf_op jit(solution)/shard_map/ppermute | solution.py:401
  55.8 19.0 %collective-permute-start.17 = (bf16[1024,128]{1,0:T(8,128)(2,1)}, bf16[1024,128]{1,0:T(8,128)(2,1)S(1)}, u32[]{:S(2)}, u32[]{:S(2)}) collective-permute-start(bf16[1024,128]{1,0:T(8,128)(2,1)} %collective-permute-done.15.refs_6_), channel_id=1, source_target_pairs={{0,24},{4,28},{8,0},{12,4},{16,8},{20,12},{24,16},{28,20},{32,56},... | collective-permute-start | bytes 786440 | tf_op jit(solution)/shard_map/ppermute | solution.py:401
  63.9 10.1 %all-to-all-start.1 = ((f32[4,32,128]{2,1,0:T(8,128)}), f32[4,32,128]{2,1,0:T(8,128)S(1)}, u32[]{:S(2)}, u32[]{:S(2)}) async-start(f32[4,32,128]{2,1,0:T(8,128)} %add_spread.2), calls=%async_computation.1 | async-start | bytes 131072 | tf_op jit(solution)/shard_map/all_to_all | solution.py:390
  68.4 14.5 %copy-start.10 = (s32[32]{0:T(128)S(1)}, s32[32]{0:T(128)}, u32[]{:S(2)}) copy-start(s32[32]{0:T(128)} %constant.134.clone) | copy-start | bytes 388
  68.4 14.5 %copy-start.11 = (s32[32]{0:T(128)S(1)}, s32[32]{0:T(128)}, u32[]{:S(2)}) copy-start(s32[32]{0:T(128)} %constant.135.clone) | copy-start | bytes 388
  68.4 14.5 %copy-start.8 = (s32[18]{0:T(128)S(1)}, s32[18]{0:T(128)}, u32[]{:S(2)}) copy-start(s32[18]{0:T(128)} %constant.136.clone) | copy-start | bytes 220
  68.4 14.5 %copy-start.9 = (s32[18]{0:T(128)S(1)}, s32[18]{0:T(128)}, u32[]{:S(2)}) copy-start(s32[18]{0:T(128)} %constant.137.clone) | copy-start | bytes 220
  74.9 8.1 %copy-start.4 = (bf16[1024,128]{1,0:T(8,128)(2,1)}, bf16[1024,128]{1,0:T(8,128)(2,1)S(1)}, u32[]{:S(2)}) copy-start(bf16[1024,128]{1,0:T(8,128)(2,1)S(1)} %collective-permute-done.14.refs_7_) | copy-start | bytes 786436
  74.9 8.1 %copy-start.5 = (bf16[1024,128]{1,0:T(8,128)(2,1)}, bf16[1024,128]{1,0:T(8,128)(2,1)S(1)}, u32[]{:S(2)}) copy-start(bf16[1024,128]{1,0:T(8,128)(2,1)S(1)} %collective-permute-done.16.refs_8_) | copy-start | bytes 786436
  74.9 8.1 %copy-start.6 = (bf16[1024,128]{1,0:T(8,128)(2,1)}, bf16[1024,128]{1,0:T(8,128)(2,1)S(1)}, u32[]{:S(2)}) copy-start(bf16[1024,128]{1,0:T(8,128)(2,1)S(1)} %collective-permute-done.17.refs_9_) | copy-start | bytes 786436
  74.9 18.6 %all-to-all-start.2 = ((f32[32,32,128]{2,1,0:T(8,128)}), f32[32,32,128]{2,1,0:T(8,128)S(1)}, u32[]{:S(2)}, u32[]{:S(2)}) async-start(f32[32,32,128]{2,1,0:T(8,128)} %add_spread.3), calls=%async_computation.2 | async-start | bytes 1048576 | tf_op jit(solution)/shard_map/all_to_all | solution.py:390
  79.6 11.1 %collective-permute-start.20 = (bf16[1024,128]{1,0:T(8,128)(2,1)}, bf16[1024,128]{1,0:T(8,128)(2,1)S(1)}, u32[]{:S(2)}, u32[]{:S(2)}) collective-permute-start(bf16[1024,128]{1,0:T(8,128)(2,1)} %copy-done.1), channel_id=1, source_target_pairs={{0,32},{4,36},{8,40},{12,44},{16,48},{20,52},{24,56},{28,60},{32,6... | collective-permute-start | bytes 786440 | tf_op jit(solution)/shard_map/ppermute | solution.py:401
  81.1 10.3 %collective-permute-start.21 = (bf16[1024,128]{1,0:T(8,128)(2,1)}, bf16[1024,128]{1,0:T(8,128)(2,1)}, u32[]{:S(2)}, u32[]{:S(2)}) collective-permute-start(bf16[1024,128]{1,0:T(8,128)(2,1)} %copy-done.1), channel_id=1, source_target_pairs={{0,96},{4,100},{8,104},{12,108},{16,112},{20,116},{24,120},{28,124... | collective-permute-start | bytes 786440 | tf_op jit(solution)/shard_map/ppermute | solution.py:401
  90.7 0.7 copy-start.7
  99.1 7.6 %collective-permute-start.22 = (f32[32,448]{1,0:T(8,128)S(1)}, f32[32,448]{1,0:T(8,128)S(1)}, u32[]{:S(2)}, u32[]{:S(2)}) collective-permute-start(f32[32,448]{1,0:T(8,128)S(1)} %get-tuple-element.60.a_ref), channel_id=1, source_target_pairs={{0,1},{1,2},{2,3},{3,0},{4,5},{5,6},{6,7},{7,4},{8,9},{9,10},{10,1... | collective-permute-start | bytes 172040 | tf_op jit(solution)/shard_map/ppermute | solution.py:395
  100.2 6.4 %collective-permute-start.23 = (f32[32,448]{1,0:T(8,128)S(1)}, f32[32,448]{1,0:T(8,128)S(1)}, u32[]{:S(2)}, u32[]{:S(2)}) collective-permute-start(f32[32,448]{1,0:T(8,128)S(1)} %get-tuple-element.60.a_ref), channel_id=1, source_target_pairs={{0,3},{1,0},{2,1},{3,2},{4,7},{5,4},{6,5},{7,6},{8,11},{9,8},{10,9... | collective-permute-start | bytes 172040 | tf_op jit(solution)/shard_map/ppermute | solution.py:395
  102.4 5.8 %collective-permute-start.24 = (f32[32,448]{1,0:T(8,128)S(1)}, f32[32,448]{1,0:T(8,128)S(1)}, u32[]{:S(2)}, u32[]{:S(2)}) collective-permute-start(f32[32,448]{1,0:T(8,128)S(1)} %get-tuple-element.60.a_ref), channel_id=1, source_target_pairs={{0,2},{1,3},{2,0},{3,1},{4,6},{5,7},{6,4},{7,5},{8,10},{9,11},{10,... | collective-permute-start | bytes 172040 | tf_op jit(solution)/shard_map/ppermute | solution.py:395
